TPU v7x, 32 devices: a whole 2x2x4 slice. The times are simulated.
32 devices in a mesh: plane: 16 (over z, x, core), mode: 2 (over y).
Axes of the slice: x: 2, y: 2, z: 4, core: 2. Of those that a mesh axis runs over, the one named last changes fastest.
Arguments:
- velocity: float32 [3, 12800, 1024], P(None, 'plane', 'mode'), may hold values from -10 to 10
- inverses: float32 [512, 25, 25], P('mode'), may hold values from -1 to 2
- neighbours: int32 [512, 4], P('plane'), may hold values from -1 to 31, as said below
- flags: int32 [512], P('plane'), may hold values 0 or 1
Outputs:
- advanced: float32 [3, 12800, 1024], P(None, 'plane', 'mode')
- viscosity: float32 [512], P('plane')
Inputs may be any that keep to these rules, and one draw needn't show every extreme that they name: Partition q holds one column of 32 elements of a structured patch, numbered in its own order; every element of it has its west neighbour in partition q - 1 and its east neighbour in partition q + 1 (none in the first and last partitions), its south and north neighbours in q, with -1 only at the patch's edges.
All inputs are finite; a program needn't handle non-finite values. No bound on the sum of `flags` on one device may be relied on, other than what follows from the above.
Results may differ from a plain program's by a relative error of at most 0.000062.
Values sent between devices are 32-bit elements; how exact they have to be, the bound alone decides.
No kernel may reach another device: no remote copies, remote signals or barrier semaphores. Data moves between devices by JAX's collectives and lax.ppermute only.
A program may use at most 128 MiB of HBM per device.

v0:
```python
import math

import jax
import jax.numpy as jnp
from jax import lax
from jax.sharding import PartitionSpec as P

ORDER = 4
NODES = 25
MODES = 512
COEFS = 1024
E_DEV = 32


highest = lax.Precision.HIGHEST


def with_halo(block, sides, width):
    for axis, dim in sides:
        count = lax.axis_size(axis)
        forward = [(i, i + 1) for i in range(count - 1)]
        backward = [(target, source) for source, target in forward]
        low = lax.ppermute(
            lax.slice_in_dim(block, block.shape[dim] - width, None, axis=dim), axis, forward
        )
        high = lax.ppermute(lax.slice_in_dim(block, 0, width, axis=dim), axis, backward)
        block = jnp.concatenate([low, block, high], axis=dim)
    return block


def basis_table():
    index = jnp.arange(COEFS, dtype=jnp.int32)
    pair = index // 2
    slot = index % 2
    freq = jnp.where((slot == 1) & (pair == 0), MODES, pair)
    phase = freq[:, None] * index[None, :] % COEFS
    angle = phase.astype(jnp.float32) * (2.0 * math.pi / COEFS)
    use_cos = (slot == 0) | (pair == 0)
    basis = jnp.where(use_cos[:, None], jnp.cos(angle), -jnp.sin(angle))
    weight = jnp.where(pair == 0, 1.0, 2.0).astype(jnp.float32)
    return (basis, weight)


def spanwise_term(flux_modes):
    index = jnp.arange(COEFS, dtype=jnp.int32)
    pair = index // 2
    rate = pair.astype(jnp.float32) / (MODES * 4.0 * math.sqrt(MODES))
    shifted = jnp.where(
        index % 2 == 0, -jnp.roll(flux_modes, -1, axis=-1), jnp.roll(flux_modes, 1, axis=-1)
    )
    return rate * shifted


def on_device(velocity, inverses, neighbours, flags):
    mode_count = lax.axis_size("mode")
    plane_count = lax.axis_size("plane")
    local_width = velocity.shape[2]
    points = velocity.shape[1]
    group_rows = points // mode_count
    basis, weight = basis_table()
    synth = weight[:, None] * basis
    grouped = velocity.reshape(3, mode_count, group_rows, local_width)
    physical = jnp.einsum(
        "cgrj,jz->cgrz",
        lax.all_to_all(grouped, "mode", split_axis=1, concat_axis=3, tiled=True),
        synth,
        precision=highest,
    )
    flux_phys = physical * physical[2:3]
    flux_modes = jnp.einsum("cgrz,jz->cgrj", flux_phys, basis, precision=highest) / COEFS
    spanwise = spanwise_term(flux_modes)
    returned = lax.all_to_all(spanwise, "mode", split_axis=3, concat_axis=1, tiled=True)
    global_index = lax.axis_index("mode") * local_width + lax.iota(jnp.int32, local_width)
    local_weight = jnp.where(global_index // 2 == 0, 1.0, 2.0).astype(jnp.float32)
    local_energy = jnp.sum(velocity * velocity * local_weight, axis=(0, 2))
    field_energy = lax.psum(jnp.sum(local_energy), ("plane", "mode"))
    speed = jnp.sqrt(field_energy / (3.0 * points * plane_count * COEFS))
    node = jnp.arange(NODES, dtype=jnp.int32)
    degree_a = node // (ORDER + 1)
    degree_b = node % (ORDER + 1)
    high_mask = ((degree_a == ORDER) | (degree_b == ORDER)).astype(jnp.float32)
    node_energy = local_energy.reshape(E_DEV, NODES)
    high, total = lax.psum(
        (jnp.sum(node_energy * high_mask, axis=1), jnp.sum(node_energy, axis=1)), "mode"
    )
    spanwise_local = returned.reshape(3, points, local_width)
    sensor = jnp.log10((high + 1e-06) / (total + 1e-06))
    ramp_value = 0.5 * (1.0 + jnp.sin(0.5 * math.pi * jnp.clip(sensor + 2.0, -1.0, 1.0)))
    viscous_shape = 0.4 * (1.0 + flags.astype(jnp.float32)) * ramp_value
    source = speed * viscous_shape
    padded = with_halo(source, (("plane", 0),), E_DEV)
    element = lax.iota(jnp.int32, E_DEV)
    base_offset = jnp.array([0, 2 * E_DEV, E_DEV, E_DEV], dtype=jnp.int32)
    target = jnp.where(neighbours >= 0, base_offset[None, :] + neighbours, E_DEV + element[:, None])
    positions = lax.iota(jnp.int32, 3 * E_DEV)
    picked = jnp.where(target[:, :, None] == positions[None, None, :], padded[None, None, :], 0.0)
    beside_all = jnp.sum(jnp.sum(picked, axis=2), axis=1)
    viscosity = (2.0 * source + beside_all) / 6.0
    damping = (degree_a * degree_a + degree_b * degree_b).astype(jnp.float32) / (
        2.0 * ORDER * ORDER
    )
    point_visc = (viscosity[:, None] * damping[None, :]).reshape(points)
    right_side = velocity - spanwise_local - point_visc[None, :, None] * velocity
    repeated = jnp.repeat(inverses, 2, axis=0)
    advanced = jnp.einsum(
        "jin,cenj->ceij",
        repeated,
        right_side.reshape(3, E_DEV, NODES, local_width),
        precision=highest,
    )
    return (advanced.reshape(3, points, local_width), viscosity)


def solution(mesh):
    in_specs = (P(None, "plane", "mode"), P("mode", None, None), P("plane", None), P("plane"))
    out_specs = (P(None, "plane", "mode"), P("plane"))
    return jax.shard_map(
        on_device, mesh=mesh, in_specs=in_specs, out_specs=out_specs, check_vma=False
    )
```

profile of v0, /device:TPU:1, one launch (start us, length us, event | category | flops | bytes accessed | tf_op | source)
XLA Modules:
  0.0 435.8 jit_solution(7905416657269573239)
XLA Ops:
  0.6 5.7 %copy.59 = f32[3,2,400,512]{3,2,0,1:T(8,128)} copy(f32[3,2,400,512]{3,2,1,0:T(8,128)} %bitcast.54) | data formatting | bytes 9830400 | tf_op jit(solution)/shard_map/reshape | solution.py:62
  6.3 5.8 %all-to-all-start = ((f32[3,2,400,512]{3,2,0,1:T(8,128)}), f32[3,2,400,512]{3,2,0,1:T(8,128)}, u32[]{:S(2)}, u32[]{:S(2)}) async-start(f32[3,2,400,512]{3,2,0,1:T(8,128)} %copy.59), calls=%async_computation | async-start | bytes 9830400 | tf_op jit(solution)/shard_map/all_to_all | solution.py:65
  12.2 19.3 %fusion.69 = f32[1024,1024,1]{1,0,2:T(8,128)} fusion(f32[1024]{0:T(1024)S(1)} %broadcast_select_fusion, s32[1024]{0:T(1024)S(1)} %fusion.34, pred[1024]{0:T(1024)(128)(4,1)S(1)} %fusion.42), kind=kLoop, calls=%fused_computation.19.clone.clone.clone.1 | loop fusion | flops 17825792 | bytes 4203520 | tf_op jit(solution)/shard_map/cgrj,jz->cgrz/dot_general | solution.py:63
  31.6 36.0 %all-to-all-done = f32[3,2,400,512]{3,2,0,1:T(8,128)} async-done(((f32[3,2,400,512]{3,2,0,1:T(8,128)}), f32[3,2,400,512]{3,2,0,1:T(8,128)}, u32[]{:S(2)}, u32[]{:S(2)}) %all-to-all-start) | async-done | bytes 4915232 | tf_op jit(solution)/shard_map/all_to_all | solution.py:65
  67.6 8.4 %copy.60 = f32[3,1,400,2,512]{4,3,2,0,1:T(2,128)} copy(f32[3,1,400,2,512]{4,2,0,3,1:T(8,128)} %bitcast.3) | data formatting | bytes 9830400 | tf_op jit(solution)/shard_map/all_to_all | solution.py:65
  76.0 7.7 %reshape.220 = f32[3,400,1024]{2,1,0:T(8,128)} reshape(f32[3,1,400,2,512]{4,3,2,0,1:T(2,128)} %copy.60) | data formatting | bytes 9830400 | tf_op jit(solution)/shard_map/reshape.1
  83.7 19.8 %fusion.17 = f32[3,400,1024]{2,1,0:T(8,128)S(1)} fusion(f32[3,400,1024]{2,1,0:T(8,128)} %reshape.220, f32[1024,1024,1]{1,0,2:T(8,128)} %fusion.69), kind=kOutput, calls=%fused_computation.26 | convolution fusion | flops 15099494400 | bytes 14024704 | tf_op jit(solution)/shard_map/cgrj,jz->cgrz/dot_general | solution.py:63
  103.5 0.2 slice_bitcast_fusion
  103.7 1.2 fusion.67
  104.9 38.1 %multiply_bitcast_fusion = f32[3,1,400,1024]{3,2,0,1:T(8,128)S(1)} fusion(s32[1024]{0:T(1024)S(1)} %fusion.34, pred[1024]{0:T(1024)(128)(4,1)S(1)} %fusion.42, f32[3,400,1024]{2,1,0:T(8,128)S(1)} %fusion.67), kind=kOutput, calls=%fused_computation.9 | convolution fusion | flops 15117500416 | bytes 9835520 | tf_op jit(solution)/shard_map/cgrz,jz->cgrj/dot_general | solution.py:70
  143.1 0.2 fusion.53
  143.3 2.0 fusion.54
  145.3 3.9 fusion.1
  149.2 15.8 %copy.61 = f32[3,1,400,1024]{2,1,0,3:T(1,128)} copy(f32[3,1,400,1024]{3,2,0,1:T(8,128)} %fusion.1) | data formatting | bytes 9830400 | tf_op jit(solution)/shard_map/mul | solution.py:51
  165.1 6.3 %all-to-all-start.1 = ((f32[3,1,400,1024]{2,1,0,3:T(1,128)}), f32[3,1,400,1024]{2,1,0,3:T(1,128)}, u32[]{:S(2)}, u32[]{:S(2)}) async-start(f32[3,1,400,1024]{2,1,0,3:T(1,128)} %copy.61), calls=%async_computation.1 | async-start | bytes 12582912 | tf_op jit(solution)/shard_map/all_to_all | solution.py:72
  171.4 0.0 copy-start.2
  171.4 0.0 copy-start.1
  171.4 0.0 copy-start.3
  171.4 0.0 copy-start
  171.4 4.4 %fusion.5 = (f32[]{:T(128)}, f32[800]{0:T(1024)S(1)}) fusion(f32[3,800,512]{2,1,0:T(8,128)} %param.5, f32[512]{0:T(512)S(1)} %fusion.44), kind=kLoop, calls=%fused_computation.13 | loop fusion | flops 4914399 | bytes 4920452 | tf_op jit(solution)/shard_map/reduce_sum | solution.py:76
  175.9 99.5 %psum.21 = f32[]{:T(128)} all-reduce(f32[]{:T(128)} %get-tuple-element.4), channel_id=1, replica_groups=mesh['plane'=16,'mode'=2] {'plane','mode'}, use_global_device_ids=true, to_apply=%region_1.2 | all-reduce | flops 1 | bytes 8 | tf_op jit(solution)/shard_map/psum | solution.py:76
  276.1 0.1 reshape.222
  276.2 0.1 multiply_reduce_fusion
  276.3 3.8 all-reduce
  280.1 0.0 copy-done.2
  280.1 0.1 multiply_multiply_fusion.1
  280.2 4.8 %collective-permute-start.1 = (f32[32]{0:T(128)S(1)}, f32[32]{0:T(128)S(1)}, u32[]{:S(2)}, u32[]{:S(2)}) collective-permute-start(f32[32]{0:T(128)S(1)} %multiply_multiply_fusion.1), channel_id=1, source_target_pairs={{2,0},{4,2},{6,4},{8,6},{10,8},{12,10},{14,12},{16,14},{18,16},{20... | collective-permute-start | bytes 392 | tf_op jit(solution)/shard_map/ppermute | solution.py:26
  285.0 3.4 collective-permute-start
  288.4 0.0 copy-done.1
  288.4 0.0 copy-done.3
  288.4 0.1 add_select_fusion.3
  288.5 0.0 copy-done
  288.5 4.5 %copy.64 = f32[256,25,25]{2,1,0:T(8,128)} copy(f32[256,25,25]{0,2,1:T(8,128)S(1)} %copy-done) | data formatting | bytes 1280000 | tf_op args[1]
  292.9 0.0 collective-permute-done.1
  292.9 0.0 collective-permute-done
  292.9 0.1 pad_maximum_fusion
  293.0 0.2 select_reduce_fusion
  293.2 0.0 copy-start.4
  293.2 0.1 broadcast_multiply_fusion
  293.3 0.1 mul.197
  293.4 0.0 all-to-all-done.1
  293.4 15.5 %copy.62 = f32[3,1,400,1024]{3,2,0,1:T(8,128)} copy(f32[3,1,400,1024]{2,1,0,3:T(1,128)} %all-to-all-done.1) | data formatting | bytes 9830400 | tf_op jit(solution)/shard_map/all_to_all | solution.py:72
  308.9 0.0 copy-done.4
  308.9 0.0 slice-start
  308.9 7.7 %all_to_all.26 = f32[3,1,400,2,512]{4,3,2,0,1:T(2,128)} reshape(f32[3,1,400,1024]{3,2,0,1:T(8,128)} %copy.62) | data formatting | bytes 9830400 | tf_op jit(solution)/shard_map/all_to_all | solution.py:72
  316.7 0.0 slice-start.1
  316.7 3.4 copy.63
  320.1 0.0 slice-done
  320.1 0.2 slice-done.1
  320.3 2.9 multiply_subtract_fusion
  323.2 5.6 %reshape.223 = f32[3,32,25,512]{3,2,1,0:T(8,128)} reshape(f32[3,800,512]{2,1,0:T(8,128)} %multiply_subtract_fusion) | data formatting | bytes 9830400 | tf_op jit(solution)/shard_map/reshape | solution.py:108
  328.9 21.0 %copy.65 = f32[3,32,25,512]{2,1,0,3:T(8,128)} copy(f32[3,32,25,512]{3,2,1,0:T(8,128)} %reshape.223) | data formatting | bytes 9830400 | tf_op jit(solution)/shard_map/reshape | solution.py:108
  349.9 3.5 broadcast_in_dim.81
  353.4 45.9 %convolution_bitcast_fusion = f32[3,32,25,512]{2,1,0,3:T(8,128)} fusion(f32[3,32,25,512]{2,1,0,3:T(8,128)} %copy.65, f32[512,25,25,1]{2,1,3,0:T(8,128)S(1)} %bitcast.57), kind=kOutput, calls=%fused_computation | convolution fusion | flops 368640000 | bytes 11110400 | tf_op jit(solution)/shard_map/jin,cenj->ceij/dot_general | solution.py:105
  399.3 27.7 %reshape.229 = f32[3,800,512]{1,0,2:T(4,128)} reshape(f32[3,32,25,512]{2,1,0,3:T(8,128)} %convolution_bitcast_fusion) | data formatting | bytes 9830400 | tf_op jit(solution)/shard_map/reshape | solution.py:111
  426.9 8.4 %copy.68 = f32[3,800,512]{2,1,0:T(8,128)} copy(f32[3,800,512]{1,0,2:T(4,128)} %reshape.229) | data formatting | bytes 9830400 | tf_op jit(solution)/shard_map/reshape | solution.py:111
  (11 shorter events, 0.1 us)
Async XLA Ops:
  6.3 61.3 %all-to-all-start = ((f32[3,2,400,512]{3,2,0,1:T(8,128)}), f32[3,2,400,512]{3,2,0,1:T(8,128)}, u32[]{:S(2)}, u32[]{:S(2)}) async-start(f32[3,2,400,512]{3,2,0,1:T(8,128)} %copy.59), calls=%async_computation | async-start | bytes 9830400 | tf_op jit(solution)/shard_map/all_to_all | solution.py:65
  165.1 128.3 %all-to-all-start.1 = ((f32[3,1,400,1024]{2,1,0,3:T(1,128)}), f32[3,1,400,1024]{2,1,0,3:T(1,128)}, u32[]{:S(2)}, u32[]{:S(2)}) async-start(f32[3,1,400,1024]{2,1,0,3:T(1,128)} %copy.61), calls=%async_computation.1 | async-start | bytes 12582912 | tf_op jit(solution)/shard_map/all_to_all | solution.py:72
  171.4 108.7 %copy-start.2 = (s32[32]{0:T(128)S(1)}, s32[32]{0:T(128)}, u32[]{:S(2)}) copy-start(s32[32]{0:T(128)} %param.8) | copy-start | bytes 388
  171.4 117.0 %copy-start.1 = (s32[32,4]{0,1:T(4,128)S(1)}, s32[32,4]{0,1:T(4,128)}, u32[]{:S(2)}) copy-start(s32[32,4]{0,1:T(4,128)} %param.7) | copy-start | bytes 1540
  171.4 117.0 %copy-start.3 = (s32[4]{0:T(128)S(1)}, s32[4]{0:T(128)}, u32[]{:S(2)}) copy-start(s32[4]{0:T(128)} %constant.136.clone) | copy-start | bytes 52
  171.4 117.1 %copy-start = (f32[256,25,25]{0,2,1:T(8,128)S(1)}, f32[256,25,25]{0,2,1:T(8,128)}, u32[]{:S(2)}) copy-start(f32[256,25,25]{0,2,1:T(8,128)} %param.6) | copy-start | bytes 1920004
  280.2 12.8 %collective-permute-start.1 = (f32[32]{0:T(128)S(1)}, f32[32]{0:T(128)S(1)}, u32[]{:S(2)}, u32[]{:S(2)}) collective-permute-start(f32[32]{0:T(128)S(1)} %multiply_multiply_fusion.1), channel_id=1, source_target_pairs={{2,0},{4,2},{6,4},{8,6},{10,8},{12,10},{14,12},{16,14},{18,16},{20... | collective-permute-start | bytes 392 | tf_op jit(solution)/shard_map/ppermute | solution.py:26
  285.0 8.0 %collective-permute-start = (f32[32]{0:T(128)S(1)}, f32[32]{0:T(128)S(1)}, u32[]{:S(2)}, u32[]{:S(2)}) collective-permute-start(f32[32]{0:T(128)S(1)} %multiply_multiply_fusion.1), channel_id=1, source_target_pairs={{0,2},{2,4},{4,6},{6,8},{8,10},{10,12},{12,14},{14,16},{16,18},{18... | collective-permute-start | bytes 392 | tf_op jit(solution)/shard_map/ppermute | solution.py:23
  293.2 15.7 %copy-start.4 = (f32[32]{0:T(128)}, f32[32]{0:T(128)S(1)}, u32[]{:S(2)}) copy-start(f32[32]{0:T(128)S(1)} %add_multiply_fusion) | copy-start | bytes 388
  308.9 11.2 %slice-start = ((s8[4915200]{0:T(1024)(128)(4,1)}), s8[720896]{0:T(1024)(128)(4,1)S(1)}, s32[]{:S(2)}) async-start(s8[4915200]{0:T(1024)(128)(4,1)} %bitcast.55), calls=%async_computation.2 | async-start | bytes 1441792
  316.7 3.7 slice-start.1
where the time goes:
time: 444 us; the launch traced here: 436 us
  local copies, waits for them, and re-layouts  138 us (31%)
  matrix products  104 us (23%)
  blocking collectives  103 us (23%)
  waiting for transfers between devices  36 us (8%)
  other arithmetic  32.5 us (7%)
  starting transfers between devices  20.3 us (5%)
    psum x1, blocking collectives, on_device(): field_energy = lax.psum(jnp.sum(local_energy), ('plane', 'mode'))  99.5 us
    dot_general x1, matrix products, on_device(): jnp.einsum('jin,cenj->ceij', repeated, right_side.reshape(3, E_DEV, NODES...  45.9 us
    dot_general x1, matrix products, on_device(): jnp.einsum('cgrz,jz->cgrj', flux_phys, basis, precision=highest) / COEFS  38.1 us
    reshape x2, local copies, waits for them, and re-layouts, on_device(): return (advanced.reshape(3, points, local_width), viscosity)  36.1 us
    all_to_all x1, waiting for transfers between devices, on_device(): lax.all_to_all(grouped, 'mode', split_axis=1, concat_axis=3, tiled=True)  36 us
    reshape x2, local copies, waits for them, and re-layouts, on_device(): right_side.reshape(3, E_DEV, NODES, local_width)  26.7 us
    all_to_all x3, local copies, waits for them, and re-layouts, on_device(): lax.all_to_all(spanwise, 'mode', split_axis=3, concat_axis=1, tiled=True)  26.7 us
    dot_general x1, matrix products, on_device(): jnp.einsum('cgrj,jz->cgrz', lax.all_to_all(grouped, 'mode', split_axis=1,...  19.8 us
  transfers between devices with their start and end apart: 4, of which 1 were waited for; matrix products, arithmetic and copies ran while one was open for 7% of the time, Pallas kernels for 0%

commit v1 on v0

v1 whole, which is shorter than its diff:
```python
import math

import jax
import jax.numpy as jnp
import ml_dtypes
import numpy as np
from jax import lax
from jax.experimental import pallas as pl
from jax.experimental.pallas import tpu as pltpu
from jax.sharding import PartitionSpec as P

ORDER = 4
NODES = (ORDER + 1) ** 2
LENGTH = 4.0
LANES = 128
SUB = 8
TILE = SUB * NODES

f32 = jnp.float32
bf16 = jnp.bfloat16

IS_HIGH = [n // (ORDER + 1) == ORDER or n % (ORDER + 1) == ORDER for n in range(NODES)]


def split_np(table):
    high = table.astype(np.float32).astype(ml_dtypes.bfloat16)
    low = (table - high.astype(np.float64)).astype(ml_dtypes.bfloat16)
    return np.stack([high, low])


def tables(coefs):
    modes = coefs // 2
    index = np.arange(coefs)
    pair = index // 2
    odd = index % 2
    freq = np.where(index == 1, modes, pair)
    angle = 2.0 * np.pi * (freq[:, None] * index[None, :] % coefs) / coefs
    use_cos = (odd == 0) | (pair == 0)
    basis = np.where(use_cos[:, None], np.cos(angle), -np.sin(angle))
    weight = np.where(pair == 0, 1.0, 2.0)
    rate = pair / (modes * LENGTH * math.sqrt(modes))
    partner = basis[index ^ 1]
    derive = (np.where(odd == 0, -rate, rate) / coefs)[:, None] * partner
    return split_np(weight[:, None] * basis), split_np(derive.T.copy())


def halves(x):
    high = x.astype(bf16)
    return high, (x - high.astype(f32)).astype(bf16)


def dot(a, b):
    return jnp.dot(a, b, preferred_element_type=f32)


def energy_kernel(first, last, vel_ref, weight_ref, out_ref, point_ref):
    step = pl.program_id(0)
    width = vel_ref.shape[2]
    weight = weight_ref[...]
    acc = None
    for lane in range(0, width, LANES):
        for comp in range(vel_ref.shape[0]):
            x = vel_ref[comp, :, lane : lane + LANES]
            term = x * x * weight[:, lane : lane + LANES]
            acc = term if acc is None else acc + term
    point_ref[...] = acc
    total = jnp.zeros((SUB, LANES), f32)
    high = jnp.zeros((SUB, LANES), f32)
    for n in range(NODES):
        part = point_ref[pl.ds(n, SUB, stride=NODES), :]
        total = total + part
        if IS_HIGH[n]:
            high = high + part
    rows = last - first
    at = pl.multiple_of(rows + step * 2 * SUB, SUB)
    out_ref[pl.ds(at, SUB), :LANES] = total
    out_ref[pl.ds(at + SUB, SUB), :LANES] = high

    @pl.when((step * TILE >= first) & (step * TILE < last))
    def _():
        out_ref[pl.ds(pl.multiple_of(step * TILE - first, SUB), TILE), :] = vel_ref[vel_ref.shape[0] - 1]


def energies(velocity, weight, first, last):
    comps, points, width = velocity.shape
    steps = points // TILE
    rows = last - first + 2 * SUB * steps
    return pl.pallas_call(
        lambda *refs: energy_kernel(first, last, *refs),
        grid=(steps,),
        in_specs=[
            pl.BlockSpec((comps, TILE, width), lambda t: (0, t, 0)),
            pl.BlockSpec((1, width), lambda t: (0, 0)),
        ],
        out_specs=pl.BlockSpec((rows, width), lambda t: (0, 0)),
        out_shape=jax.ShapeDtypeStruct((rows, width), f32),
        scratch_shapes=[pltpu.VMEM((TILE, LANES), f32)],
        compiler_params=pltpu.CompilerParams(vmem_limit_bytes=16 << 20),
        name="energies",
    )(velocity, weight)


def expand_kernel(inv_ref, spread_ref, out_ref):
    spread = spread_ref[...]
    for i in range(NODES):
        x = inv_ref[i]
        high, rest = halves(x)
        mid, low = halves(x - high.astype(f32))
        y = (dot(high, spread) + dot(mid, spread)) + dot(low, spread)
        for t in range(out_ref.shape[0]):
            out_ref[t, i] = y[:, t * LANES : (t + 1) * LANES]


def expand(inverses, width):
    pairs = inverses.shape[0]
    spread = np.repeat(np.eye(pairs), 2, axis=1).astype(ml_dtypes.bfloat16)
    return pl.pallas_call(
        expand_kernel,
        out_shape=jax.ShapeDtypeStruct((width // LANES, NODES, NODES, LANES), f32),
        compiler_params=pltpu.CompilerParams(vmem_limit_bytes=16 << 20),
        name="expand",
    )(jnp.transpose(inverses, (1, 2, 0)), spread)


def chunk_kernel(n_far, is_w, aliased, *refs):
    refs = list(refs)
    own_ref = refs.pop(0)
    far_refs = [refs.pop(0) for _ in range(n_far)]
    wphys_ref = None if is_w else refs.pop(0)
    damp_ref, synth_ref, derive_ref, inv_ref = refs[:4]
    refs = refs[4 + aliased :]
    out_ref = refs.pop(0)
    if is_w:
        wphys_ref = refs.pop(0)
    rhs_ref, res_ref = refs
    width = own_ref.shape[2]
    own = own_ref[0]
    phys = None
    for s, x in enumerate([own] + [r[...] for r in far_refs]):
        high, low = halves(x)
        rows = slice(s * width, (s + 1) * width)
        part = dot(high, synth_ref[0, rows, :])
        part = part + dot(high, synth_ref[1, rows, :])
        part = part + dot(low, synth_ref[0, rows, :])
        phys = part if phys is None else phys + part
    if is_w:
        wphys_ref[...] = phys
        flux = phys * phys
    else:
        flux = phys * wphys_ref[...]
    high, low = halves(flux)
    span = dot(high, derive_ref[0]) + dot(high, derive_ref[1]) + dot(low, derive_ref[0])
    damp = damp_ref[...]
    for t in range(width // LANES):
        lanes = slice(t * LANES, (t + 1) * LANES)
        x = own[:, lanes]
        rhs_ref[t] = x - span[:, lanes] - damp * x

    def solve(t, carry):
        right = [rhs_ref[t, pl.ds(n, SUB, stride=NODES), :] for n in range(NODES)]
        for i in range(NODES):
            acc = None
            for n in range(NODES):
                term = inv_ref[t, i, n : n + 1, :] * right[n]
                acc = term if acc is None else acc + term
            res_ref[t, pl.ds(i, SUB, stride=NODES), :] = acc
        return carry

    lax.fori_loop(0, width // LANES, solve, 0)
    for t in range(width // LANES):
        out_ref[0, :, t * LANES : (t + 1) * LANES] = res_ref[t]


def advance(velocity, far, comp, first, rows, wphys, damp, synth, derive, inv, out):
    comps, points, width = velocity.shape
    coefs = synth.shape[1]
    tiles = width // LANES
    is_w = comp == comps - 1
    at = first // TILE
    whole = lambda shape: pl.BlockSpec(shape, lambda t: (0,) * len(shape), pipeline_mode=pl.Buffered(1))
    row = lambda w: pl.BlockSpec((TILE, w), lambda t: (at + t, 0))
    block = pl.BlockSpec((1, TILE, width), lambda t: (comp, at + t, 0))
    args = [velocity, *far]
    specs = [block] + [pl.BlockSpec((TILE, width), lambda t: (t, 0)) for _ in far]
    if not is_w:
        args.append(wphys)
        specs.append(row(coefs))
    args += [damp, synth, derive, inv]
    specs += [row(LANES), whole(synth.shape), whole(derive.shape), whole(inv.shape)]
    out_shape = [jax.ShapeDtypeStruct(velocity.shape, f32)]
    out_specs = [block]
    aliases = {}
    if out is not None:
        aliases[len(args)] = 0
        args.append(out)
        specs.append(pl.BlockSpec(memory_space=pl.ANY))
    if is_w:
        if wphys is not None:
            aliases[len(args)] = 1
            args.append(wphys)
            specs.append(pl.BlockSpec(memory_space=pl.ANY))
        out_shape.append(jax.ShapeDtypeStruct((points, coefs), f32))
        out_specs.append(row(coefs))
    result = pl.pallas_call(
        lambda *refs: chunk_kernel(len(far), is_w, len(aliases), *refs),
        grid=(rows // TILE,),
        in_specs=specs,
        out_specs=out_specs,
        out_shape=out_shape,
        scratch_shapes=[pltpu.VMEM((tiles, TILE, LANES), f32)] * 2,
        input_output_aliases=aliases,
        compiler_params=pltpu.CompilerParams(vmem_limit_bytes=32 << 20),
        cost_estimate=pl.CostEstimate(
            flops=6 * rows * coefs * (coefs + width), bytes_accessed=8 * rows * width, transcendentals=0
        ),
        name=f"advance_{comp}_{first}",
    )(*args)
    return (result[0], result[1] if is_w else wphys)


def exchange(block):
    count = lax.axis_size("mode")
    return [
        lax.ppermute(block, "mode", [(i, (i + s) % count) for i in range(count)])
        for s in range(1, count)
    ]


def sum_over_plane(value):
    count = lax.axis_size("plane")
    if count & (count - 1):
        return lax.psum(value, "plane")
    step = 1
    while step < count:
        value = value + lax.ppermute(value, "plane", [(i, i ^ step) for i in range(count)])
        step *= 2
    return value


def on_device(velocity, inverses, neighbours, flags):
    mode_count = lax.axis_size("mode")
    plane_count = lax.axis_size("plane")
    mine = lax.axis_index("mode")
    comps, points, width = velocity.shape
    coefs = width * mode_count
    elements = neighbours.shape[0]
    w = comps - 1

    first = velocity[w, :TILE]
    far = {(w, 0, TILE): exchange(first)}
    held, velocity = lax.optimization_barrier((first, velocity))
    index = mine * width + lax.iota(jnp.int32, width)
    weight = jnp.where(index < 2, 1.0, 2.0).astype(f32)[None, :]
    split = 2 * TILE
    packed = energies(velocity, weight, TILE, split)
    packed_far = exchange(packed)
    count = split - TILE
    far[w, TILE, count] = [x[:count] for x in packed_far]
    tail, velocity = lax.optimization_barrier((packed, velocity))
    for comp, begin, rows in (
        [(w, split, points - split)]
        + [(c, 0, points) for c in range(w - 1)]
        + [(w - 1, 0, points // 2 // TILE * TILE)]
        + [(w - 1, r, TILE) for r in range(points // 2 // TILE * TILE, points, TILE)]
    ):
        far[comp, begin, rows] = exchange(velocity[comp, begin : begin + rows])

    parts = jnp.stack([x[count:, :LANES] for x in [packed] + packed_far])
    order = (mine - lax.iota(jnp.int32, mode_count)) % mode_count
    parts = jnp.sum(parts.reshape(mode_count, elements // SUB, 2, SUB, LANES), axis=-1)
    if mode_count == 2:
        sums = parts[0] + parts[1]
    else:
        sums = jnp.sum(jnp.take(parts, order, axis=0), axis=0)
    total = sums[:, 0].reshape(elements)
    high = sums[:, 1].reshape(elements)
    field = sum_over_plane(jnp.sum(total))
    speed = jnp.sqrt(field / (1.0 * comps * points * plane_count * coefs))
    sensor = jnp.log10((high + 1e-06) / (total + 1e-06))
    ramp = 0.5 * (1.0 + jnp.sin(0.5 * math.pi * jnp.clip(sensor + 2.0, -1.0, 1.0)))
    shape = 0.4 * (1.0 + flags.astype(f32)) * ramp
    forward = [(i, i + 1) for i in range(plane_count - 1)]
    west = lax.ppermute(shape, "plane", forward)
    east = lax.ppermute(shape, "plane", [(b, a) for a, b in forward])
    source = speed * shape
    padded = speed * jnp.concatenate([west, shape, east])
    element = lax.iota(jnp.int32, elements)
    base = jnp.array([0, 2 * elements, elements, elements], dtype=jnp.int32)
    target = jnp.where(neighbours >= 0, base[None, :] + neighbours, elements + element[:, None])
    positions = lax.iota(jnp.int32, 3 * elements)
    picked = jnp.where(target[:, :, None] == positions[None, None, :], padded[None, None, :], 0.0)
    beside = jnp.sum(jnp.sum(picked, axis=2), axis=1)
    viscosity = (2.0 * source + beside) / 6.0
    node = np.arange(NODES)
    degrees = (node // (ORDER + 1)) ** 2 + (node % (ORDER + 1)) ** 2
    factor = (degrees / (2.0 * ORDER * ORDER)).astype(np.float32)
    damp = (viscosity[:, None] * factor[None, :]).reshape(points)
    damp = jnp.broadcast_to(damp[:, None], (points, LANES))

    synth_all, derive_all = tables(coefs)
    synth_all = jnp.asarray(synth_all.reshape(2, mode_count, width, coefs))
    synth = jnp.concatenate(
        [lax.dynamic_index_in_dim(synth_all, order[s], 1, keepdims=False) for s in range(mode_count)], axis=1
    )
    derive_all = jnp.asarray(
        np.ascontiguousarray(derive_all.reshape(2, coefs, mode_count, width).transpose(2, 0, 1, 3))
    )
    derive = lax.dynamic_index_in_dim(derive_all, mine, 0, keepdims=False)
    inv = expand(inverses, width)

    out = wphys = None
    for (comp, begin, rows), blocks in far.items():
        out, wphys = advance(
            velocity, blocks, comp, begin, rows, wphys, damp, synth, derive, inv, out
        )
    return (out, viscosity)


def solution(mesh):
    in_specs = (P(None, "plane", "mode"), P("mode", None, None), P("plane", None), P("plane"))
    out_specs = (P(None, "plane", "mode"), P("plane"))
    return jax.shard_map(
        on_device, mesh=mesh, in_specs=in_specs, out_specs=out_specs, check_vma=False
    )
```

time: 444 us -> 119 us (0.27)
  the two profiles are of different devices: /device:TPU:1 before, /device:TPU:0 now
where the time goes in v1:
time: 119 us; the launch traced here: 118 us
  Pallas kernels  51.6 us (43%)
  local copies, waits for them, and re-layouts  24.6 us (21%)
  starting transfers between devices  21.5 us (18%)
  waiting for transfers between devices  9.17 us (8%)
  between operations  7.82 us (7%)
  other arithmetic  3.6 us (3%)
    pallas_call x7, Pallas kernels, advance(): pl.pallas_call(lambda *refs: chunk_kernel(len(far), is_w, len(aliases), *...  47 us
    unnamed x26, local copies, waits for them, and re-layouts  10.8 us
    ppermute x4, starting transfers between devices, sum_over_plane(): lax.ppermute(value, 'plane', [(i, i ^ step) for i in range(count)])  9.76 us
    ppermute x7, starting transfers between devices, exchange(): lax.ppermute(block, 'mode', [(i, (i + s) % count) for i in range(count)])  8.08 us
    ppermute x7, waiting for transfers between devices, exchange(): lax.ppermute(block, 'mode', [(i, (i + s) % count) for i in range(count)])  6.73 us
    squeeze x3, local copies, waits for them, and re-layouts, on_device(): far[comp, begin, rows] = exchange(velocity[comp, begin:begin + rows])  4.79 us
    pallas_call x1, Pallas kernels, expand(): pl.pallas_call(expand_kernel, out_shape=jax.ShapeDtypeStruct((width // LA...  3.48 us
    squeeze x1, local copies, waits for them, and re-layouts, on_device(): lax.dynamic_index_in_dim(synth_all, order[s], 1, keepdims=False)  2.67 us
  transfers between devices with their start and end apart: 13, of which 7 were waited for; matrix products, arithmetic and copies ran while one was open for 13% of the time, Pallas kernels for 40%

profile of v1, /device:TPU:0, one launch (start us, length us, event | category | flops | bytes accessed | tf_op | source)
XLA Modules:
  0.0 118.3 jit_solution(995380199911538236)
XLA Ops:
  0.6 1.8 %slice_bitcast_fusion.5 = f32[200,512]{1,0:T(8,128)} fusion(f32[3,800,512]{2,1,0:T(8,128)} %refs_0_.7), kind=kLoop, calls=%fused_computation.9 | loop fusion | bytes 819200 | tf_op jit(solution)/shard_map/squeeze | solution.py:249
  2.4 3.0 %collective-permute-start.9 = (f32[200,512]{1,0:T(8,128)}, f32[200,512]{1,0:T(8,128)}, u32[]{:S(2)}, u32[]{:S(2)}) collective-permute-start(f32[200,512]{1,0:T(8,128)} %slice_bitcast_fusion.5), channel_id=1, source_target_pairs={{0,1},{1,0},{2,3},{3,2},{4,5},{5,4},{6,7},{7,6},{8,9},{9,8},{10,11... | collective-permute-start | bytes 1228808 | tf_op jit(solution)/shard_map/ppermute | solution.py:224
  5.4 2.4 %copy-done = f32[3,800,512]{2,1,0:T(8,128)S(1)} copy-done((f32[3,800,512]{2,1,0:T(8,128)S(1)}, f32[3,800,512]{2,1,0:T(8,128)}, u32[]{:S(2)}) %copy-start) | copy-done | bytes 4915224
  7.8 1.2 energies.1
  9.0 0.1 collective-permute-start.2
  9.1 1.2 copy-done.1
  10.2 1.3 %slice_bitcast_fusion.1 = (f32[400,512]{1,0:T(8,128)}, f32[400,512]{1,0:T(8,128)}) fusion(f32[3,800,512]{2,1,0:T(8,128)S(1)} %copy-done.1), kind=kLoop, calls=%fused_computation.5 | loop fusion | bytes 3276800 | tf_op jit(solution)/shard_map/squeeze | solution.py:266
  11.6 0.9 collective-permute-start.1
  12.4 1.3 %slice_bitcast_fusion = f32[800,512]{1,0:T(8,128)} fusion(f32[3,800,512]{2,1,0:T(8,128)S(1)} %copy-done.1), kind=kLoop, calls=%fused_computation.4 | loop fusion | bytes 3276800 | tf_op jit(solution)/shard_map/squeeze | solution.py:266
  13.8 1.2 collective-permute-start.12
  14.9 0.6 fusion.4
  19.4 2.7 %dynamic-slice_bitcast_fusion.2 = (bf16[2,512,1024]{2,1,0:T(8,128)(2,1)S(1)}, bf16[2,512,1024]{2,1,0:T(8,128)(2,1)S(1)}) fusion(bf16[2,2,512,1024]{3,2,0,1:T(8,128)(2,1)} %constant.73.clone, s32[]{:T(128)S(6)} %select_n.41, s32[]{:T(128)S(6)} %select_n.42), kind=kLoop, calls=%fused_computation.3 | loop fusion | bytes 8388616 | tf_op jit(solution)/shard_map/jit(dynamic_index_in_dim)/squeeze | solution.py:303
  22.1 2.5 %pad_maximum_fusion.refs_3_.refs_4_ = bf16[2,1024,1024]{2,1,0:T(8,128)(2,1)} fusion(bf16[2,512,1024]{2,1,0:T(8,128)(2,1)S(1)} %get-tuple-element.23, bf16[2,512,1024]{2,1,0:T(8,128)(2,1)S(1)} %get-tuple-element.22), kind=kLoop, calls=%fused_computation | loop fusion | flops 8388608 | bytes 8388608 | tf_op jit(solution)/shard_map/concatenate | solution.py:302
  24.5 0.0 copy-start.12
  24.6 0.0 copy-start.10
  24.6 1.8 %dynamic-slice_bitcast_fusion.refs_4_.refs_5_ = bf16[2,1024,512]{2,1,0:T(8,128)(2,1)S(1)} fusion(bf16[2,2,1024,512]{3,2,1,0:T(8,128)(2,1)} %constant.74.clone, s32[]{:T(128)S(6)} %select_n.43), kind=kLoop, calls=%fused_computation.1 | loop fusion | bytes 4194308 | tf_op jit(solution)/shard_map/jit(dynamic_index_in_dim)/squeeze | solution.py:308
  26.4 3.5 %expand.1.refs_5_.refs_6_ = f32[4,25,25,128]{3,2,1,0:T(8,128)S(1)} custom-call(f32[25,25,256]{2,1,0:T(8,128)S(1)} %bitcast.29, bf16[256,512]{1,0:T(8,128)(2,1)S(1)} %copy-done.7), custom_call_target="tpu_custom_call" | custom-call | tf_op jit(solution)/shard_map/expand/pallas_call | solution.py:117
  29.9 1.2 copy-done.4
  31.1 0.1 add_select_fusion
  31.2 2.1 %slice_bitcast_fusion.3 = (f32[200,512]{1,0:T(8,128)}, f32[200,512]{1,0:T(8,128)}) fusion(f32[3,800,512]{2,1,0:T(8,128)} %refs_0_.7), kind=kLoop, calls=%fused_computation.7 | loop fusion | bytes 1638400 | tf_op jit(solution)/shard_map/squeeze | solution.py:266
  33.3 0.0 collective-permute-done.2
  33.3 0.8 slice.61
  34.0 0.1 maximum_reduce_fusion
  34.2 0.6 fusion.3
  34.8 0.0 collective-permute-start.3
  34.8 0.1 reshape.86
  34.9 2.4 %collective-permute-start.7 = (f32[32]{0:T(128)S(1)}, f32[32]{0:T(128)S(1)}, u32[]{:S(2)}, u32[]{:S(2)}) collective-permute-start(f32[32]{0:T(128)S(1)} %multiply_multiply_fusion), channel_id=1, source_target_pairs={{0,2},{2,4},{4,6},{6,8},{8,10},{10,12},{12,14},{14,16},{16,18},{18... | collective-permute-start | bytes 392 | tf_op jit(solution)/shard_map/ppermute | solution.py:283
  37.3 1.0 slice.66.refs_1_
  38.3 0.0 collective-permute-done.3
  39.7 2.9 %collective-permute-start.4 = (f32[]{:T(128)}, f32[]{:T(128)}, u32[]{:S(2)}, u32[]{:S(2)}) collective-permute-start(f32[]{:T(128)} %add.91), channel_id=1, source_target_pairs={{0,4},{2,6},{4,0},{6,2},{8,12},{10,14},{12,8},{14,10},{16,20},{18,... | collective-permute-start | bytes 20 | tf_op jit(solution)/shard_map/ppermute | solution.py:235
  42.5 0.9 collective-permute-done.4
  43.9 2.9 %collective-permute-start.5 = (f32[]{:T(128)}, f32[]{:T(128)}, u32[]{:S(2)}, u32[]{:S(2)}) collective-permute-start(f32[]{:T(128)} %add.92), channel_id=1, source_target_pairs={{0,8},{2,10},{4,12},{6,14},{8,0},{10,2},{12,4},{14,6},{16,24},{18,... | collective-permute-start | bytes 20 | tf_op jit(solution)/shard_map/ppermute | solution.py:235
  46.9 0.8 collective-permute-done.5
  48.2 4.0 %collective-permute-start.6 = (f32[]{:T(128)}, f32[]{:T(128)}, u32[]{:S(2)}, u32[]{:S(2)}) collective-permute-start(f32[]{:T(128)} %add.93), channel_id=1, source_target_pairs={{0,16},{2,18},{4,20},{6,22},{8,24},{10,26},{12,28},{14,30},{16,0},... | collective-permute-start | bytes 20 | tf_op jit(solution)/shard_map/ppermute | solution.py:235
  52.2 0.7 collective-permute-done.6
  52.8 1.3 %collective-permute-start.8 = (f32[32]{0:T(128)S(1)}, f32[32]{0:T(128)S(1)}, u32[]{:S(2)}, u32[]{:S(2)}) collective-permute-start(f32[32]{0:T(128)S(1)} %multiply_multiply_fusion), channel_id=1, source_target_pairs={{2,0},{4,2},{6,4},{8,6},{10,8},{12,10},{14,12},{16,14},{18,16},{20... | collective-permute-start | bytes 392 | tf_op jit(solution)/shard_map/ppermute | solution.py:284
  54.7 0.0 collective-permute-done.7
  54.8 0.9 collective-permute-start.11
  55.7 0.2 collective-permute-done.8
  55.8 1.0 collective-permute-start.10
  56.8 0.1 maximum_multiply_fusion
  56.9 0.2 select_reduce_fusion
  57.1 0.0 copy-start.9
  57.1 0.1 broadcast_multiply_fusion
  57.2 0.1 mul.94
  57.3 0.0 collective-permute-done.9.refs_1_
  57.3 1.1 collective-permute-start
  58.4 0.2 broadcast_in_dim.45.refs_2_.refs_3_
  58.6 0.0 copy-start.2
  58.6 2.4 %copy-done.2 = f32[3,800,512]{2,1,0:T(8,128)S(1)} copy-done((f32[3,800,512]{2,1,0:T(8,128)S(1)}, f32[3,800,512]{2,1,0:T(8,128)}, u32[]{:S(2)}) %copy-start.2) | copy-done | bytes 4915224
  61.0 2.2 %copy-done.3 = bf16[2,1024,1024]{2,1,0:T(8,128)(2,1)S(1)} copy-done((bf16[2,1024,1024]{2,1,0:T(8,128)(2,1)S(1)}, bf16[2,1024,1024]{2,1,0:T(8,128)(2,1)}, u32[]{:S(2)}) %copy-start.3) | copy-done | bytes 4194328
  63.2 1.4 %copy-done.5 = f32[4,25,25,128]{3,2,1,0:T(8,128)S(1)} copy-done((f32[4,25,25,128]{3,2,1,0:T(8,128)S(1)}, f32[4,25,25,128]{3,2,1,0:T(8,128)}, u32[]{:S(2)}) %copy-start.5) | copy-done | bytes 1280024
  64.6 5.1 %advance_2_0.1 = (f32[3,800,512]{2,1,0:T(8,128)}, f32[800,1024]{1,0:T(8,128)S(1)}) custom-call(f32[3,800,512]{2,1,0:T(8,128)S(1)} %copy-done.2, f32[200,512]{1,0:T(8,128)} %collective-permute-done.9.refs_1_, f32[800,128]{1,0:T(8,128)S(1)} %broadcast_in_dim.45.refs_2_.refs_3_, bf16[2,1024,1024]{2,1,0:T(8,128)(2,1)S(1)} %copy-done.3, ...), custom_call_target="tpu_custom_call" | custom-call | flops 1887436800 | bytes 819200 | tf_op jit(solution)/shard_map/advance_2_0/pallas_call | solution.py:204
  69.7 3.9 %advance_2_200.1 = (f32[3,800,512]{2,1,0:T(8,128)}, f32[800,1024]{1,0:T(8,128)S(1)}) custom-call(f32[3,800,512]{2,1,0:T(8,128)S(1)} %copy-done.2, f32[200,512]{1,0:T(8,128)S(1)} %slice.66.refs_1_, f32[800,128]{1,0:T(8,128)S(1)} %broadcast_in_dim.45.refs_2_.refs_3_, ...), custom_call_target="tpu_custom_call", output_to_operand_aliasing={{0}: (6, {}), {1}: (7, {})} | custom-call | flops 1887436800 | bytes 819200 | tf_op jit(solution)/shard_map/advance_2_200/pallas_call | solution.py:204
  73.5 0.0 collective-permute-done.1.refs_1_
  73.6 8.0 %advance_2_400.1 = (f32[3,800,512]{2,1,0:T(8,128)}, f32[800,1024]{1,0:T(8,128)S(1)}) custom-call(f32[3,800,512]{2,1,0:T(8,128)S(1)} %copy-done.2, f32[400,512]{1,0:T(8,128)} %collective-permute-done.1.refs_1_, f32[800,128]{1,0:T(8,128)S(1)} %broadcast_in_dim.45.refs_2_.refs_3_, ...), custom_call_target="tpu_custom_call", output_to_operand_aliasing={{0}: (6, {}), {1}: (7, {})} | custom-call | flops 3774873600 | bytes 1638400 | tf_op jit(solution)/shard_map/advance_2_400/pallas_call | solution.py:204
  81.6 0.0 collective-permute-done.12.refs_1_
  81.6 14.3 %advance_0_0.1.refs_7_ = f32[3,800,512]{2,1,0:T(8,128)} custom-call(f32[3,800,512]{2,1,0:T(8,128)S(1)} %copy-done.2, f32[800,512]{1,0:T(8,128)} %collective-permute-done.12.refs_1_, f32[800,1024]{1,0:T(8,128)S(1)} %get-tuple-element.16.refs_2_, f32[800,128]{1,0:T(8,128)S(1)} %broadcast_in_dim.45.refs_2_.refs_3_, ...), custom_call_target="tpu_custom_call", output_to_operand_aliasing={{}: (7, {})} | custom-call | flops 7549747200 | bytes 3276800 | tf_op jit(solution)/shard_map/advance_0_0/pallas_call | solution.py:204
  95.9 1.9 %collective-permute-done.11.refs_1_ = f32[400,512]{1,0:T(8,128)S(1)} collective-permute-done((f32[400,512]{1,0:T(8,128)}, f32[400,512]{1,0:T(8,128)S(1)}, u32[]{:S(2)}, u32[]{:S(2)}) %collective-permute-start.11) | collective-permute-done | bytes 819232 | tf_op jit(solution)/shard_map/ppermute | solution.py:224
  97.7 7.0 %advance_1_0.1.refs_7_ = f32[3,800,512]{2,1,0:T(8,128)} custom-call(f32[3,800,512]{2,1,0:T(8,128)S(1)} %copy-done.2, f32[400,512]{1,0:T(8,128)S(1)} %collective-permute-done.11.refs_1_, f32[800,1024]{1,0:T(8,128)S(1)} %get-tuple-element.16.refs_2_, f32[800,128]{1,0:T(8,128)S(1)} %broadcast_in_dim.45.refs_2_.refs_3_, ...), custom_call_target="tpu_custom_call", output_to_operand_aliasing={{}: (7, {})} | custom-call | flops 3774873600 | bytes 1638400 | tf_op jit(solution)/shard_map/advance_1_0/pallas_call | solution.py:204
  104.7 1.9 %collective-permute-done.10.refs_1_ = f32[200,512]{1,0:T(8,128)} collective-permute-done((f32[200,512]{1,0:T(8,128)}, f32[200,512]{1,0:T(8,128)}, u32[]{:S(2)}, u32[]{:S(2)}) %collective-permute-start.10) | collective-permute-done | bytes 409632 | tf_op jit(solution)/shard_map/ppermute | solution.py:224
  106.6 4.9 %advance_1_400.1.refs_7_ = f32[3,800,512]{2,1,0:T(8,128)} custom-call(f32[3,800,512]{2,1,0:T(8,128)S(1)} %copy-done.2, f32[200,512]{1,0:T(8,128)} %collective-permute-done.10.refs_1_, f32[800,1024]{1,0:T(8,128)S(1)} %get-tuple-element.16.refs_2_, f32[800,128]{1,0:T(8,128)S(1)} %broadcast_in_dim.45.refs_2_.refs_3_, ...), custom_call_target="tpu_custom_call", output_to_operand_aliasing={{}: (7, {})} | custom-call | flops 1887436800 | bytes 819200 | tf_op jit(solution)/shard_map/advance_1_400/pallas_call | solution.py:204
  111.5 3.0 %collective-permute-done.refs_1_ = f32[200,512]{1,0:T(8,128)S(1)} collective-permute-done((f32[200,512]{1,0:T(8,128)}, f32[200,512]{1,0:T(8,128)S(1)}, u32[]{:S(2)}, u32[]{:S(2)}) %collective-permute-start) | collective-permute-done | bytes 409632 | tf_op jit(solution)/shard_map/ppermute | solution.py:224
  114.4 3.9 %advance_1_600.1 = f32[3,800,512]{2,1,0:T(8,128)} custom-call(f32[3,800,512]{2,1,0:T(8,128)S(1)} %copy-done.2, f32[200,512]{1,0:T(8,128)S(1)} %collective-permute-done.refs_1_, f32[800,1024]{1,0:T(8,128)S(1)} %get-tuple-element.16.refs_2_, f32[800,128]{1,0:T(8,128)S(1)} %broadcast_in_dim.45.refs_2_.refs_3_, ...), custom_call_target="tpu_custom_call", output_to_operand_aliasing={{}: (7, {})} | custom-call | flops 1887436800 | bytes 819200 | tf_op jit(solution)/shard_map/advance_1_600/pallas_call | solution.py:204
  (24 shorter events, 0.1 us)
Async XLA Ops:
  2.4 54.9 %collective-permute-start.9 = (f32[200,512]{1,0:T(8,128)}, f32[200,512]{1,0:T(8,128)}, u32[]{:S(2)}, u32[]{:S(2)}) collective-permute-start(f32[200,512]{1,0:T(8,128)} %slice_bitcast_fusion.5), channel_id=1, source_target_pairs={{0,1},{1,0},{2,3},{3,2},{4,5},{5,4},{6,7},{7,6},{8,9},{9,8},{10,11... | collective-permute-start | bytes 1228808 | tf_op jit(solution)/shard_map/ppermute | solution.py:224
  5.4 2.4 %copy-start = (f32[3,800,512]{2,1,0:T(8,128)S(1)}, f32[3,800,512]{2,1,0:T(8,128)}, u32[]{:S(2)}) copy-start(f32[3,800,512]{2,1,0:T(8,128)} %refs_0_.7) | copy-start | bytes 14745604
  7.8 2.4 %copy-start.1 = (f32[3,800,512]{2,1,0:T(8,128)S(1)}, f32[3,800,512]{2,1,0:T(8,128)}, u32[]{:S(2)}) copy-start(f32[3,800,512]{2,1,0:T(8,128)} %refs_0_.7) | copy-start | bytes 14745604
  9.0 24.3 %collective-permute-start.2 = (f32[264,512]{1,0:T(8,128)S(1)}, f32[264,512]{1,0:T(8,128)}, u32[]{:S(2)}, u32[]{:S(2)}) collective-permute-start(f32[264,512]{1,0:T(8,128)S(1)} %energies.1), channel_id=1, source_target_pairs={{0,1},{1,0},{2,3},{3,2},{4,5},{5,4},{6,7},{7,6},{8,9},{9,8},{10,11... | collective-permute-start | bytes 1622024 | tf_op jit(solution)/shard_map/ppermute | solution.py:224
  11.6 62.0 %collective-permute-start.1 = (f32[400,512]{1,0:T(8,128)}, f32[400,512]{1,0:T(8,128)}, u32[]{:S(2)}, u32[]{:S(2)}) collective-permute-start(f32[400,512]{1,0:T(8,128)} %get-tuple-element.19), channel_id=1, source_target_pairs={{0,1},{1,0},{2,3},{3,2},{4,5},{5,4},{6,7},{7,6},{8,9},{9,8},{10,11... | collective-permute-start | bytes 2457608 | tf_op jit(solution)/shard_map/ppermute | solution.py:224
  13.8 67.8 %collective-permute-start.12 = (f32[800,512]{1,0:T(8,128)}, f32[800,512]{1,0:T(8,128)}, u32[]{:S(2)}, u32[]{:S(2)}) collective-permute-start(f32[800,512]{1,0:T(8,128)} %slice_bitcast_fusion), channel_id=1, source_target_pairs={{0,1},{1,0},{2,3},{3,2},{4,5},{5,4},{6,7},{7,6},{8,9},{9,8},{10,11... | collective-permute-start | bytes 4915208 | tf_op jit(solution)/shard_map/ppermute | solution.py:224
  24.5 1.9 %copy-start.6 = (f32[256,25,25]{0,2,1:T(8,128)S(1)}, f32[256,25,25]{0,2,1:T(8,128)}, u32[]{:S(2)}) copy-start(f32[256,25,25]{0,2,1:T(8,128)} %param.10) | copy-start | bytes 1920004
  24.5 6.6 %copy-start.8 = (s32[32,4]{0,1:T(4,128)S(1)}, s32[32,4]{0,1:T(4,128)}, u32[]{:S(2)}) copy-start(s32[32,4]{0,1:T(4,128)} %param.11) | copy-start | bytes 1540
  24.5 6.6 %copy-start.11 = (s32[4]{0:T(128)S(1)}, s32[4]{0:T(128)}, u32[]{:S(2)}) copy-start(s32[4]{0:T(128)} %constant.71.clone) | copy-start | bytes 52
  24.5 1.9 %copy-start.7 = (bf16[256,512]{1,0:T(8,128)(2,1)S(1)}, bf16[256,512]{1,0:T(8,128)(2,1)}, u32[]{:S(2)}) copy-start(bf16[256,512]{1,0:T(8,128)(2,1)} %constant.75.clone.spread_ref) | copy-start | bytes 786436
  24.5 10.3 %copy-start.12 = (s32[32]{0:T(128)S(1)}, s32[32]{0:T(128)}, u32[]{:S(2)}) copy-start(s32[32]{0:T(128)} %param.12) | copy-start | bytes 388
  24.6 32.6 %copy-start.10 = (f32[25]{0:T(128)S(1)}, f32[25]{0:T(128)}, u32[]{:S(2)}) copy-start(f32[25]{0:T(128)} %constant.76) | copy-start | bytes 304
  29.9 1.2 copy-start.4
  34.8 3.5 %collective-permute-start.3 = (f32[]{:T(128)}, f32[]{:T(128)}, u32[]{:S(2)}, u32[]{:S(2)}) collective-permute-start(f32[]{:T(128)} %get-tuple-element.26), channel_id=1, source_target_pairs={{0,2},{2,0},{4,6},{6,4},{8,10},{10,8},{12,14},{14,12},{16,18},{18,... | collective-permute-start | bytes 20 | tf_op jit(solution)/shard_map/ppermute | solution.py:235
  34.9 19.9 %collective-permute-start.7 = (f32[32]{0:T(128)S(1)}, f32[32]{0:T(128)S(1)}, u32[]{:S(2)}, u32[]{:S(2)}) collective-permute-start(f32[32]{0:T(128)S(1)} %multiply_multiply_fusion), channel_id=1, source_target_pairs={{0,2},{2,4},{4,6},{6,8},{8,10},{10,12},{12,14},{14,16},{16,18},{18... | collective-permute-start | bytes 392 | tf_op jit(solution)/shard_map/ppermute | solution.py:283
  39.7 3.7 %collective-permute-start.4 = (f32[]{:T(128)}, f32[]{:T(128)}, u32[]{:S(2)}, u32[]{:S(2)}) collective-permute-start(f32[]{:T(128)} %add.91), channel_id=1, source_target_pairs={{0,4},{2,6},{4,0},{6,2},{8,12},{10,14},{12,8},{14,10},{16,20},{18,... | collective-permute-start | bytes 20 | tf_op jit(solution)/shard_map/ppermute | solution.py:235
  43.9 3.7 %collective-permute-start.5 = (f32[]{:T(128)}, f32[]{:T(128)}, u32[]{:S(2)}, u32[]{:S(2)}) collective-permute-start(f32[]{:T(128)} %add.92), channel_id=1, source_target_pairs={{0,8},{2,10},{4,12},{6,14},{8,0},{10,2},{12,4},{14,6},{16,24},{18,... | collective-permute-start | bytes 20 | tf_op jit(solution)/shard_map/ppermute | solution.py:235
  48.2 4.6 %collective-permute-start.6 = (f32[]{:T(128)}, f32[]{:T(128)}, u32[]{:S(2)}, u32[]{:S(2)}) collective-permute-start(f32[]{:T(128)} %add.93), channel_id=1, source_target_pairs={{0,16},{2,18},{4,20},{6,22},{8,24},{10,26},{12,28},{14,30},{16,0},... | collective-permute-start | bytes 20 | tf_op jit(solution)/shard_map/ppermute | solution.py:235
  52.8 3.0 %collective-permute-start.8 = (f32[32]{0:T(128)S(1)}, f32[32]{0:T(128)S(1)}, u32[]{:S(2)}, u32[]{:S(2)}) collective-permute-start(f32[32]{0:T(128)S(1)} %multiply_multiply_fusion), channel_id=1, source_target_pairs={{2,0},{4,2},{6,4},{8,6},{10,8},{12,10},{14,12},{16,14},{18,16},{20... | collective-permute-start | bytes 392 | tf_op jit(solution)/shard_map/ppermute | solution.py:284
  54.8 43.0 %collective-permute-start.11 = (f32[400,512]{1,0:T(8,128)}, f32[400,512]{1,0:T(8,128)S(1)}, u32[]{:S(2)}, u32[]{:S(2)}) collective-permute-start(f32[400,512]{1,0:T(8,128)} %get-tuple-element.18), channel_id=1, source_target_pairs={{0,1},{1,0},{2,3},{3,2},{4,5},{5,4},{6,7},{7,6},{8,9},{9,8},{10,11... | collective-permute-start | bytes 2457608 | tf_op jit(solution)/shard_map/ppermute | solution.py:224
  55.8 50.8 %collective-permute-start.10 = (f32[200,512]{1,0:T(8,128)}, f32[200,512]{1,0:T(8,128)}, u32[]{:S(2)}, u32[]{:S(2)}) collective-permute-start(f32[200,512]{1,0:T(8,128)} %get-tuple-element.20), channel_id=1, source_target_pairs={{0,1},{1,0},{2,3},{3,2},{4,5},{5,4},{6,7},{7,6},{8,9},{9,8},{10,11... | collective-permute-start | bytes 1228808 | tf_op jit(solution)/shard_map/ppermute | solution.py:224
  57.1 12.5 %copy-start.9 = (f32[32]{0:T(128)}, f32[32]{0:T(128)S(1)}, u32[]{:S(2)}) copy-start(f32[32]{0:T(128)S(1)} %add_multiply_fusion.1) | copy-start | bytes 388
  57.3 57.1 %collective-permute-start = (f32[200,512]{1,0:T(8,128)}, f32[200,512]{1,0:T(8,128)S(1)}, u32[]{:S(2)}, u32[]{:S(2)}) collective-permute-start(f32[200,512]{1,0:T(8,128)} %get-tuple-element.21), channel_id=1, source_target_pairs={{0,1},{1,0},{2,3},{3,2},{4,5},{5,4},{6,7},{7,6},{8,9},{9,8},{10,11... | collective-permute-start | bytes 1228808 | tf_op jit(solution)/shard_map/ppermute | solution.py:224
  58.6 2.4 %copy-start.2 = (f32[3,800,512]{2,1,0:T(8,128)S(1)}, f32[3,800,512]{2,1,0:T(8,128)}, u32[]{:S(2)}) copy-start(f32[3,800,512]{2,1,0:T(8,128)} %refs_0_.7) | copy-start | bytes 14745604
  61.0 2.2 %copy-start.3 = (bf16[2,1024,1024]{2,1,0:T(8,128)(2,1)S(1)}, bf16[2,1024,1024]{2,1,0:T(8,128)(2,1)}, u32[]{:S(2)}) copy-start(bf16[2,1024,1024]{2,1,0:T(8,128)(2,1)} %pad_maximum_fusion.refs_3_.refs_4_) | copy-start | bytes 12582916
  63.2 1.4 %copy-start.5 = (f32[4,25,25,128]{3,2,1,0:T(8,128)S(1)}, f32[4,25,25,128]{3,2,1,0:T(8,128)}, u32[]{:S(2)}) copy-start(f32[4,25,25,128]{3,2,1,0:T(8,128)} %copy-done.4) | copy-start | bytes 3840004

commit v2 on v1

--- a/solution.py
+++ b/solution.py
@@ -28,20 +28,66 @@
     return np.stack([high, low])
 
 
-def tables(coefs):
+def parity_order(width):
+    if width == LANES:
+        index = np.arange(width)
+        return index[index // 2 % 2 == 0], index[index // 2 % 2 == 1]
+    index = np.arange(width).reshape(-1, 2, LANES)
+    even = index[:, :, np.arange(LANES) // 2 % 2 == 0]
+    odd = index[:, ::-1][:, :, np.arange(LANES) // 2 % 2 == 1]
+    return even.reshape(-1), odd.reshape(-1)
+
+
+def tables(coefs, width):
     modes = coefs // 2
     index = np.arange(coefs)
     pair = index // 2
     odd = index % 2
     freq = np.where(index == 1, modes, pair)
-    angle = 2.0 * np.pi * (freq[:, None] * index[None, :] % coefs) / coefs
+    angle = 2.0 * np.pi * (freq[:, None] * index[None, :modes] % coefs) / coefs
     use_cos = (odd == 0) | (pair == 0)
     basis = np.where(use_cos[:, None], np.cos(angle), -np.sin(angle))
     weight = np.where(pair == 0, 1.0, 2.0)
     rate = pair / (modes * LENGTH * math.sqrt(modes))
     partner = basis[index ^ 1]
     derive = (np.where(odd == 0, -rate, rate) / coefs)[:, None] * partner
-    return split_np(weight[:, None] * basis), split_np(derive.T.copy())
+    groups = coefs // width
+    synth = (weight[:, None] * basis).reshape(groups, width, modes)
+    derive = derive.reshape(groups, width, modes).transpose(0, 2, 1)
+    orders = parity_order(width)
+    synth = np.stack([split_np(synth[:, o]) for o in orders])
+    derive = [derive[:, :, o] for o in orders]
+    if width == LANES:
+        derive = [np.pad(derive[p], ((0, 0), (0, 0), (p * LANES // 2, (1 - p) * LANES // 2))) for p in (0, 1)]
+    derive = np.stack([split_np(d) for d in derive])
+    return np.moveaxis(synth, 2, 0).copy(), np.moveaxis(derive, 2, 0).copy()
+
+
+def lane_index(shape):
+    return lax.broadcasted_iota(jnp.int32, shape, 1)
+
+
+def take_lanes(x, index):
+    return jnp.take_along_axis(x, index, axis=1, mode="promise_in_bounds")
+
+
+def deinterleave(first, second):
+    lane = lane_index(first.shape)
+    half = LANES // 2
+    low = lane < half
+    place = 4 * (lane % half // 2) + lane % 2
+    first = take_lanes(first, place + jnp.where(low, 0, 2))
+    second = take_lanes(second, place + jnp.where(low, 2, 0))
+    return jnp.where(low, first, second), jnp.where(low, second, first)
+
+
+def interleave(low_part, high_part, flip):
+    lane = lane_index(low_part.shape)
+    half = LANES // 2
+    both = jnp.where(lane < half, low_part, high_part)
+    is_odd = lane // 2 % 2
+    upper = 1 - is_odd if flip else is_odd
+    return take_lanes(both, lane // 4 * 2 + lane % 2 + upper * half)
 
 
 def halves(x):
@@ -72,9 +118,16 @@
         if IS_HIGH[n]:
             high = high + part
     rows = last - first
-    at = pl.multiple_of(rows + step * 2 * SUB, SUB)
-    out_ref[pl.ds(at, SUB), :LANES] = total
-    out_ref[pl.ds(at + SUB, SUB), :LANES] = high
+
+    @pl.when(step == 0)
+    def _():
+        out_ref[rows:, :] = jnp.zeros((SUB, width), f32)
+
+    lane = lane_index((SUB, LANES))
+    held = out_ref[rows:, :LANES]
+    held = jnp.where(lane == 2 * step, jnp.sum(total, axis=1, keepdims=True), held)
+    held = jnp.where(lane == 2 * step + 1, jnp.sum(high, axis=1, keepdims=True), held)
+    out_ref[rows:, :LANES] = held
 
     @pl.when((step * TILE >= first) & (step * TILE < last))
     def _():
@@ -84,7 +137,7 @@
 def energies(velocity, weight, first, last):
     comps, points, width = velocity.shape
     steps = points // TILE
-    rows = last - first + 2 * SUB * steps
+    rows = last - first + SUB
     return pl.pallas_call(
         lambda *refs: energy_kernel(first, last, *refs),
         grid=(steps,),
@@ -122,10 +175,28 @@
     )(jnp.transpose(inverses, (1, 2, 0)), spread)
 
 
-def chunk_kernel(n_far, is_w, aliased, *refs):
+def synthesis(blocks, synth_ref, skip):
+    tiles = [x[:, t : t + LANES] for x in blocks for t in range(0, x.shape[1], LANES)]
+    pairs = [deinterleave(tiles[t], tiles[t + 1]) for t in range(0, len(tiles), 2)]
+    sums = []
+    for parity in (0, 1):
+        high, low = halves(jnp.concatenate([p[parity] for p in pairs], axis=1))
+        rows = slice(skip, skip + high.shape[1])
+        first = synth_ref[parity, 0, rows, :]
+        sums.append(dot(high, first) + dot(high, synth_ref[parity, 1, rows, :]) + dot(low, first))
+    return sums
+
+
+def early_kernel(own_ref, synth_ref, out_ref):
+    modes = out_ref.shape[1] // 2
+    out_ref[:, :modes], out_ref[:, modes:] = synthesis([own_ref[0]], synth_ref, 0)
+
+
+def chunk_kernel(n_far, is_w, is_late, aliased, *refs):
     refs = list(refs)
     own_ref = refs.pop(0)
     far_refs = [refs.pop(0) for _ in range(n_far)]
+    early_ref = refs.pop(0) if is_late else None
     wphys_ref = None if is_w else refs.pop(0)
     damp_ref, synth_ref, derive_ref, inv_ref = refs[:4]
     refs = refs[4 + aliased :]
@@ -134,36 +205,46 @@
         wphys_ref = refs.pop(0)
     rhs_ref, res_ref = refs
     width = own_ref.shape[2]
+    modes = wphys_ref.shape[1] // 2
     own = own_ref[0]
-    phys = None
-    for s, x in enumerate([own] + [r[...] for r in far_refs]):
-        high, low = halves(x)
-        rows = slice(s * width, (s + 1) * width)
-        part = dot(high, synth_ref[0, rows, :])
-        part = part + dot(high, synth_ref[1, rows, :])
-        part = part + dot(low, synth_ref[0, rows, :])
-        phys = part if phys is None else phys + part
+    far = [r[...] for r in far_refs]
+    if is_late:
+        even, odd = synthesis(far, synth_ref, width // 2)
+        even = even + early_ref[:, :modes]
+        odd = odd + early_ref[:, modes:]
+    else:
+        even, odd = synthesis([own] + far, synth_ref, 0)
+    near, away = even + odd, even - odd
     if is_w:
-        wphys_ref[...] = phys
-        flux = phys * phys
+        wphys_ref[:, :modes] = near
+        wphys_ref[:, modes:] = away
+        near, away = near * near, away * away
     else:
-        flux = phys * wphys_ref[...]
-    high, low = halves(flux)
-    span = dot(high, derive_ref[0]) + dot(high, derive_ref[1]) + dot(low, derive_ref[0])
+        near, away = near * wphys_ref[:, :modes], away * wphys_ref[:, modes:]
+    span = []
+    for parity, flux in enumerate((near + away, near - away)):
+        high, low = halves(flux)
+        first = derive_ref[parity, 0]
+        span.append(dot(high, first) + dot(high, derive_ref[parity, 1]) + dot(low, first))
     damp = damp_ref[...]
     for t in range(width // LANES):
         lanes = slice(t * LANES, (t + 1) * LANES)
+        if width == LANES:
+            term = interleave(span[0], span[1], False)
+        else:
+            at = slice(t // 2 * LANES, (t // 2 + 1) * LANES)
+            term = interleave(span[t % 2][:, at], span[1 - t % 2][:, at], t % 2 == 1)
         x = own[:, lanes]
-        rhs_ref[t] = x - span[:, lanes] - damp * x
+        rhs_ref[t] = x - term - damp * x
 
     def solve(t, carry):
         right = [rhs_ref[t, pl.ds(n, SUB, stride=NODES), :] for n in range(NODES)]
         for i in range(NODES):
-            acc = None
+            acc = [None, None]
             for n in range(NODES):
                 term = inv_ref[t, i, n : n + 1, :] * right[n]
-                acc = term if acc is None else acc + term
-            res_ref[t, pl.ds(i, SUB, stride=NODES), :] = acc
+                acc[n % 2] = term if n < 2 else acc[n % 2] + term
+            res_ref[t, pl.ds(i, SUB, stride=NODES), :] = acc[0] + acc[1]
         return carry
 
     lax.fori_loop(0, width // LANES, solve, 0)
@@ -171,17 +252,37 @@
         out_ref[0, :, t * LANES : (t + 1) * LANES] = res_ref[t]
 
 
-def advance(velocity, far, comp, first, rows, wphys, damp, synth, derive, inv, out):
+def whole(shape):
+    return pl.BlockSpec(shape, lambda t: (0,) * len(shape), pipeline_mode=pl.Buffered(1))
+
+
+def early(velocity, comp, first, rows, synth):
+    width = velocity.shape[2]
+    coefs = 2 * synth.shape[3]
+    return pl.pallas_call(
+        early_kernel,
+        grid=(rows // TILE,),
+        in_specs=[pl.BlockSpec((1, TILE, width), lambda t: (comp, first // TILE + t, 0)), whole(synth.shape)],
+        out_specs=pl.BlockSpec((TILE, coefs), lambda t: (t, 0)),
+        out_shape=jax.ShapeDtypeStruct((rows, coefs), f32),
+        compiler_params=pltpu.CompilerParams(vmem_limit_bytes=16 << 20),
+        name="early",
+    )(velocity, synth)
+
+
+def advance(velocity, far, comp, first, rows, ahead, wphys, damp, synth, derive, inv, out):
     comps, points, width = velocity.shape
-    coefs = synth.shape[1]
+    coefs = 2 * synth.shape[3]
     tiles = width // LANES
     is_w = comp == comps - 1
     at = first // TILE
-    whole = lambda shape: pl.BlockSpec(shape, lambda t: (0,) * len(shape), pipeline_mode=pl.Buffered(1))
     row = lambda w: pl.BlockSpec((TILE, w), lambda t: (at + t, 0))
     block = pl.BlockSpec((1, TILE, width), lambda t: (comp, at + t, 0))
     args = [velocity, *far]
     specs = [block] + [pl.BlockSpec((TILE, width), lambda t: (t, 0)) for _ in far]
+    if ahead is not None:
+        args.append(ahead)
+        specs.append(pl.BlockSpec((TILE, coefs), lambda t: (t, 0)))
     if not is_w:
         args.append(wphys)
         specs.append(row(coefs))
@@ -202,7 +303,7 @@
         out_shape.append(jax.ShapeDtypeStruct((points, coefs), f32))
         out_specs.append(row(coefs))
     result = pl.pallas_call(
-        lambda *refs: chunk_kernel(len(far), is_w, len(aliases), *refs),
+        lambda *refs: chunk_kernel(len(far), is_w, ahead is not None, len(aliases), *refs),
         grid=(rows // TILE,),
         in_specs=specs,
         out_specs=out_specs,
@@ -211,7 +312,7 @@
         input_output_aliases=aliases,
         compiler_params=pltpu.CompilerParams(vmem_limit_bytes=32 << 20),
         cost_estimate=pl.CostEstimate(
-            flops=6 * rows * coefs * (coefs + width), bytes_accessed=8 * rows * width, transcendentals=0
+            flops=3 * rows * coefs * (coefs + width), bytes_accessed=8 * rows * width, transcendentals=0
         ),
         name=f"advance_{comp}_{first}",
     )(*args)
@@ -265,15 +366,15 @@
     ):
         far[comp, begin, rows] = exchange(velocity[comp, begin : begin + rows])
 
-    parts = jnp.stack([x[count:, :LANES] for x in [packed] + packed_far])
+    steps = points // TILE
+    parts = jnp.stack([x[count:, : 2 * steps] for x in [packed] + packed_far])
     order = (mine - lax.iota(jnp.int32, mode_count)) % mode_count
-    parts = jnp.sum(parts.reshape(mode_count, elements // SUB, 2, SUB, LANES), axis=-1)
     if mode_count == 2:
         sums = parts[0] + parts[1]
     else:
         sums = jnp.sum(jnp.take(parts, order, axis=0), axis=0)
-    total = sums[:, 0].reshape(elements)
-    high = sums[:, 1].reshape(elements)
+    sums = jnp.transpose(sums.reshape(SUB, steps, 2), (2, 1, 0)).reshape(2, elements)
+    total, high = sums[0], sums[1]
     field = sum_over_plane(jnp.sum(total))
     speed = jnp.sqrt(field / (1.0 * comps * points * plane_count * coefs))
     sensor = jnp.log10((high + 1e-06) / (total + 1e-06))
@@ -297,21 +398,23 @@
     damp = (viscosity[:, None] * factor[None, :]).reshape(points)
     damp = jnp.broadcast_to(damp[:, None], (points, LANES))
 
-    synth_all, derive_all = tables(coefs)
-    synth_all = jnp.asarray(synth_all.reshape(2, mode_count, width, coefs))
-    synth = jnp.concatenate(
-        [lax.dynamic_index_in_dim(synth_all, order[s], 1, keepdims=False) for s in range(mode_count)], axis=1
+    synth_all, derive_all = tables(coefs, width)
+    pick = lambda s: lax.dynamic_index_in_dim(jnp.asarray(synth_all), order[s], 0, keepdims=False)
+    blocks = [pick(s) for s in range(mode_count)]
+    swapped = blocks if width > LANES else [blocks[s ^ 1] for s in range(mode_count)]
+    synth = jnp.stack(
+        [jnp.concatenate([b[p] for b in group], axis=1) for p, group in enumerate((blocks, swapped))]
     )
-    derive_all = jnp.asarray(
-        np.ascontiguousarray(derive_all.reshape(2, coefs, mode_count, width).transpose(2, 0, 1, 3))
-    )
-    derive = lax.dynamic_index_in_dim(derive_all, mine, 0, keepdims=False)
+    derive = lax.dynamic_index_in_dim(jnp.asarray(derive_all), mine, 0, keepdims=False)
     inv = expand(inverses, width)
 
     out = wphys = None
-    for (comp, begin, rows), blocks in far.items():
+    for place, (comp, begin, rows) in enumerate(far):
+        ahead = None
+        if place == len(far) - 1 and width > LANES:
+            ahead = early(velocity, comp, begin, rows, synth)
         out, wphys = advance(
-            velocity, blocks, comp, begin, rows, wphys, damp, synth, derive, inv, out
+            velocity, far[comp, begin, rows], comp, begin, rows, ahead, wphys, damp, synth, derive, inv, out
         )
     return (out, viscosity)
 

time: 119 us -> 116 us (0.975)
  waiting for transfers between devices: 9.17 us -> 6.16 us
  other arithmetic: 3.6 us -> 6.6 us
  local copies, waits for them, and re-layouts: 24.6 us -> 22.3 us
  Pallas kernels: 51.6 us -> 49.9 us
    squeeze x2, local copies, waits for them, and re-layouts: 4.5 us -> 0.25 us  [the longest x1 0.18 us: on_device(): b[p]]
    ppermute x7, waiting for transfers between devices: 6.73 us -> 3.48 us  [exchange(): lax.ppermute(block, 'mode', [(i, (i + s) % count) for i in range(count)])]
    pallas_call x7 -> x8, Pallas kernels: 47 us -> 44.2 us  [the longest x7 43.5 us: advance(): pl.pallas_call(lambda *refs: chunk_kernel(len(far), is_w, ahead is not No...]
    concatenate x1 -> x0, other arithmetic: 2.45 us -> none  [on_device(): jnp.concatenate([lax.dynamic_index_in_dim(synth_all, order[s], 1, keepdim...]
    mul x1, local copies, waits for them, and re-layouts: 0.1 us -> 1.41 us  [on_device(): damp = (viscosity[:, None] * factor[None, :]).reshape(points)]
    mul x1, other arithmetic: 0.07 us -> 1.33 us  [on_device(): damp = (viscosity[:, None] * factor[None, :]).reshape(points)]
    unnamed x26 -> x32, local copies, waits for them, and re-layouts: 10.8 us -> 11.4 us
  transfers between devices with their start and end apart: 13 -> 13, of which waited for: 7 -> 5; matrix products, arithmetic and copies ran while one was open for 13% -> 14% of each run, Pallas kernels for 40% -> 41%
where the time goes in v2:
time: 116 us; the launch traced here: 115 us
  Pallas kernels  49.9 us (43%)
  local copies, waits for them, and re-layouts  22.3 us (19%)
  starting transfers between devices  22.2 us (19%)
  between operations  7.85 us (7%)
  other arithmetic  6.6 us (6%)
  waiting for transfers between devices  6.16 us (5%)
    pallas_call x7, Pallas kernels, advance(): pl.pallas_call(lambda *refs: chunk_kernel(len(far), is_w, ahead is not No...  43.5 us
    unnamed x32, local copies, waits for them, and re-layouts  11.4 us
    ppermute x4, starting transfers between devices, sum_over_plane(): lax.ppermute(value, 'plane', [(i, i ^ step) for i in range(count)])  8.9 us
    ppermute x7, starting transfers between devices, exchange(): lax.ppermute(block, 'mode', [(i, (i + s) % count) for i in range(count)])  8.89 us
    squeeze x3, local copies, waits for them, and re-layouts, on_device(): far[comp, begin, rows] = exchange(velocity[comp, begin:begin + rows])  4.79 us
    ppermute x7, waiting for transfers between devices, exchange(): lax.ppermute(block, 'mode', [(i, (i + s) % count) for i in range(count)])  3.48 us
    pallas_call x1, Pallas kernels, expand(): pl.pallas_call(expand_kernel, out_shape=jax.ShapeDtypeStruct((width // LA...  3.48 us
    ppermute x1, starting transfers between devices, on_device(): west = lax.ppermute(shape, 'plane', forward)  2.98 us
  transfers between devices with their start and end apart: 13, of which 5 were waited for; matrix products, arithmetic and copies ran while one was open for 14% of the time, Pallas kernels for 41%

profile of v2, /device:TPU:0, one launch (start us, length us, event | category | flops | bytes accessed | tf_op | source)
XLA Modules:
  0.0 115.0 jit_solution(15267586029890361871)
XLA Ops:
  0.6 1.8 %slice_bitcast_fusion.5 = f32[200,512]{1,0:T(8,128)} fusion(f32[3,800,512]{2,1,0:T(8,128)} %refs_0_.7), kind=kLoop, calls=%fused_computation.13 | loop fusion | bytes 819200 | tf_op jit(solution)/shard_map/squeeze | solution.py:350
  2.4 3.0 %collective-permute-start.9 = (f32[200,512]{1,0:T(8,128)}, f32[200,512]{1,0:T(8,128)}, u32[]{:S(2)}, u32[]{:S(2)}) collective-permute-start(f32[200,512]{1,0:T(8,128)} %slice_bitcast_fusion.5), channel_id=1, source_target_pairs={{0,1},{1,0},{2,3},{3,2},{4,5},{5,4},{6,7},{7,6},{8,9},{9,8},{10,11... | collective-permute-start | bytes 1228808 | tf_op jit(solution)/shard_map/ppermute | solution.py:325
  5.4 2.4 %copy-done = f32[3,800,512]{2,1,0:T(8,128)S(1)} copy-done((f32[3,800,512]{2,1,0:T(8,128)S(1)}, f32[3,800,512]{2,1,0:T(8,128)}, u32[]{:S(2)}) %copy-start) | copy-done | bytes 4915224
  7.8 2.2 %energies.1 = f32[208,512]{1,0:T(8,128)} custom-call(f32[3,800,512]{2,1,0:T(8,128)S(1)} %copy-done, f32[1,512]{1,0:T(1,128)S(1)} %compare_select_fusion.refs_1_), custom_call_target="tpu_custom_call" | custom-call | tf_op jit(solution)/shard_map/energies/pallas_call | solution.py:141
  10.0 0.0 collective-permute-start.2
  10.0 0.2 copy-done.1
  10.2 1.3 %slice_bitcast_fusion.1 = (f32[400,512]{1,0:T(8,128)}, f32[400,512]{1,0:T(8,128)}) fusion(f32[3,800,512]{2,1,0:T(8,128)S(1)} %copy-done.1), kind=kLoop, calls=%fused_computation.5 | loop fusion | bytes 3276800 | tf_op jit(solution)/shard_map/squeeze | solution.py:367
  11.5 1.8 %collective-permute-start.1 = (f32[400,512]{1,0:T(8,128)}, f32[400,512]{1,0:T(8,128)}, u32[]{:S(2)}, u32[]{:S(2)}) collective-permute-start(f32[400,512]{1,0:T(8,128)} %get-tuple-element.19), channel_id=1, source_target_pairs={{0,1},{1,0},{2,3},{3,2},{4,5},{5,4},{6,7},{7,6},{8,9},{9,8},{10,11... | collective-permute-start | bytes 2457608 | tf_op jit(solution)/shard_map/ppermute | solution.py:325
  13.3 1.3 %slice_bitcast_fusion = f32[800,512]{1,0:T(8,128)} fusion(f32[3,800,512]{2,1,0:T(8,128)S(1)} %copy-done.1), kind=kLoop, calls=%fused_computation.1 | loop fusion | bytes 3276800 | tf_op jit(solution)/shard_map/squeeze | solution.py:367
  14.7 0.2 collective-permute-start.12
  14.9 0.6 fusion.2
  19.4 0.7 add_select_fusion
  20.1 0.2 dynamic-slice_bitcast_fusion.4
  20.2 0.2 maximum_bitcast_fusion
  20.4 0.2 pad_maximum_fusion.synth_ref.refs_3_.refs_4_.refs_5_
  20.6 0.0 copy-start.2
  20.7 2.4 %copy-done.2 = f32[3,800,512]{2,1,0:T(8,128)S(1)} copy-done((f32[3,800,512]{2,1,0:T(8,128)S(1)}, f32[3,800,512]{2,1,0:T(8,128)}, u32[]{:S(2)}) %copy-start.2) | copy-done | bytes 4915224
  23.0 0.7 early.1.refs_2_
  23.8 0.9 copy-done.6
  24.7 3.5 %expand.1.refs_5_.refs_6_.refs_7_ = f32[4,25,25,128]{3,2,1,0:T(8,128)S(1)} custom-call(f32[25,25,256]{2,1,0:T(8,128)S(1)} %bitcast.33, bf16[256,512]{1,0:T(8,128)(2,1)S(1)} %copy-done.9), custom_call_target="tpu_custom_call" | custom-call | tf_op jit(solution)/shard_map/expand/pallas_call | solution.py:170
  28.2 1.2 %copy-done.4 = f32[4,25,25,128]{3,2,1,0:T(8,128)} copy-done((f32[4,25,25,128]{3,2,1,0:T(8,128)}, f32[4,25,25,128]{3,2,1,0:T(8,128)S(1)}, u32[]{:S(2)}) %copy-start.4) | copy-done | bytes 1280024
  29.3 0.1 dynamic-slice_bitcast_fusion.refs_4_.refs_5_.refs_6_
  29.4 2.2 %slice_bitcast_fusion.3 = (f32[200,512]{1,0:T(8,128)}, f32[200,512]{1,0:T(8,128)}) fusion(f32[3,800,512]{2,1,0:T(8,128)} %refs_0_.7), kind=kLoop, calls=%fused_computation.11 | loop fusion | bytes 1638400 | tf_op jit(solution)/shard_map/squeeze | solution.py:367
  31.6 0.0 collective-permute-done.2
  31.6 0.7 slice_add_fusion
  32.3 0.1 copy.22
  32.4 0.6 slice_reduce_fusion
  33.0 0.0 collective-permute-start.3
  33.0 0.1 reshape.97
  33.1 0.6 multiply_multiply_fusion
  33.6 3.0 %collective-permute-start.7 = (f32[32]{0:T(128)}, f32[32]{0:T(128)}, u32[]{:S(2)}, u32[]{:S(2)}) collective-permute-start(f32[32]{0:T(128)} %multiply_multiply_fusion), channel_id=1, source_target_pairs={{0,2},{2,4},{4,6},{6,8},{8,10},{10,12},{12,14},{14,16},{16,18},{18... | collective-permute-start | bytes 392 | tf_op jit(solution)/shard_map/ppermute | solution.py:384
  36.6 1.0 slice.78.refs_1_
  38.9 2.6 %collective-permute-start.4 = (f32[]{:T(128)}, f32[]{:T(128)}, u32[]{:S(2)}, u32[]{:S(2)}) collective-permute-start(f32[]{:T(128)} %add.90), channel_id=1, source_target_pairs={{0,4},{2,6},{4,0},{6,2},{8,12},{10,14},{12,8},{14,10},{16,20},{18,... | collective-permute-start | bytes 20 | tf_op jit(solution)/shard_map/ppermute | solution.py:336
  41.5 1.0 collective-permute-done.4
  43.1 2.7 %collective-permute-start.5 = (f32[]{:T(128)}, f32[]{:T(128)}, u32[]{:S(2)}, u32[]{:S(2)}) collective-permute-start(f32[]{:T(128)} %add.91), channel_id=1, source_target_pairs={{0,8},{2,10},{4,12},{6,14},{8,0},{10,2},{12,4},{14,6},{16,24},{18,... | collective-permute-start | bytes 20 | tf_op jit(solution)/shard_map/ppermute | solution.py:336
  45.8 0.9 collective-permute-done.5
  47.3 3.7 %collective-permute-start.6 = (f32[]{:T(128)}, f32[]{:T(128)}, u32[]{:S(2)}, u32[]{:S(2)}) collective-permute-start(f32[]{:T(128)} %add.92), channel_id=1, source_target_pairs={{0,16},{2,18},{4,20},{6,22},{8,24},{10,26},{12,28},{14,30},{16,0},... | collective-permute-start | bytes 20 | tf_op jit(solution)/shard_map/ppermute | solution.py:336
  51.0 0.8 collective-permute-done.6
  51.8 1.5 %collective-permute-start.8 = (f32[32]{0:T(128)}, f32[32]{0:T(128)}, u32[]{:S(2)}, u32[]{:S(2)}) collective-permute-start(f32[32]{0:T(128)} %multiply_multiply_fusion), channel_id=1, source_target_pairs={{2,0},{4,2},{6,4},{8,6},{10,8},{12,10},{14,12},{16,14},{18,16},{20... | collective-permute-start | bytes 392 | tf_op jit(solution)/shard_map/ppermute | solution.py:385
  53.9 0.0 collective-permute-done.7
  53.9 1.9 %collective-permute-start.11 = (f32[400,512]{1,0:T(8,128)}, f32[400,512]{1,0:T(8,128)}, u32[]{:S(2)}, u32[]{:S(2)}) collective-permute-start(f32[400,512]{1,0:T(8,128)} %get-tuple-element.18), channel_id=1, source_target_pairs={{0,1},{1,0},{2,3},{3,2},{4,5},{5,4},{6,7},{7,6},{8,9},{9,8},{10,11... | collective-permute-start | bytes 2457608 | tf_op jit(solution)/shard_map/ppermute | solution.py:325
  55.8 1.0 collective-permute-start.10
  56.8 0.7 maximum_multiply_fusion
  57.5 0.9 select_reduce_fusion
  58.4 0.7 add_multiply_fusion.1
  59.0 0.5 copy-done.13
  59.6 1.3 %broadcast_multiply_fusion = f32[32,25]{1,0:T(8,128)} fusion(f32[25]{0:T(128)} %constant.76, f32[32]{0:T(128)S(1)} %add_multiply_fusion.1), kind=kLoop, calls=%fused_computation.16 | loop fusion | flops 800 | bytes 3428 | tf_op jit(solution)/shard_map/mul | solution.py:398
  60.9 1.4 %mul.94 = f32[800]{0:T(1024)} reshape(f32[32,25]{1,0:T(8,128)} %broadcast_multiply_fusion) | data formatting | bytes 6400 | tf_op jit(solution)/shard_map/mul | solution.py:398
  62.3 0.0 collective-permute-done.9.refs_1_
  62.3 1.0 collective-permute-start
  63.4 0.8 broadcast_in_dim.45.refs_2_.refs_3_.refs_4_
  64.2 0.0 copy-start.3
  64.2 2.4 %copy-done.3 = f32[3,800,512]{2,1,0:T(8,128)S(1)} copy-done((f32[3,800,512]{2,1,0:T(8,128)S(1)}, f32[3,800,512]{2,1,0:T(8,128)}, u32[]{:S(2)}) %copy-start.3) | copy-done | bytes 4915224
  66.6 1.4 %copy-done.5 = f32[4,25,25,128]{3,2,1,0:T(8,128)S(1)} copy-done((f32[4,25,25,128]{3,2,1,0:T(8,128)S(1)}, f32[4,25,25,128]{3,2,1,0:T(8,128)}, u32[]{:S(2)}) %copy-start.5) | copy-done | bytes 1280024
  68.0 4.6 %advance_2_0.1 = (f32[3,800,512]{2,1,0:T(8,128)}, f32[800,1024]{1,0:T(8,128)S(1)}) custom-call(f32[3,800,512]{2,1,0:T(8,128)S(1)} %copy-done.3, f32[200,512]{1,0:T(8,128)} %collective-permute-done.9.refs_1_, f32[800,128]{1,0:T(8,128)S(1)} %broadcast_in_dim.45.refs_2_.refs_3_.refs_4_, ...), custom_call_target="tpu_custom_call" | custom-call | flops 943718400 | bytes 819200 | tf_op jit(solution)/shard_map/advance_2_0/pallas_call | solution.py:305
  72.6 3.6 %advance_2_200.1 = (f32[3,800,512]{2,1,0:T(8,128)}, f32[800,1024]{1,0:T(8,128)S(1)}) custom-call(f32[3,800,512]{2,1,0:T(8,128)S(1)} %copy-done.3, f32[200,512]{1,0:T(8,128)S(1)} %slice.78.refs_1_, f32[800,128]{1,0:T(8,128)S(1)} %broadcast_in_dim.45.refs_2_.refs_3_.refs_4_, ...), custom_call_target="tpu_custom_call", output_to_operand_aliasing={{0}: (6, {}), {1}: (7, {})} | custom-call | flops 943718400 | bytes 819200 | tf_op jit(solution)/shard_map/advance_2_200/pallas_call | solution.py:305
  76.2 0.0 collective-permute-done.1.refs_1_
  76.2 7.4 %advance_2_400.1 = (f32[3,800,512]{2,1,0:T(8,128)}, f32[800,1024]{1,0:T(8,128)S(1)}) custom-call(f32[3,800,512]{2,1,0:T(8,128)S(1)} %copy-done.3, f32[400,512]{1,0:T(8,128)} %collective-permute-done.1.refs_1_, f32[800,128]{1,0:T(8,128)S(1)} %broadcast_in_dim.45.refs_2_.refs_3_.refs_4_, ...), custom_call_target="tpu_custom_call", output_to_operand_aliasing={{0}: (6, {}), {1}: (7, {})} | custom-call | flops 1887436800 | bytes 1638400 | tf_op jit(solution)/shard_map/advance_2_400/pallas_call | solution.py:305
  83.6 13.0 %advance_0_0.1.refs_7_ = f32[3,800,512]{2,1,0:T(8,128)} custom-call(f32[3,800,512]{2,1,0:T(8,128)S(1)} %copy-done.3, f32[800,512]{1,0:T(8,128)} %collective-permute-done.12.refs_1_, f32[800,1024]{1,0:T(8,128)S(1)} %get-tuple-element.16.refs_2_.refs_3_, f32[800,128]{1,0:T(8,128)S(1)} %broadcast_in_dim.45.refs_2_.refs_3_.refs_4_, ...), custom_call_target="tpu_custom_call", output_to_operand_aliasing={{}: (7, {})} | custom-call | flops 3774873600 | bytes 3276800 | tf_op jit(solution)/shard_map/advance_0_0/pallas_call | solution.py:305
  96.6 7.4 %advance_1_0.1.refs_7_ = f32[3,800,512]{2,1,0:T(8,128)} custom-call(f32[3,800,512]{2,1,0:T(8,128)S(1)} %copy-done.3, f32[400,512]{1,0:T(8,128)} %collective-permute-done.11.refs_1_, f32[800,1024]{1,0:T(8,128)S(1)} %get-tuple-element.16.refs_2_.refs_3_, f32[800,128]{1,0:T(8,128)S(1)} %broadcast_in_dim.45.refs_2_.refs_3_.refs_4_, ...), custom_call_target="tpu_custom_call", output_to_operand_aliasing={{}: (7, {})} | custom-call | flops 1887436800 | bytes 1638400 | tf_op jit(solution)/shard_map/advance_1_0/pallas_call | solution.py:305
  103.9 0.2 collective-permute-done.10.refs_1_
  104.1 4.6 %advance_1_400.1.refs_8_ = f32[3,800,512]{2,1,0:T(8,128)} custom-call(f32[3,800,512]{2,1,0:T(8,128)S(1)} %copy-done.3, f32[200,512]{1,0:T(8,128)} %collective-permute-done.10.refs_1_, f32[800,1024]{1,0:T(8,128)S(1)} %get-tuple-element.16.refs_2_.refs_3_, f32[800,128]{1,0:T(8,128)S(1)} %broadcast_in_dim.45.refs_2_.refs_3_.refs_4_, ...), custom_call_target="tpu_custom_call", output_to_operand_aliasing={{}: (7, {})} | custom-call | flops 943718400 | bytes 819200 | tf_op jit(solution)/shard_map/advance_1_400/pallas_call | solution.py:305
  108.7 3.3 %collective-permute-done.refs_1_ = f32[200,512]{1,0:T(8,128)S(1)} collective-permute-done((f32[200,512]{1,0:T(8,128)}, f32[200,512]{1,0:T(8,128)S(1)}, u32[]{:S(2)}, u32[]{:S(2)}) %collective-permute-start) | collective-permute-done | bytes 409632 | tf_op jit(solution)/shard_map/ppermute | solution.py:325
  112.0 3.0 %advance_1_600.1 = f32[3,800,512]{2,1,0:T(8,128)} custom-call(f32[3,800,512]{2,1,0:T(8,128)S(1)} %copy-done.3, f32[200,512]{1,0:T(8,128)S(1)} %collective-permute-done.refs_1_, f32[200,1024]{1,0:T(8,128)S(1)} %copy-done.7, f32[800,1024]{1,0:T(8,128)S(1)} %get-tuple-element.16.refs_2_.refs_3_, ...), custom_call_target="tpu_custom_call", output_to_operand_aliasing={{}: (8, {})} | custom-call | flops 943718400 | bytes 819200 | tf_op jit(solution)/shard_map/advance_1_600/pallas_call | solution.py:305
  (30 shorter events, 0.1 us)
Async XLA Ops:
  2.4 59.9 %collective-permute-start.9 = (f32[200,512]{1,0:T(8,128)}, f32[200,512]{1,0:T(8,128)}, u32[]{:S(2)}, u32[]{:S(2)}) collective-permute-start(f32[200,512]{1,0:T(8,128)} %slice_bitcast_fusion.5), channel_id=1, source_target_pairs={{0,1},{1,0},{2,3},{3,2},{4,5},{5,4},{6,7},{7,6},{8,9},{9,8},{10,11... | collective-permute-start | bytes 1228808 | tf_op jit(solution)/shard_map/ppermute | solution.py:325
  5.4 2.4 %copy-start = (f32[3,800,512]{2,1,0:T(8,128)S(1)}, f32[3,800,512]{2,1,0:T(8,128)}, u32[]{:S(2)}) copy-start(f32[3,800,512]{2,1,0:T(8,128)} %refs_0_.7) | copy-start | bytes 14745604
  7.8 2.4 %copy-start.1 = (f32[3,800,512]{2,1,0:T(8,128)S(1)}, f32[3,800,512]{2,1,0:T(8,128)}, u32[]{:S(2)}) copy-start(f32[3,800,512]{2,1,0:T(8,128)} %refs_0_.7) | copy-start | bytes 14745604
  10.0 21.6 %collective-permute-start.2 = (f32[208,512]{1,0:T(8,128)}, f32[208,512]{1,0:T(8,128)}, u32[]{:S(2)}, u32[]{:S(2)}) collective-permute-start(f32[208,512]{1,0:T(8,128)} %energies.1), channel_id=1, source_target_pairs={{0,1},{1,0},{2,3},{3,2},{4,5},{5,4},{6,7},{7,6},{8,9},{9,8},{10,11... | collective-permute-start | bytes 1277960 | tf_op jit(solution)/shard_map/ppermute | solution.py:325
  11.5 7.8 %copy-start.12 = (s32[32,4]{0,1:T(4,128)S(1)}, s32[32,4]{0,1:T(4,128)}, u32[]{:S(2)}) copy-start(s32[32,4]{0,1:T(4,128)} %param.11) | copy-start | bytes 1540
  11.5 7.8 %copy-start.14 = (s32[4]{0:T(128)S(1)}, s32[4]{0:T(128)}, u32[]{:S(2)}) copy-start(s32[4]{0:T(128)} %constant.71.clone) | copy-start | bytes 52
  11.5 8.5 %copy-start.10 = (bf16[2,2,2,256,512]{4,3,2,1,0:T(8,128)(2,1)S(1)}, bf16[2,2,2,256,512]{4,3,2,1,0:T(8,128)(2,1)}, u32[]{:S(2)}) copy-start(bf16[2,2,2,256,512]{4,3,2,1,0:T(8,128)(2,1)} %constant.73.clone) | copy-start | bytes 6291460
  11.5 64.6 %collective-permute-start.1 = (f32[400,512]{1,0:T(8,128)}, f32[400,512]{1,0:T(8,128)}, u32[]{:S(2)}, u32[]{:S(2)}) collective-permute-start(f32[400,512]{1,0:T(8,128)} %get-tuple-element.19), channel_id=1, source_target_pairs={{0,1},{1,0},{2,3},{3,2},{4,5},{5,4},{6,7},{7,6},{8,9},{9,8},{10,11... | collective-permute-start | bytes 2457608 | tf_op jit(solution)/shard_map/ppermute | solution.py:325
  14.7 68.9 %collective-permute-start.12 = (f32[800,512]{1,0:T(8,128)}, f32[800,512]{1,0:T(8,128)}, u32[]{:S(2)}, u32[]{:S(2)}) collective-permute-start(f32[800,512]{1,0:T(8,128)} %slice_bitcast_fusion), channel_id=1, source_target_pairs={{0,1},{1,0},{2,3},{3,2},{4,5},{5,4},{6,7},{7,6},{8,9},{9,8},{10,11... | collective-permute-start | bytes 4915208 | tf_op jit(solution)/shard_map/ppermute | solution.py:325
  20.6 2.4 %copy-start.2 = (f32[3,800,512]{2,1,0:T(8,128)S(1)}, f32[3,800,512]{2,1,0:T(8,128)}, u32[]{:S(2)}) copy-start(f32[3,800,512]{2,1,0:T(8,128)} %refs_0_.7) | copy-start | bytes 14745604
  23.0 1.6 %copy-start.8 = (f32[256,25,25]{0,2,1:T(8,128)S(1)}, f32[256,25,25]{0,2,1:T(8,128)}, u32[]{:S(2)}) copy-start(f32[256,25,25]{0,2,1:T(8,128)} %param.10) | copy-start | bytes 1920004
  23.0 1.6 %copy-start.9 = (bf16[256,512]{1,0:T(8,128)(2,1)S(1)}, bf16[256,512]{1,0:T(8,128)(2,1)}, u32[]{:S(2)}) copy-start(bf16[256,512]{1,0:T(8,128)(2,1)} %constant.75.clone.spread_ref) | copy-start | bytes 786436
  23.8 0.9 copy-start.6
  24.7 4.7 %copy-start.11 = (bf16[2,2,2,512,256]{4,3,2,1,0:T(8,128)(2,1)S(1)}, bf16[2,2,2,512,256]{4,3,2,1,0:T(8,128)(2,1)}, u32[]{:S(2)}) copy-start(bf16[2,2,2,512,256]{4,3,2,1,0:T(8,128)(2,1)} %constant.74.clone) | copy-start | bytes 6291460
  28.1 1.2 %copy-start.4 = (f32[4,25,25,128]{3,2,1,0:T(8,128)}, f32[4,25,25,128]{3,2,1,0:T(8,128)S(1)}, u32[]{:S(2)}) copy-start(f32[4,25,25,128]{3,2,1,0:T(8,128)S(1)} %expand.1.refs_5_.refs_6_.refs_7_) | copy-start | bytes 3840004
  29.3 3.7 %copy-start.15 = (s32[32]{0:T(128)S(1)}, s32[32]{0:T(128)}, u32[]{:S(2)}) copy-start(s32[32]{0:T(128)} %param.12) | copy-start | bytes 388
  33.0 4.7 %collective-permute-start.3 = (f32[]{:T(128)}, f32[]{:T(128)}, u32[]{:S(2)}, u32[]{:S(2)}) collective-permute-start(f32[]{:T(128)} %get-tuple-element.26), channel_id=1, source_target_pairs={{0,2},{2,0},{4,6},{6,4},{8,10},{10,8},{12,14},{14,12},{16,18},{18,... | collective-permute-start | bytes 20 | tf_op jit(solution)/shard_map/ppermute | solution.py:336
  33.6 20.3 %collective-permute-start.7 = (f32[32]{0:T(128)}, f32[32]{0:T(128)}, u32[]{:S(2)}, u32[]{:S(2)}) collective-permute-start(f32[32]{0:T(128)} %multiply_multiply_fusion), channel_id=1, source_target_pairs={{0,2},{2,4},{4,6},{6,8},{8,10},{10,12},{12,14},{14,16},{16,18},{18... | collective-permute-start | bytes 392 | tf_op jit(solution)/shard_map/ppermute | solution.py:384
  38.9 3.6 %collective-permute-start.4 = (f32[]{:T(128)}, f32[]{:T(128)}, u32[]{:S(2)}, u32[]{:S(2)}) collective-permute-start(f32[]{:T(128)} %add.90), channel_id=1, source_target_pairs={{0,4},{2,6},{4,0},{6,2},{8,12},{10,14},{12,8},{14,10},{16,20},{18,... | collective-permute-start | bytes 20 | tf_op jit(solution)/shard_map/ppermute | solution.py:336
  43.1 3.6 %collective-permute-start.5 = (f32[]{:T(128)}, f32[]{:T(128)}, u32[]{:S(2)}, u32[]{:S(2)}) collective-permute-start(f32[]{:T(128)} %add.91), channel_id=1, source_target_pairs={{0,8},{2,10},{4,12},{6,14},{8,0},{10,2},{12,4},{14,6},{16,24},{18,... | collective-permute-start | bytes 20 | tf_op jit(solution)/shard_map/ppermute | solution.py:336
  47.3 4.5 %collective-permute-start.6 = (f32[]{:T(128)}, f32[]{:T(128)}, u32[]{:S(2)}, u32[]{:S(2)}) collective-permute-start(f32[]{:T(128)} %add.92), channel_id=1, source_target_pairs={{0,16},{2,18},{4,20},{6,22},{8,24},{10,26},{12,28},{14,30},{16,0},... | collective-permute-start | bytes 20 | tf_op jit(solution)/shard_map/ppermute | solution.py:336
  51.8 4.0 %collective-permute-start.8 = (f32[32]{0:T(128)}, f32[32]{0:T(128)}, u32[]{:S(2)}, u32[]{:S(2)}) collective-permute-start(f32[32]{0:T(128)} %multiply_multiply_fusion), channel_id=1, source_target_pairs={{2,0},{4,2},{6,4},{8,6},{10,8},{12,10},{14,12},{16,14},{18,16},{20... | collective-permute-start | bytes 392 | tf_op jit(solution)/shard_map/ppermute | solution.py:385
  53.9 42.7 %collective-permute-start.11 = (f32[400,512]{1,0:T(8,128)}, f32[400,512]{1,0:T(8,128)}, u32[]{:S(2)}, u32[]{:S(2)}) collective-permute-start(f32[400,512]{1,0:T(8,128)} %get-tuple-element.18), channel_id=1, source_target_pairs={{0,1},{1,0},{2,3},{3,2},{4,5},{5,4},{6,7},{7,6},{8,9},{9,8},{10,11... | collective-permute-start | bytes 2457608 | tf_op jit(solution)/shard_map/ppermute | solution.py:325
  55.8 48.4 %collective-permute-start.10 = (f32[200,512]{1,0:T(8,128)}, f32[200,512]{1,0:T(8,128)}, u32[]{:S(2)}, u32[]{:S(2)}) collective-permute-start(f32[200,512]{1,0:T(8,128)} %get-tuple-element.20), channel_id=1, source_target_pairs={{0,1},{1,0},{2,3},{3,2},{4,5},{5,4},{6,7},{7,6},{8,9},{9,8},{10,11... | collective-permute-start | bytes 1228808 | tf_op jit(solution)/shard_map/ppermute | solution.py:325
  59.0 0.5 copy-start.13
  62.3 49.7 %collective-permute-start = (f32[200,512]{1,0:T(8,128)}, f32[200,512]{1,0:T(8,128)S(1)}, u32[]{:S(2)}, u32[]{:S(2)}) collective-permute-start(f32[200,512]{1,0:T(8,128)} %get-tuple-element.21), channel_id=1, source_target_pairs={{0,1},{1,0},{2,3},{3,2},{4,5},{5,4},{6,7},{7,6},{8,9},{9,8},{10,11... | collective-permute-start | bytes 1228808 | tf_op jit(solution)/shard_map/ppermute | solution.py:325
  64.2 2.4 %copy-start.3 = (f32[3,800,512]{2,1,0:T(8,128)S(1)}, f32[3,800,512]{2,1,0:T(8,128)}, u32[]{:S(2)}) copy-start(f32[3,800,512]{2,1,0:T(8,128)} %refs_0_.7) | copy-start | bytes 14745604
  66.6 1.4 %copy-start.5 = (f32[4,25,25,128]{3,2,1,0:T(8,128)S(1)}, f32[4,25,25,128]{3,2,1,0:T(8,128)}, u32[]{:S(2)}) copy-start(f32[4,25,25,128]{3,2,1,0:T(8,128)} %copy-done.4) | copy-start | bytes 3840004
  103.9 8.1 %copy-start.7 = (f32[200,1024]{1,0:T(8,128)S(1)}, f32[200,1024]{1,0:T(8,128)}, u32[]{:S(2)}) copy-start(f32[200,1024]{1,0:T(8,128)} %copy-done.6) | copy-start | bytes 2457604

commit v3 on v2

--- a/solution.py
+++ b/solution.py
@@ -99,13 +99,13 @@
     return jnp.dot(a, b, preferred_element_type=f32)
 
 
-def energy_kernel(first, last, vel_ref, weight_ref, out_ref, point_ref):
+def first_kernel(at_ref, vel_ref, weight_ref, energy_ref, rest_ref, point_ref):
     step = pl.program_id(0)
-    width = vel_ref.shape[2]
+    comps, _, width = vel_ref.shape
     weight = weight_ref[...]
     acc = None
     for lane in range(0, width, LANES):
-        for comp in range(vel_ref.shape[0]):
+        for comp in range(comps):
             x = vel_ref[comp, :, lane : lane + LANES]
             term = x * x * weight[:, lane : lane + LANES]
             acc = term if acc is None else acc + term
@@ -117,40 +117,47 @@
         total = total + part
         if IS_HIGH[n]:
             high = high + part
-    rows = last - first
 
     @pl.when(step == 0)
     def _():
-        out_ref[rows:, :] = jnp.zeros((SUB, width), f32)
-
-    lane = lane_index((SUB, LANES))
-    held = out_ref[rows:, :LANES]
-    held = jnp.where(lane == 2 * step, jnp.sum(total, axis=1, keepdims=True), held)
-    held = jnp.where(lane == 2 * step + 1, jnp.sum(high, axis=1, keepdims=True), held)
-    out_ref[rows:, :LANES] = held
-
-    @pl.when((step * TILE >= first) & (step * TILE < last))
+        energy_ref[...] = jnp.zeros(energy_ref.shape, f32)
+
+    here = lane_index((SUB, LANES)) == step
+    for q, part in enumerate((total, high)):
+        energy_ref[q] = jnp.where(here, jnp.sum(part, axis=1, keepdims=True), energy_ref[q])
+
+    @pl.when(step > 0)
     def _():
-        out_ref[pl.ds(pl.multiple_of(step * TILE - first, SUB), TILE), :] = vel_ref[vel_ref.shape[0] - 1]
-
-
-def energies(velocity, weight, first, last):
+        rest_ref[pl.ds(pl.multiple_of((step - 1) * TILE, SUB), TILE), :] = vel_ref[comps - 1]
+
+    @pl.when(step == at_ref[0])
+    def _():
+        rest_ref[rest_ref.shape[0] - TILE :, :] = vel_ref[comps - 2]
+
+
+def first_pass(velocity, weight, there, lend):
     comps, points, width = velocity.shape
-    steps = points // TILE
-    rows = last - first + SUB
+    shape = (2, SUB, LANES)
+    rest = points if lend else points - TILE
     return pl.pallas_call(
-        lambda *refs: energy_kernel(first, last, *refs),
-        grid=(steps,),
-        in_specs=[
-            pl.BlockSpec((comps, TILE, width), lambda t: (0, t, 0)),
-            pl.BlockSpec((1, width), lambda t: (0, 0)),
-        ],
-        out_specs=pl.BlockSpec((rows, width), lambda t: (0, 0)),
-        out_shape=jax.ShapeDtypeStruct((rows, width), f32),
-        scratch_shapes=[pltpu.VMEM((TILE, LANES), f32)],
+        first_kernel,
+        grid_spec=pltpu.PrefetchScalarGridSpec(
+            num_scalar_prefetch=1,
+            grid=(points // TILE,),
+            in_specs=[
+                pl.BlockSpec((comps, TILE, width), lambda t, at: (0, t, 0)),
+                pl.BlockSpec((1, width), lambda t, at: (0, 0)),
+            ],
+            out_specs=[
+                pl.BlockSpec(shape, lambda t, at: (0, 0, 0)),
+                pl.BlockSpec((rest, width), lambda t, at: (0, 0)),
+            ],
+            scratch_shapes=[pltpu.VMEM((TILE, LANES), f32)],
+        ),
+        out_shape=[jax.ShapeDtypeStruct(shape, f32), jax.ShapeDtypeStruct((rest, width), f32)],
         compiler_params=pltpu.CompilerParams(vmem_limit_bytes=16 << 20),
-        name="energies",
-    )(velocity, weight)
+        name="first_pass",
+    )(there, velocity, weight)
 
 
 def expand_kernel(inv_ref, spread_ref, out_ref):
@@ -175,28 +182,54 @@
     )(jnp.transpose(inverses, (1, 2, 0)), spread)
 
 
-def synthesis(blocks, synth_ref, skip):
+def synthesis(blocks, synth_ref):
     tiles = [x[:, t : t + LANES] for x in blocks for t in range(0, x.shape[1], LANES)]
     pairs = [deinterleave(tiles[t], tiles[t + 1]) for t in range(0, len(tiles), 2)]
     sums = []
     for parity in (0, 1):
         high, low = halves(jnp.concatenate([p[parity] for p in pairs], axis=1))
-        rows = slice(skip, skip + high.shape[1])
-        first = synth_ref[parity, 0, rows, :]
-        sums.append(dot(high, first) + dot(high, synth_ref[parity, 1, rows, :]) + dot(low, first))
+        first = synth_ref[parity, 0]
+        sums.append(dot(high, first) + dot(high, synth_ref[parity, 1]) + dot(low, first))
     return sums
 
 
-def early_kernel(own_ref, synth_ref, out_ref):
-    modes = out_ref.shape[1] // 2
-    out_ref[:, :modes], out_ref[:, modes:] = synthesis([own_ref[0]], synth_ref, 0)
-
-
-def chunk_kernel(n_far, is_w, is_late, aliased, *refs):
+def spanwise(near, away, width, derive_refs):
+    parts = [halves(near + away), halves(near - away)]
+    groups = []
+    for derive_ref in derive_refs:
+        span = []
+        for parity, (high, low) in enumerate(parts):
+            first = derive_ref[parity, 0]
+            span.append(dot(high, first) + dot(high, derive_ref[parity, 1]) + dot(low, first))
+        if width == LANES:
+            groups.append([interleave(span[0], span[1], False)])
+            continue
+        tiles = []
+        for t in range(width // LANES):
+            at = slice(t // 2 * LANES, (t // 2 + 1) * LANES)
+            tiles.append(interleave(span[t % 2][:, at], span[1 - t % 2][:, at], t % 2 == 1))
+        groups.append(tiles)
+    return groups
+
+
+def element_solve(rhs_ref, res_ref, inv_ref):
+    def solve(t, carry):
+        right = [rhs_ref[t, pl.ds(n, SUB, stride=NODES), :] for n in range(NODES)]
+        for i in range(NODES):
+            acc = [None, None]
+            for n in range(NODES):
+                term = inv_ref[t, i, n : n + 1, :] * right[n]
+                acc[n % 2] = term if n < 2 else acc[n % 2] + term
+            res_ref[t, pl.ds(i, SUB, stride=NODES), :] = acc[0] + acc[1]
+        return carry
+
+    lax.fori_loop(0, inv_ref.shape[0], solve, 0)
+
+
+def chunk_kernel(n_far, is_w, aliased, *refs):
     refs = list(refs)
     own_ref = refs.pop(0)
     far_refs = [refs.pop(0) for _ in range(n_far)]
-    early_ref = refs.pop(0) if is_late else None
     wphys_ref = None if is_w else refs.pop(0)
     damp_ref, synth_ref, derive_ref, inv_ref = refs[:4]
     refs = refs[4 + aliased :]
@@ -207,13 +240,7 @@
     width = own_ref.shape[2]
     modes = wphys_ref.shape[1] // 2
     own = own_ref[0]
-    far = [r[...] for r in far_refs]
-    if is_late:
-        even, odd = synthesis(far, synth_ref, width // 2)
-        even = even + early_ref[:, :modes]
-        odd = odd + early_ref[:, modes:]
-    else:
-        even, odd = synthesis([own] + far, synth_ref, 0)
+    even, odd = synthesis([own] + [r[...] for r in far_refs], synth_ref)
     near, away = even + odd, even - odd
     if is_w:
         wphys_ref[:, :modes] = near
@@ -221,56 +248,20 @@
         near, away = near * near, away * away
     else:
         near, away = near * wphys_ref[:, :modes], away * wphys_ref[:, modes:]
-    span = []
-    for parity, flux in enumerate((near + away, near - away)):
-        high, low = halves(flux)
-        first = derive_ref[parity, 0]
-        span.append(dot(high, first) + dot(high, derive_ref[parity, 1]) + dot(low, first))
     damp = damp_ref[...]
-    for t in range(width // LANES):
-        lanes = slice(t * LANES, (t + 1) * LANES)
-        if width == LANES:
-            term = interleave(span[0], span[1], False)
-        else:
-            at = slice(t // 2 * LANES, (t // 2 + 1) * LANES)
-            term = interleave(span[t % 2][:, at], span[1 - t % 2][:, at], t % 2 == 1)
-        x = own[:, lanes]
+    for t, term in enumerate(spanwise(near, away, width, [derive_ref])[0]):
+        x = own[:, t * LANES : (t + 1) * LANES]
         rhs_ref[t] = x - term - damp * x
-
-    def solve(t, carry):
-        right = [rhs_ref[t, pl.ds(n, SUB, stride=NODES), :] for n in range(NODES)]
-        for i in range(NODES):
-            acc = [None, None]
-            for n in range(NODES):
-                term = inv_ref[t, i, n : n + 1, :] * right[n]
-                acc[n % 2] = term if n < 2 else acc[n % 2] + term
-            res_ref[t, pl.ds(i, SUB, stride=NODES), :] = acc[0] + acc[1]
-        return carry
-
-    lax.fori_loop(0, width // LANES, solve, 0)
+    element_solve(rhs_ref, res_ref, inv_ref)
     for t in range(width // LANES):
         out_ref[0, :, t * LANES : (t + 1) * LANES] = res_ref[t]
 
 
 def whole(shape):
-    return pl.BlockSpec(shape, lambda t: (0,) * len(shape), pipeline_mode=pl.Buffered(1))
-
-
-def early(velocity, comp, first, rows, synth):
-    width = velocity.shape[2]
-    coefs = 2 * synth.shape[3]
-    return pl.pallas_call(
-        early_kernel,
-        grid=(rows // TILE,),
-        in_specs=[pl.BlockSpec((1, TILE, width), lambda t: (comp, first // TILE + t, 0)), whole(synth.shape)],
-        out_specs=pl.BlockSpec((TILE, coefs), lambda t: (t, 0)),
-        out_shape=jax.ShapeDtypeStruct((rows, coefs), f32),
-        compiler_params=pltpu.CompilerParams(vmem_limit_bytes=16 << 20),
-        name="early",
-    )(velocity, synth)
-
-
-def advance(velocity, far, comp, first, rows, ahead, wphys, damp, synth, derive, inv, out):
+    return pl.BlockSpec(shape, lambda *t: (0,) * len(shape), pipeline_mode=pl.Buffered(1))
+
+
+def advance(velocity, far, comp, first, rows, wphys, damp, synth, derive, inv, out):
     comps, points, width = velocity.shape
     coefs = 2 * synth.shape[3]
     tiles = width // LANES
@@ -280,9 +271,6 @@
     block = pl.BlockSpec((1, TILE, width), lambda t: (comp, at + t, 0))
     args = [velocity, *far]
     specs = [block] + [pl.BlockSpec((TILE, width), lambda t: (t, 0)) for _ in far]
-    if ahead is not None:
-        args.append(ahead)
-        specs.append(pl.BlockSpec((TILE, coefs), lambda t: (t, 0)))
     if not is_w:
         args.append(wphys)
         specs.append(row(coefs))
@@ -303,20 +291,92 @@
         out_shape.append(jax.ShapeDtypeStruct((points, coefs), f32))
         out_specs.append(row(coefs))
     result = pl.pallas_call(
-        lambda *refs: chunk_kernel(len(far), is_w, ahead is not None, len(aliases), *refs),
+        lambda *refs: chunk_kernel(len(far), is_w, len(aliases), *refs),
         grid=(rows // TILE,),
         in_specs=specs,
         out_specs=out_specs,
         out_shape=out_shape,
         scratch_shapes=[pltpu.VMEM((tiles, TILE, LANES), f32)] * 2,
         input_output_aliases=aliases,
-        compiler_params=pltpu.CompilerParams(vmem_limit_bytes=32 << 20),
+        compiler_params=pltpu.CompilerParams(vmem_limit_bytes=20 << 20),
         cost_estimate=pl.CostEstimate(
             flops=3 * rows * coefs * (coefs + width), bytes_accessed=8 * rows * width, transcendentals=0
         ),
         name=f"advance_{comp}_{first}",
     )(*args)
     return (result[0], result[1] if is_w else wphys)
+
+
+def both_kernel(at_ref, own_ref, far_ref, wphys_ref, synth_ref, derive_ref, other_ref, span_ref, back_ref):
+    modes = wphys_ref.shape[1] // 2
+    width = far_ref.shape[1]
+    even, odd = synthesis([own_ref[0], far_ref[...]], synth_ref)
+    near = (even + odd) * wphys_ref[:, :modes]
+    away = (even - odd) * wphys_ref[:, modes:]
+    groups = spanwise(near, away, width, [derive_ref, other_ref])
+    for ref, tiles in zip((span_ref, back_ref), groups):
+        for t, term in enumerate(tiles):
+            ref[:, t * LANES : (t + 1) * LANES] = term
+
+
+def both_groups(velocity, comp, at, far, wphys, synth, derive, other):
+    width = velocity.shape[2]
+    last = far.shape[0] // TILE - 1
+    return pl.pallas_call(
+        both_kernel,
+        grid_spec=pltpu.PrefetchScalarGridSpec(
+            num_scalar_prefetch=1,
+            grid=(1,),
+            in_specs=[
+                pl.BlockSpec((1, TILE, width), lambda t, at: (comp, at[0], 0)),
+                pl.BlockSpec((TILE, width), lambda t, at: (last, 0)),
+                pl.BlockSpec((TILE, wphys.shape[1]), lambda t, at: (at[0], 0)),
+                whole(synth.shape),
+                whole(derive.shape),
+                whole(other.shape),
+            ],
+            out_specs=[pl.BlockSpec((TILE, width), lambda t, at: (0, 0))] * 2,
+        ),
+        out_shape=[jax.ShapeDtypeStruct((TILE, width), f32)] * 2,
+        compiler_params=pltpu.CompilerParams(vmem_limit_bytes=20 << 20),
+        name="both_groups",
+    )(at, velocity, far, wphys, synth, derive, other)
+
+
+def finish_kernel(at_ref, own_ref, span_ref, damp_ref, inv_ref, held_ref, out_ref, rhs_ref, res_ref):
+    damp = damp_ref[...]
+    for t in range(inv_ref.shape[0]):
+        lanes = slice(t * LANES, (t + 1) * LANES)
+        x = own_ref[0, :, lanes]
+        rhs_ref[t] = x - span_ref[:, lanes] - damp * x
+    element_solve(rhs_ref, res_ref, inv_ref)
+    for t in range(inv_ref.shape[0]):
+        out_ref[0, :, t * LANES : (t + 1) * LANES] = res_ref[t]
+
+
+def finish(velocity, comp, at, span, damp, inv, out, name):
+    width = velocity.shape[2]
+    block = pl.BlockSpec((1, TILE, width), lambda t, at: (comp, at[0], 0))
+    return pl.pallas_call(
+        finish_kernel,
+        grid_spec=pltpu.PrefetchScalarGridSpec(
+            num_scalar_prefetch=1,
+            grid=(1,),
+            in_specs=[
+                block,
+                pl.BlockSpec((TILE, width), lambda t, at: (0, 0)),
+                pl.BlockSpec((TILE, LANES), lambda t, at: (at[0], 0)),
+                whole(inv.shape),
+                pl.BlockSpec(memory_space=pl.ANY),
+            ],
+            out_specs=block,
+            scratch_shapes=[pltpu.VMEM((width // LANES, TILE, LANES), f32)] * 2,
+        ),
+        out_shape=jax.ShapeDtypeStruct(velocity.shape, f32),
+        input_output_aliases={5: 0},
+        compiler_params=pltpu.CompilerParams(vmem_limit_bytes=8 << 20),
+        name=name,
+    )(at, velocity, span, damp, inv, out)
 
 
 def exchange(block):
@@ -352,28 +412,28 @@
     held, velocity = lax.optimization_barrier((first, velocity))
     index = mine * width + lax.iota(jnp.int32, width)
     weight = jnp.where(index < 2, 1.0, 2.0).astype(f32)[None, :]
-    split = 2 * TILE
-    packed = energies(velocity, weight, TILE, split)
+    blocks = points // TILE
+    shared = mode_count == 2 and width > LANES and blocks > 2
+    here = jnp.reshape(blocks - 2 + mine, (1,))
+    there = jnp.reshape(blocks - 1 - mine if shared else -1, (1,))
+    packed, rest = first_pass(velocity, weight, there, shared)
     packed_far = exchange(packed)
-    count = split - TILE
-    far[w, TILE, count] = [x[:count] for x in packed_far]
+    far[w, TILE, points - TILE] = exchange(rest)
     tail, velocity = lax.optimization_barrier((packed, velocity))
-    for comp, begin, rows in (
-        [(w, split, points - split)]
-        + [(c, 0, points) for c in range(w - 1)]
-        + [(w - 1, 0, points // 2 // TILE * TILE)]
-        + [(w - 1, r, TILE) for r in range(points // 2 // TILE * TILE, points, TILE)]
-    ):
-        far[comp, begin, rows] = exchange(velocity[comp, begin : begin + rows])
+    for comp in range(w - 1):
+        far[comp, 0, points] = exchange(velocity[comp])
+    stop = points - 2 * TILE if shared else points
+    for begin in range(0, stop, TILE):
+        far[w - 1, begin, TILE] = exchange(velocity[w - 1, begin : begin + TILE])
 
     steps = points // TILE
-    parts = jnp.stack([x[count:, : 2 * steps] for x in [packed] + packed_far])
+    parts = jnp.stack([x[:, :, :steps] for x in [packed] + packed_far])
     order = (mine - lax.iota(jnp.int32, mode_count)) % mode_count
     if mode_count == 2:
         sums = parts[0] + parts[1]
     else:
         sums = jnp.sum(jnp.take(parts, order, axis=0), axis=0)
-    sums = jnp.transpose(sums.reshape(SUB, steps, 2), (2, 1, 0)).reshape(2, elements)
+    sums = jnp.transpose(sums, (0, 2, 1)).reshape(2, elements)
     total, high = sums[0], sums[1]
     field = sum_over_plane(jnp.sum(total))
     speed = jnp.sqrt(field / (1.0 * comps * points * plane_count * coefs))
@@ -398,24 +458,24 @@
     damp = (viscosity[:, None] * factor[None, :]).reshape(points)
     damp = jnp.broadcast_to(damp[:, None], (points, LANES))
 
-    synth_all, derive_all = tables(coefs, width)
-    pick = lambda s: lax.dynamic_index_in_dim(jnp.asarray(synth_all), order[s], 0, keepdims=False)
-    blocks = [pick(s) for s in range(mode_count)]
-    swapped = blocks if width > LANES else [blocks[s ^ 1] for s in range(mode_count)]
-    synth = jnp.stack(
-        [jnp.concatenate([b[p] for b in group], axis=1) for p, group in enumerate((blocks, swapped))]
-    )
-    derive = lax.dynamic_index_in_dim(jnp.asarray(derive_all), mine, 0, keepdims=False)
+    synth_all, derive_all = (jnp.asarray(x) for x in tables(coefs, width))
+    group = lambda table, at: lax.dynamic_index_in_dim(table, at, 0, keepdims=False)
+    rows = [group(synth_all, order[s]) for s in range(mode_count)]
+    swapped = rows if width > LANES else [rows[s ^ 1] for s in range(mode_count)]
+    synth = jnp.stack([jnp.concatenate([x[p] for x in part], axis=1) for p, part in enumerate((rows, swapped))])
+    derive = group(derive_all, mine)
     inv = expand(inverses, width)
 
-    out = wphys = None
-    for place, (comp, begin, rows) in enumerate(far):
-        ahead = None
-        if place == len(far) - 1 and width > LANES:
-            ahead = early(velocity, comp, begin, rows, synth)
-        out, wphys = advance(
-            velocity, far[comp, begin, rows], comp, begin, rows, ahead, wphys, damp, synth, derive, inv, out
-        )
+    out = wphys = back = None
+    for (comp, begin, count), blocks in far.items():
+        if shared and back is None and comp != w:
+            lent = far[w, TILE, points - TILE][0]
+            span, back = both_groups(velocity, w - 1, here, lent, wphys, synth, derive, group(derive_all, 1 - mine))
+            back = exchange(back)[0]
+        out, wphys = advance(velocity, blocks, comp, begin, count, wphys, damp, synth, derive, inv, out)
+    if shared:
+        out = finish(velocity, w - 1, here, span, damp, inv, out, "finish_here")
+        out = finish(velocity, w - 1, there, back, damp, inv, out, "finish_there")
     return (out, viscosity)
 
 

time: 116 us -> 114 us (0.983)
  waiting for transfers between devices: 6.16 us -> 14.2 us
  local copies, waits for them, and re-layouts: 22.3 us -> 17 us
  other arithmetic: 6.6 us -> 2.72 us
  Pallas kernels: 49.9 us -> 47.8 us
  starting transfers between devices: 22.2 us -> 24 us
    ppermute x7, waiting for transfers between devices: 3.48 us -> 13.1 us  [exchange(): lax.ppermute(block, 'mode', [(i, (i + s) % count) for i in range(count)])]
    unnamed x32 -> x24, local copies, waits for them, and re-layouts: 11.4 us -> 6.41 us
    squeeze x5 -> x4, local copies, waits for them, and re-layouts: 5.04 us -> 7.78 us  [the longest x1 2.75 us: on_device(): lax.dynamic_index_in_dim(table, at, 0, keepdims=False)]
    ppermute x4, starting transfers between devices: 8.9 us -> 11.1 us  [sum_over_plane(): lax.ppermute(value, 'plane', [(i, i ^ step) for i in range(count)])]
    pallas_call x9, Pallas kernels: 46.4 us -> 44.3 us  [the longest x5 35 us: advance(): pl.pallas_call(lambda *refs: chunk_kernel(len(far), is_w, len(aliases), *...]
    ppermute x4, waiting for transfers between devices: 2.67 us -> 1.08 us  [sum_over_plane(): lax.ppermute(value, 'plane', [(i, i ^ step) for i in range(count)])]
    mul x1, local copies, waits for them, and re-layouts: 1.41 us -> 0.1 us  [on_device(): damp = (viscosity[:, None] * factor[None, :]).reshape(points)]
    another operation x2, other arithmetic: 0.38 us -> 1.66 us  [on_device(): jnp.stack([jnp.concatenate([x[p] for x in part], axis=1) for p, part in e...]
  transfers between devices with their start and end apart: 13 -> 13, of which waited for: 5 -> 5; matrix products, arithmetic and copies ran while one was open for 14% -> 10% of each run, Pallas kernels for 41% -> 41%
where the time goes in v3:
time: 114 us
  Pallas kernels  47.8 us (42%)
  starting transfers between devices  24 us (21%)
  local copies, waits for them, and re-layouts  17 us (15%)
  waiting for transfers between devices  14.2 us (12%)
  between operations  7.85 us (7%)
  other arithmetic  2.72 us (2%)
    pallas_call x5, Pallas kernels, advance(): pl.pallas_call(lambda *refs: chunk_kernel(len(far), is_w, len(aliases), *...  35 us
    ppermute x7, waiting for transfers between devices, exchange(): lax.ppermute(block, 'mode', [(i, (i + s) % count) for i in range(count)])  13.1 us
    ppermute x4, starting transfers between devices, sum_over_plane(): lax.ppermute(value, 'plane', [(i, i ^ step) for i in range(count)])  11.1 us
    ppermute x7, starting transfers between devices, exchange(): lax.ppermute(block, 'mode', [(i, (i + s) % count) for i in range(count)])  9.05 us
    unnamed x24, local copies, waits for them, and re-layouts  6.41 us
    pallas_call x1, Pallas kernels, expand(): pl.pallas_call(expand_kernel, out_shape=jax.ShapeDtypeStruct((width // LA...  3.48 us
    pallas_call x2, Pallas kernels, finish(): pl.pallas_call(finish_kernel, grid_spec=pltpu.PrefetchScalarGridSpec(num_...  3.38 us
    pallas_call x1, Pallas kernels, both_groups(): pl.pallas_call(both_kernel, grid_spec=pltpu.PrefetchScalarGridSpec(num_sc...  3.26 us
  transfers between devices with their start and end apart: 13, of which 5 were waited for; matrix products, arithmetic and copies ran while one was open for 10% of the time, Pallas kernels for 41%

profile of v3, /device:TPU:0, one launch (start us, length us, event | category | flops | bytes accessed | tf_op | source)
XLA Modules:
  0.0 113.5 jit_solution(13872578917259014206)
XLA Ops:
  0.6 1.8 %slice_bitcast_fusion.3 = f32[200,512]{1,0:T(8,128)} fusion(f32[3,800,512]{2,1,0:T(8,128)} %own_ref.2), kind=kLoop, calls=%fused_computation.12 | loop fusion | bytes 819200 | tf_op jit(solution)/shard_map/squeeze | solution.py:410
  2.5 3.0 %collective-permute-start.8 = (f32[200,512]{1,0:T(8,128)}, f32[200,512]{1,0:T(8,128)S(1)}, u32[]{:S(2)}, u32[]{:S(2)}) collective-permute-start(f32[200,512]{1,0:T(8,128)} %slice_bitcast_fusion.3), channel_id=1, source_target_pairs={{0,1},{1,0},{2,3},{3,2},{4,5},{5,4},{6,7},{7,6},{8,9},{9,8},{10,11... | collective-permute-start | bytes 1228808 | tf_op jit(solution)/shard_map/ppermute | solution.py:385
  5.4 2.4 %copy-done = f32[3,800,512]{2,1,0:T(8,128)S(1)} copy-done((f32[3,800,512]{2,1,0:T(8,128)S(1)}, f32[3,800,512]{2,1,0:T(8,128)}, u32[]{:S(2)}) %copy-start) | copy-done | bytes 4915224
  7.8 2.7 %first_pass.1 = (f32[2,8,128]{2,1,0:T(8,128)S(1)}, f32[800,512]{1,0:T(8,128)}) custom-call(s32[1]{0:T(128)} %bitcast.at_ref, f32[3,800,512]{2,1,0:T(8,128)S(1)} %copy-done, f32[1,512]{1,0:T(1,128)S(1)} %compare_select_fusion.weight_ref), custom_call_target="tpu_custom_call" | custom-call | tf_op jit(solution)/shard_map/first_pass/pallas_call | solution.py:142
  10.5 0.0 collective-permute-start.1
  10.5 2.0 %collective-permute-start = (f32[800,512]{1,0:T(8,128)}, f32[800,512]{1,0:T(8,128)}, u32[]{:S(2)}, u32[]{:S(2)}) collective-permute-start(f32[800,512]{1,0:T(8,128)} %get-tuple-element.15), channel_id=1, source_target_pairs={{0,1},{1,0},{2,3},{3,2},{4,5},{5,4},{6,7},{7,6},{8,9},{9,8},{10,11... | collective-permute-start | bytes 4915208 | tf_op jit(solution)/shard_map/ppermute | solution.py:385
  12.5 2.7 %slice_bitcast_fusion = f32[800,512]{1,0:T(8,128)} fusion(f32[3,800,512]{2,1,0:T(8,128)} %own_ref.2), kind=kLoop, calls=%fused_computation.1 | loop fusion | bytes 3276800 | tf_op jit(solution)/shard_map/squeeze | solution.py:424
  15.2 0.2 collective-permute-start.12
  15.5 0.6 fusion.9
  18.7 2.1 %slice_bitcast_fusion.1 = (f32[200,512]{1,0:T(8,128)}, f32[200,512]{1,0:T(8,128)}) fusion(f32[3,800,512]{2,1,0:T(8,128)} %own_ref.2), kind=kLoop, calls=%fused_computation.10 | loop fusion | bytes 1638400 | tf_op jit(solution)/shard_map/squeeze | solution.py:427
  22.1 0.0 copy-done.7
  22.1 0.0 copy-done.10
  22.1 0.1 add_select_fusion
  22.2 0.0 copy-done.6
  22.2 0.2 dynamic-slice_bitcast_fusion.5
  22.4 0.2 maximum_bitcast_fusion
  22.5 1.5 %pad_maximum_fusion.refs_3_.synth_ref.refs_4_ = bf16[2,2,512,512]{3,2,1,0:T(8,128)(2,1)} fusion(bf16[1,2,512,512]{3,2,1,0:T(8,128)(2,1)S(1)} %get-tuple-element.35, bf16[1,2,512,512]{3,2,1,0:T(8,128)(2,1)S(1)} %get-tuple-element.34), kind=kLoop, calls=%fused_computation | loop fusion | flops 1048576 | bytes 4194304 | tf_op jit(solution)/shard_map/stack | solution.py:465
  24.0 2.7 %dynamic-slice_bitcast_fusion = (bf16[2,2,512,256]{3,2,1,0:T(8,128)(2,1)}, bf16[2,2,512,256]{3,2,1,0:T(8,128)(2,1)S(1)}) fusion(bf16[2,2,2,512,256]{4,3,2,1,0:T(8,128)(2,1)} %constant.80.clone, s32[]{:T(128)S(6)} %select_n.47, s32[]{:T(128)S(6)} %select_n.46), kind=kLoop, calls=%fused_computation.4 | loop fusion | bytes 4194312 | tf_op jit(solution)/shard_map/jit(dynamic_index_in_dim)/squeeze | solution.py:462
  26.8 0.0 copy-done.4
  26.8 3.5 %expand.1.refs_5_.refs_6_.inv_ref = f32[4,25,25,128]{3,2,1,0:T(8,128)S(1)} custom-call(f32[25,25,256]{2,1,0:T(8,128)S(1)} %bitcast.31, bf16[256,512]{1,0:T(8,128)(2,1)S(1)} %copy-done.5), custom_call_target="tpu_custom_call" | custom-call | tf_op jit(solution)/shard_map/expand/pallas_call | solution.py:177
  30.3 0.0 collective-permute-done.1
  30.3 0.6 slice_reduce_fusion
  30.9 0.0 collective-permute-start.2
  30.9 0.1 copy.20
  31.0 0.1 reshape.101
  31.1 2.4 %collective-permute-start.6 = (f32[32]{0:T(128)S(1)}, f32[32]{0:T(128)S(1)}, u32[]{:S(2)}, u32[]{:S(2)}) collective-permute-start(f32[32]{0:T(128)S(1)} %multiply_multiply_fusion), channel_id=1, source_target_pairs={{0,2},{2,4},{4,6},{6,8},{8,10},{10,12},{12,14},{14,16},{16,18},{18... | collective-permute-start | bytes 392 | tf_op jit(solution)/shard_map/ppermute | solution.py:444
  33.5 0.0 collective-permute-done.2
  34.8 3.3 %collective-permute-start.3 = (f32[]{:T(128)}, f32[]{:T(128)}, u32[]{:S(2)}, u32[]{:S(2)}) collective-permute-start(f32[]{:T(128)} %add.91), channel_id=1, source_target_pairs={{0,4},{2,6},{4,0},{6,2},{8,12},{10,14},{12,8},{14,10},{16,20},{18,... | collective-permute-start | bytes 20 | tf_op jit(solution)/shard_map/ppermute | solution.py:396
  38.1 0.4 collective-permute-done.3
  39.1 3.4 %collective-permute-start.4 = (f32[]{:T(128)}, f32[]{:T(128)}, u32[]{:S(2)}, u32[]{:S(2)}) collective-permute-start(f32[]{:T(128)} %add.92), channel_id=1, source_target_pairs={{0,8},{2,10},{4,12},{6,14},{8,0},{10,2},{12,4},{14,6},{16,24},{18,... | collective-permute-start | bytes 20 | tf_op jit(solution)/shard_map/ppermute | solution.py:396
  42.5 0.3 collective-permute-done.4
  43.4 4.4 %collective-permute-start.5 = (f32[]{:T(128)}, f32[]{:T(128)}, u32[]{:S(2)}, u32[]{:S(2)}) collective-permute-start(f32[]{:T(128)} %add.93), channel_id=1, source_target_pairs={{0,16},{2,18},{4,20},{6,22},{8,24},{10,26},{12,28},{14,30},{16,0},... | collective-permute-start | bytes 20 | tf_op jit(solution)/shard_map/ppermute | solution.py:396
  47.8 0.3 collective-permute-done.5
  48.2 1.5 %collective-permute-start.7 = (f32[32]{0:T(128)S(1)}, f32[32]{0:T(128)S(1)}, u32[]{:S(2)}, u32[]{:S(2)}) collective-permute-start(f32[32]{0:T(128)S(1)} %multiply_multiply_fusion), channel_id=1, source_target_pairs={{2,0},{4,2},{6,4},{8,6},{10,8},{12,10},{14,12},{16,14},{18,16},{20... | collective-permute-start | bytes 392 | tf_op jit(solution)/shard_map/ppermute | solution.py:445
  50.3 0.0 collective-permute-done.6
  50.3 1.8 %collective-permute-start.11 = (f32[200,512]{1,0:T(8,128)}, f32[200,512]{1,0:T(8,128)}, u32[]{:S(2)}, u32[]{:S(2)}) collective-permute-start(f32[200,512]{1,0:T(8,128)} %get-tuple-element.22), channel_id=1, source_target_pairs={{0,1},{1,0},{2,3},{3,2},{4,5},{5,4},{6,7},{7,6},{8,9},{9,8},{10,11... | collective-permute-start | bytes 1228808 | tf_op jit(solution)/shard_map/ppermute | solution.py:385
  52.1 0.0 collective-permute-done.7
  52.1 0.8 collective-permute-start.10
  52.9 0.1 maximum_multiply_fusion
  52.9 0.2 select_reduce_fusion
  53.1 0.0 copy-done.9
  53.2 0.0 copy-start.8
  53.2 0.1 broadcast_multiply_fusion
  53.2 0.1 mul.94
  53.3 0.0 collective-permute-done.8.refs_1_
  53.4 0.2 broadcast_in_dim.45.refs_2_.refs_3_.damp_ref
  53.5 0.0 copy-start.1
  53.5 2.4 %copy-done.1 = f32[3,800,512]{2,1,0:T(8,128)S(1)} copy-done((f32[3,800,512]{2,1,0:T(8,128)S(1)}, f32[3,800,512]{2,1,0:T(8,128)}, u32[]{:S(2)}) %copy-start.1) | copy-done | bytes 4915224
  55.9 1.6 %copy-done.2 = bf16[2,2,512,512]{3,2,1,0:T(8,128)(2,1)S(1)} copy-done((bf16[2,2,512,512]{3,2,1,0:T(8,128)(2,1)S(1)}, bf16[2,2,512,512]{3,2,1,0:T(8,128)(2,1)}, u32[]{:S(2)}) %copy-start.2) | copy-done | bytes 2097176
  57.5 3.6 %advance_2_0.1 = (f32[3,800,512]{2,1,0:T(8,128)}, f32[800,1024]{1,0:T(8,128)S(1)}) custom-call(f32[3,800,512]{2,1,0:T(8,128)S(1)} %copy-done.1, f32[200,512]{1,0:T(8,128)S(1)} %collective-permute-done.8.refs_1_, f32[800,128]{1,0:T(8,128)S(1)} %broadcast_in_dim.45.refs_2_.refs_3_.damp_ref, bf16[2,2,512,512]{3,2,1,0:T(8,128)(2,1)S(1)} %copy-done.2, ...), custom_call_target="tpu_custom_call" | custom-call | flops 943718400 | bytes 819200 | tf_op jit(solution)/shard_map/advance_2_0/pallas_call | solution.py:293
  61.1 0.0 copy-done.8
  61.1 0.0 collective-permute-done.refs_1_.far_ref
  61.1 10.3 %advance_2_200.1 = (f32[3,800,512]{2,1,0:T(8,128)}, f32[800,1024]{1,0:T(8,128)S(1)}) custom-call(f32[3,800,512]{2,1,0:T(8,128)S(1)} %copy-done.1, f32[800,512]{1,0:T(8,128)} %collective-permute-done.refs_1_.far_ref, f32[800,128]{1,0:T(8,128)S(1)} %broadcast_in_dim.45.refs_2_.refs_3_.damp_ref, ...), custom_call_target="tpu_custom_call", output_to_operand_aliasing={{0}: (6, {}), {1}: (7, {})} | custom-call | flops 2831155200 | bytes 2457600 | tf_op jit(solution)/shard_map/advance_2_200/pallas_call | solution.py:293
  71.4 3.3 %both_groups.1 = (f32[200,512]{1,0:T(8,128)S(1)}, f32[200,512]{1,0:T(8,128)S(1)}) custom-call(s32[1]{0:T(128)} %bitcast.2.at_ref, f32[3,800,512]{2,1,0:T(8,128)S(1)} %copy-done.1, f32[800,512]{1,0:T(8,128)} %collective-permute-done.refs_1_.far_ref, f32[800,1024]{1,0:T(8,128)S(1)} %get-tuple-element.18.wphys_ref.refs_2_, ...), custom_call_target="tpu_custom_call" | custom-call | tf_op jit(solution)/shard_map/both_groups/pallas_call | solution.py:325
  74.7 1.3 %collective-permute-start.9 = (f32[200,512]{1,0:T(8,128)S(1)}, f32[200,512]{1,0:T(8,128)S(1)}, u32[]{:S(2)}, u32[]{:S(2)}) collective-permute-start(f32[200,512]{1,0:T(8,128)S(1)} %get-tuple-element.19), channel_id=1, source_target_pairs={{0,1},{1,0},{2,3},{3,2},{4,5},{5,4},{6,7},{7,6},{8,9},{9,8},{10,11... | collective-permute-start | bytes 1228808 | tf_op jit(solution)/shard_map/ppermute | solution.py:385
  76.0 10.5 %collective-permute-done.12.refs_1_ = f32[800,512]{1,0:T(8,128)} collective-permute-done((f32[800,512]{1,0:T(8,128)}, f32[800,512]{1,0:T(8,128)}, u32[]{:S(2)}, u32[]{:S(2)}) %collective-permute-start.12) | collective-permute-done | bytes 1638432 | tf_op jit(solution)/shard_map/ppermute | solution.py:385
  86.4 13.0 %advance_0_0.1.refs_7_ = f32[3,800,512]{2,1,0:T(8,128)} custom-call(f32[3,800,512]{2,1,0:T(8,128)S(1)} %copy-done.1, f32[800,512]{1,0:T(8,128)} %collective-permute-done.12.refs_1_, f32[800,1024]{1,0:T(8,128)S(1)} %get-tuple-element.18.wphys_ref.refs_2_, f32[800,128]{1,0:T(8,128)S(1)} %broadcast_in_dim.45.refs_2_.refs_3_.damp_ref, ...), custom_call_target="tpu_custom_call", output_to_operand_aliasing={{}: (7, {})} | custom-call | flops 3774873600 | bytes 3276800 | tf_op jit(solution)/shard_map/advance_0_0/pallas_call | solution.py:293
  99.4 0.0 collective-permute-done.11.refs_1_
  99.4 4.5 %advance_1_0.1.refs_7_ = f32[3,800,512]{2,1,0:T(8,128)} custom-call(f32[3,800,512]{2,1,0:T(8,128)S(1)} %copy-done.1, f32[200,512]{1,0:T(8,128)} %collective-permute-done.11.refs_1_, f32[800,1024]{1,0:T(8,128)S(1)} %get-tuple-element.18.wphys_ref.refs_2_, f32[800,128]{1,0:T(8,128)S(1)} %broadcast_in_dim.45.refs_2_.refs_3_.damp_ref, ...), custom_call_target="tpu_custom_call", output_to_operand_aliasing={{}: (7, {})} | custom-call | flops 943718400 | bytes 819200 | tf_op jit(solution)/shard_map/advance_1_0/pallas_call | solution.py:293
  104.0 0.0 collective-permute-done.10.refs_1_
  104.0 3.5 %advance_1_200.1.held_ref = f32[3,800,512]{2,1,0:T(8,128)} custom-call(f32[3,800,512]{2,1,0:T(8,128)S(1)} %copy-done.1, f32[200,512]{1,0:T(8,128)S(1)} %collective-permute-done.10.refs_1_, f32[800,1024]{1,0:T(8,128)S(1)} %get-tuple-element.18.wphys_ref.refs_2_, ...), custom_call_target="tpu_custom_call", output_to_operand_aliasing={{}: (7, {})} | custom-call | flops 943718400 | bytes 819200 | tf_op jit(solution)/shard_map/advance_1_200/pallas_call | solution.py:293
  107.5 1.7 %finish_here.1.held_ref = f32[3,800,512]{2,1,0:T(8,128)} custom-call(s32[1]{0:T(128)} %bitcast.2.at_ref, f32[3,800,512]{2,1,0:T(8,128)S(1)} %copy-done.1, f32[200,512]{1,0:T(8,128)S(1)} %get-tuple-element.20.span_ref, f32[800,128]{1,0:T(8,128)S(1)} %broadcast_in_dim.45.refs_2_.refs_3_.damp_ref, ...), custom_call_target="tpu_custom_call", output_to_operand_aliasing={{}: (5, {})} | custom-call | tf_op jit(solution)/shard_map/finish_here/pallas_call | solution.py:360
  109.2 2.6 %collective-permute-done.9.span_ref = f32[200,512]{1,0:T(8,128)S(1)} collective-permute-done((f32[200,512]{1,0:T(8,128)S(1)}, f32[200,512]{1,0:T(8,128)S(1)}, u32[]{:S(2)}, u32[]{:S(2)}) %collective-permute-start.9) | collective-permute-done | bytes 409632 | tf_op jit(solution)/shard_map/ppermute | solution.py:385
  111.8 1.7 %finish_there.1 = f32[3,800,512]{2,1,0:T(8,128)} custom-call(s32[1]{0:T(128)} %bitcast.at_ref, f32[3,800,512]{2,1,0:T(8,128)S(1)} %copy-done.1, f32[200,512]{1,0:T(8,128)S(1)} %collective-permute-done.9.span_ref, f32[800,128]{1,0:T(8,128)S(1)} %broadcast_in_dim.45.refs_2_.refs_3_.damp_ref, ...), custom_call_target="tpu_custom_call", output_to_operand_aliasing={{}: (5, {})} | custom-call | tf_op jit(solution)/shard_map/finish_there/pallas_call | solution.py:360
  (19 shorter events, 0.1 us)
Async XLA Ops:
  2.5 50.9 %collective-permute-start.8 = (f32[200,512]{1,0:T(8,128)}, f32[200,512]{1,0:T(8,128)S(1)}, u32[]{:S(2)}, u32[]{:S(2)}) collective-permute-start(f32[200,512]{1,0:T(8,128)} %slice_bitcast_fusion.3), channel_id=1, source_target_pairs={{0,1},{1,0},{2,3},{3,2},{4,5},{5,4},{6,7},{7,6},{8,9},{9,8},{10,11... | collective-permute-start | bytes 1228808 | tf_op jit(solution)/shard_map/ppermute | solution.py:385
  5.4 2.4 %copy-start = (f32[3,800,512]{2,1,0:T(8,128)S(1)}, f32[3,800,512]{2,1,0:T(8,128)}, u32[]{:S(2)}) copy-start(f32[3,800,512]{2,1,0:T(8,128)} %own_ref.2) | copy-start | bytes 14745604
  10.5 19.8 %collective-permute-start.1 = (f32[2,8,128]{2,1,0:T(8,128)S(1)}, f32[2,8,128]{2,1,0:T(8,128)S(1)}, u32[]{:S(2)}, u32[]{:S(2)}) collective-permute-start(f32[2,8,128]{2,1,0:T(8,128)S(1)} %get-tuple-element.13), channel_id=1, source_target_pairs={{0,1},{1,0},{2,3},{3,2},{4,5},{5,4},{6,7},{7,6},{8,9},{9,8},{10,11... | collective-permute-start | bytes 24584 | tf_op jit(solution)/shard_map/ppermute | solution.py:385
  10.5 11.6 %copy-start.7 = (s32[32,4]{0,1:T(4,128)S(1)}, s32[32,4]{0,1:T(4,128)}, u32[]{:S(2)}) copy-start(s32[32,4]{0,1:T(4,128)} %param.11) | copy-start | bytes 1540
  10.5 11.6 %copy-start.10 = (s32[4]{0:T(128)S(1)}, s32[4]{0:T(128)}, u32[]{:S(2)}) copy-start(s32[4]{0:T(128)} %constant.77.clone) | copy-start | bytes 52
  10.5 11.7 %copy-start.6 = (bf16[2,2,2,256,512]{4,3,2,1,0:T(8,128)(2,1)S(1)}, bf16[2,2,2,256,512]{4,3,2,1,0:T(8,128)(2,1)}, u32[]{:S(2)}) copy-start(bf16[2,2,2,256,512]{4,3,2,1,0:T(8,128)(2,1)} %constant.79.clone) | copy-start | bytes 6291460
  10.5 50.6 %collective-permute-start = (f32[800,512]{1,0:T(8,128)}, f32[800,512]{1,0:T(8,128)}, u32[]{:S(2)}, u32[]{:S(2)}) collective-permute-start(f32[800,512]{1,0:T(8,128)} %get-tuple-element.15), channel_id=1, source_target_pairs={{0,1},{1,0},{2,3},{3,2},{4,5},{5,4},{6,7},{7,6},{8,9},{9,8},{10,11... | collective-permute-start | bytes 4915208 | tf_op jit(solution)/shard_map/ppermute | solution.py:385
  15.2 71.2 %collective-permute-start.12 = (f32[800,512]{1,0:T(8,128)}, f32[800,512]{1,0:T(8,128)}, u32[]{:S(2)}, u32[]{:S(2)}) collective-permute-start(f32[800,512]{1,0:T(8,128)} %slice_bitcast_fusion), channel_id=1, source_target_pairs={{0,1},{1,0},{2,3},{3,2},{4,5},{5,4},{6,7},{7,6},{8,9},{9,8},{10,11... | collective-permute-start | bytes 4915208 | tf_op jit(solution)/shard_map/ppermute | solution.py:385
  24.0 2.8 %copy-start.4 = (f32[256,25,25]{0,2,1:T(8,128)S(1)}, f32[256,25,25]{0,2,1:T(8,128)}, u32[]{:S(2)}) copy-start(f32[256,25,25]{0,2,1:T(8,128)} %param.10) | copy-start | bytes 1920004
  24.0 2.8 %copy-start.5 = (bf16[256,512]{1,0:T(8,128)(2,1)S(1)}, bf16[256,512]{1,0:T(8,128)(2,1)}, u32[]{:S(2)}) copy-start(bf16[256,512]{1,0:T(8,128)(2,1)} %constant.81.clone.spread_ref) | copy-start | bytes 786436
  26.8 4.3 %copy-start.11 = (s32[32]{0:T(128)S(1)}, s32[32]{0:T(128)}, u32[]{:S(2)}) copy-start(s32[32]{0:T(128)} %param.12) | copy-start | bytes 388
  26.8 26.4 %copy-start.9 = (f32[25]{0:T(128)S(1)}, f32[25]{0:T(128)}, u32[]{:S(2)}) copy-start(f32[25]{0:T(128)} %constant.82) | copy-start | bytes 304
  30.9 2.6 %collective-permute-start.2 = (f32[]{:T(128)}, f32[]{:T(128)}, u32[]{:S(2)}, u32[]{:S(2)}) collective-permute-start(f32[]{:T(128)} %get-tuple-element.30), channel_id=1, source_target_pairs={{0,2},{2,0},{4,6},{6,4},{8,10},{10,8},{12,14},{14,12},{16,18},{18,... | collective-permute-start | bytes 20 | tf_op jit(solution)/shard_map/ppermute | solution.py:396
  31.1 19.2 %collective-permute-start.6 = (f32[32]{0:T(128)S(1)}, f32[32]{0:T(128)S(1)}, u32[]{:S(2)}, u32[]{:S(2)}) collective-permute-start(f32[32]{0:T(128)S(1)} %multiply_multiply_fusion), channel_id=1, source_target_pairs={{0,2},{2,4},{4,6},{6,8},{8,10},{10,12},{12,14},{14,16},{16,18},{18... | collective-permute-start | bytes 392 | tf_op jit(solution)/shard_map/ppermute | solution.py:444
  34.8 3.7 %collective-permute-start.3 = (f32[]{:T(128)}, f32[]{:T(128)}, u32[]{:S(2)}, u32[]{:S(2)}) collective-permute-start(f32[]{:T(128)} %add.91), channel_id=1, source_target_pairs={{0,4},{2,6},{4,0},{6,2},{8,12},{10,14},{12,8},{14,10},{16,20},{18,... | collective-permute-start | bytes 20 | tf_op jit(solution)/shard_map/ppermute | solution.py:396
  39.1 3.7 %collective-permute-start.4 = (f32[]{:T(128)}, f32[]{:T(128)}, u32[]{:S(2)}, u32[]{:S(2)}) collective-permute-start(f32[]{:T(128)} %add.92), channel_id=1, source_target_pairs={{0,8},{2,10},{4,12},{6,14},{8,0},{10,2},{12,4},{14,6},{16,24},{18,... | collective-permute-start | bytes 20 | tf_op jit(solution)/shard_map/ppermute | solution.py:396
  43.4 4.7 %collective-permute-start.5 = (f32[]{:T(128)}, f32[]{:T(128)}, u32[]{:S(2)}, u32[]{:S(2)}) collective-permute-start(f32[]{:T(128)} %add.93), channel_id=1, source_target_pairs={{0,16},{2,18},{4,20},{6,22},{8,24},{10,26},{12,28},{14,30},{16,0},... | collective-permute-start | bytes 20 | tf_op jit(solution)/shard_map/ppermute | solution.py:396
  48.2 3.9 %collective-permute-start.7 = (f32[32]{0:T(128)S(1)}, f32[32]{0:T(128)S(1)}, u32[]{:S(2)}, u32[]{:S(2)}) collective-permute-start(f32[32]{0:T(128)S(1)} %multiply_multiply_fusion), channel_id=1, source_target_pairs={{2,0},{4,2},{6,4},{8,6},{10,8},{12,10},{14,12},{16,14},{18,16},{20... | collective-permute-start | bytes 392 | tf_op jit(solution)/shard_map/ppermute | solution.py:445
  50.3 49.1 %collective-permute-start.11 = (f32[200,512]{1,0:T(8,128)}, f32[200,512]{1,0:T(8,128)}, u32[]{:S(2)}, u32[]{:S(2)}) collective-permute-start(f32[200,512]{1,0:T(8,128)} %get-tuple-element.22), channel_id=1, source_target_pairs={{0,1},{1,0},{2,3},{3,2},{4,5},{5,4},{6,7},{7,6},{8,9},{9,8},{10,11... | collective-permute-start | bytes 1228808 | tf_op jit(solution)/shard_map/ppermute | solution.py:385
  52.1 51.9 %collective-permute-start.10 = (f32[200,512]{1,0:T(8,128)}, f32[200,512]{1,0:T(8,128)S(1)}, u32[]{:S(2)}, u32[]{:S(2)}) collective-permute-start(f32[200,512]{1,0:T(8,128)} %get-tuple-element.23), channel_id=1, source_target_pairs={{0,1},{1,0},{2,3},{3,2},{4,5},{5,4},{6,7},{7,6},{8,9},{9,8},{10,11... | collective-permute-start | bytes 1228808 | tf_op jit(solution)/shard_map/ppermute | solution.py:385
  53.2 7.9 %copy-start.8 = (f32[32]{0:T(128)}, f32[32]{0:T(128)S(1)}, u32[]{:S(2)}) copy-start(f32[32]{0:T(128)S(1)} %add_multiply_fusion.1) | copy-start | bytes 388
  53.5 2.4 %copy-start.1 = (f32[3,800,512]{2,1,0:T(8,128)S(1)}, f32[3,800,512]{2,1,0:T(8,128)}, u32[]{:S(2)}) copy-start(f32[3,800,512]{2,1,0:T(8,128)} %own_ref.2) | copy-start | bytes 14745604
  55.9 1.6 %copy-start.2 = (bf16[2,2,512,512]{3,2,1,0:T(8,128)(2,1)S(1)}, bf16[2,2,512,512]{3,2,1,0:T(8,128)(2,1)}, u32[]{:S(2)}) copy-start(bf16[2,2,512,512]{3,2,1,0:T(8,128)(2,1)} %pad_maximum_fusion.refs_3_.synth_ref.refs_4_) | copy-start | bytes 6291460
  61.1 10.3 %copy-start.3 = (bf16[2,2,512,256]{3,2,1,0:T(8,128)(2,1)S(1)}, bf16[2,2,512,256]{3,2,1,0:T(8,128)(2,1)}, u32[]{:S(2)}) copy-start(bf16[2,2,512,256]{3,2,1,0:T(8,128)(2,1)} %get-tuple-element.24.other_ref) | copy-start | bytes 3145732
  74.7 37.1 %collective-permute-start.9 = (f32[200,512]{1,0:T(8,128)S(1)}, f32[200,512]{1,0:T(8,128)S(1)}, u32[]{:S(2)}, u32[]{:S(2)}) collective-permute-start(f32[200,512]{1,0:T(8,128)S(1)} %get-tuple-element.19), channel_id=1, source_target_pairs={{0,1},{1,0},{2,3},{3,2},{4,5},{5,4},{6,7},{7,6},{8,9},{9,8},{10,11... | collective-permute-start | bytes 1228808 | tf_op jit(solution)/shard_map/ppermute | solution.py:385

commit v4 on v3

--- a/solution.py
+++ b/solution.py
@@ -307,21 +307,24 @@
     return (result[0], result[1] if is_w else wphys)
 
 
-def both_kernel(at_ref, own_ref, far_ref, wphys_ref, synth_ref, derive_ref, other_ref, span_ref, back_ref):
+def both_kernel(at_ref, own_ref, far_ref, wphys_ref, synth_ref, derive_ref, other_ref, span_ref, *back_refs):
     modes = wphys_ref.shape[1] // 2
     width = far_ref.shape[1]
     even, odd = synthesis([own_ref[0], far_ref[...]], synth_ref)
     near = (even + odd) * wphys_ref[:, :modes]
     away = (even - odd) * wphys_ref[:, modes:]
-    groups = spanwise(near, away, width, [derive_ref, other_ref])
-    for ref, tiles in zip((span_ref, back_ref), groups):
-        for t, term in enumerate(tiles):
-            ref[:, t * LANES : (t + 1) * LANES] = term
-
-
-def both_groups(velocity, comp, at, far, wphys, synth, derive, other):
+    here, there = spanwise(near, away, width, [derive_ref, other_ref])
+    for t, term in enumerate(here):
+        span_ref[:, t * LANES : (t + 1) * LANES] = term
+    for ref in back_refs:
+        for t in range(0, ref.shape[1], LANES):
+            ref[:, t : t + LANES] = there.pop(0)
+
+
+def both_groups(velocity, comp, at, far, wphys, synth, derive, other, parts):
     width = velocity.shape[2]
     last = far.shape[0] // TILE - 1
+    shapes = [(TILE, width)] + [(TILE, LANES * n) for n in parts]
     return pl.pallas_call(
         both_kernel,
         grid_spec=pltpu.PrefetchScalarGridSpec(
@@ -335,42 +338,43 @@
                 whole(derive.shape),
                 whole(other.shape),
             ],
-            out_specs=[pl.BlockSpec((TILE, width), lambda t, at: (0, 0))] * 2,
+            out_specs=[pl.BlockSpec(shape, lambda t, at: (0, 0)) for shape in shapes],
         ),
-        out_shape=[jax.ShapeDtypeStruct((TILE, width), f32)] * 2,
+        out_shape=[jax.ShapeDtypeStruct(shape, f32) for shape in shapes],
         compiler_params=pltpu.CompilerParams(vmem_limit_bytes=20 << 20),
         name="both_groups",
     )(at, velocity, far, wphys, synth, derive, other)
 
 
-def finish_kernel(at_ref, own_ref, span_ref, damp_ref, inv_ref, held_ref, out_ref, rhs_ref, res_ref):
-    damp = damp_ref[...]
-    for t in range(inv_ref.shape[0]):
-        lanes = slice(t * LANES, (t + 1) * LANES)
-        x = own_ref[0, :, lanes]
-        rhs_ref[t] = x - span_ref[:, lanes] - damp * x
-    element_solve(rhs_ref, res_ref, inv_ref)
-    for t in range(inv_ref.shape[0]):
-        out_ref[0, :, t * LANES : (t + 1) * LANES] = res_ref[t]
-
-
-def finish(velocity, comp, at, span, damp, inv, out, name):
-    width = velocity.shape[2]
-    block = pl.BlockSpec((1, TILE, width), lambda t, at: (comp, at[0], 0))
+def finish_kernel(at_ref, own_ref, span_ref, damp_ref, inv_ref, held_ref, out_ref):
+    right = []
+    for n in range(NODES):
+        rows = pl.ds(n, SUB, stride=NODES)
+        x = own_ref[0, rows, :]
+        right.append(x - span_ref[rows, :] - damp_ref[rows, :] * x)
+    for i in range(NODES):
+        acc = [None, None]
+        for n in range(NODES):
+            term = inv_ref[0, i, n : n + 1, :] * right[n]
+            acc[n % 2] = term if n < 2 else acc[n % 2] + term
+        out_ref[0, pl.ds(i, SUB, stride=NODES), :] = acc[0] + acc[1]
+
+
+def finish(velocity, comp, at, lane, span, damp, inv, out, name):
+    block = pl.BlockSpec((1, TILE, LANES), lambda t, at: (comp, at[0], lane + t))
     return pl.pallas_call(
         finish_kernel,
         grid_spec=pltpu.PrefetchScalarGridSpec(
             num_scalar_prefetch=1,
-            grid=(1,),
+            grid=(span.shape[1] // LANES,),
             in_specs=[
                 block,
-                pl.BlockSpec((TILE, width), lambda t, at: (0, 0)),
+                pl.BlockSpec((TILE, LANES), lambda t, at: (0, t)),
                 pl.BlockSpec((TILE, LANES), lambda t, at: (at[0], 0)),
-                whole(inv.shape),
+                pl.BlockSpec((1, NODES, NODES, LANES), lambda t, at: (lane + t, 0, 0, 0)),
                 pl.BlockSpec(memory_space=pl.ANY),
             ],
             out_specs=block,
-            scratch_shapes=[pltpu.VMEM((width // LANES, TILE, LANES), f32)] * 2,
         ),
         out_shape=jax.ShapeDtypeStruct(velocity.shape, f32),
         input_output_aliases={5: 0},
@@ -426,6 +430,7 @@
     for begin in range(0, stop, TILE):
         far[w - 1, begin, TILE] = exchange(velocity[w - 1, begin : begin + TILE])
 
+    packed_far, far[w, 0, TILE] = lax.optimization_barrier((packed_far, far[w, 0, TILE]))
     steps = points // TILE
     parts = jnp.stack([x[:, :, :steps] for x in [packed] + packed_far])
     order = (mine - lax.iota(jnp.int32, mode_count)) % mode_count
@@ -470,12 +475,15 @@
     for (comp, begin, count), blocks in far.items():
         if shared and back is None and comp != w:
             lent = far[w, TILE, points - TILE][0]
-            span, back = both_groups(velocity, w - 1, here, lent, wphys, synth, derive, group(derive_all, 1 - mine))
-            back = exchange(back)[0]
+            other = group(derive_all, 1 - mine)
+            parts = [width // LANES - 1, 1]
+            span, *back = both_groups(velocity, w - 1, here, lent, wphys, synth, derive, other, parts)
+            back = [exchange(x)[0] for x in back]
+            out = finish(velocity, w - 1, here, 0, span, damp, inv, out, "finish_here")
         out, wphys = advance(velocity, blocks, comp, begin, count, wphys, damp, synth, derive, inv, out)
     if shared:
-        out = finish(velocity, w - 1, here, span, damp, inv, out, "finish_here")
-        out = finish(velocity, w - 1, there, back, damp, inv, out, "finish_there")
+        out = finish(velocity, w - 1, there, 0, back[0], damp, inv, out, "finish_there")
+        out = finish(velocity, w - 1, there, parts[0], back[1], damp, inv, out, "finish_last")
     return (out, viscosity)
 
 

time: 114 us -> 114 us (level)
  local copies, waits for them, and re-layouts: 17 us -> 14.4 us
  waiting for transfers between devices: 14.2 us -> 16.1 us
  Pallas kernels: 47.8 us -> 49 us
    squeeze x1, local copies, waits for them, and re-layouts: 2.73 us -> 1.29 us  [on_device(): far[comp, 0, points] = exchange(velocity[comp])]
    ppermute x4, starting transfers between devices: 11.1 us -> 9.75 us  [sum_over_plane(): lax.ppermute(value, 'plane', [(i, i ^ step) for i in range(count)])]
    pallas_call x2 -> x3, Pallas kernels: 3.38 us -> 4.63 us  [finish(): pl.pallas_call(finish_kernel, grid_spec=pltpu.PrefetchScalarGridSpec(num_...]
    squeeze x1, local copies, waits for them, and re-layouts: 2.13 us -> 0.97 us  [on_device(): far[w - 1, begin, TILE] = exchange(velocity[w - 1, begin:begin + TILE])]
    ppermute x7 -> x8, waiting for transfers between devices: 13.1 us -> 13.7 us  [exchange(): lax.ppermute(block, 'mode', [(i, (i + s) % count) for i in range(count)])]
    ppermute x7 -> x8, starting transfers between devices: 9.05 us -> 9.37 us  [exchange(): lax.ppermute(block, 'mode', [(i, (i + s) % count) for i in range(count)])]
    unnamed x24 -> x28, local copies, waits for them, and re-layouts: 6.41 us -> 6.42 us
  transfers between devices with their start and end apart: 13 -> 14, of which waited for: 5 -> 7; matrix products, arithmetic and copies ran while one was open for 10% -> 8% of each run, Pallas kernels for 41% -> 43%
where the time goes in v4:
time: 114 us; the launch traced here: 113 us
  Pallas kernels  49 us (43%)
  starting transfers between devices  23 us (20%)
  waiting for transfers between devices  16.1 us (14%)
  local copies, waits for them, and re-layouts  14.4 us (13%)
  between operations  7.7 us (7%)
  other arithmetic  2.76 us (2%)
    pallas_call x5, Pallas kernels, advance(): pl.pallas_call(lambda *refs: chunk_kernel(len(far), is_w, len(aliases), *...  35 us
    ppermute x8, waiting for transfers between devices, exchange(): lax.ppermute(block, 'mode', [(i, (i + s) % count) for i in range(count)])  13.7 us
    ppermute x4, starting transfers between devices, sum_over_plane(): lax.ppermute(value, 'plane', [(i, i ^ step) for i in range(count)])  9.75 us
    ppermute x8, starting transfers between devices, exchange(): lax.ppermute(block, 'mode', [(i, (i + s) % count) for i in range(count)])  9.37 us
    unnamed x28, local copies, waits for them, and re-layouts  6.42 us
    pallas_call x3, Pallas kernels, finish(): pl.pallas_call(finish_kernel, grid_spec=pltpu.PrefetchScalarGridSpec(num_...  4.63 us
    pallas_call x1, Pallas kernels, expand(): pl.pallas_call(expand_kernel, out_shape=jax.ShapeDtypeStruct((width // LA...  3.48 us
    pallas_call x1, Pallas kernels, both_groups(): pl.pallas_call(both_kernel, grid_spec=pltpu.PrefetchScalarGridSpec(num_sc...  3.26 us
  transfers between devices with their start and end apart: 14, of which 7 were waited for; matrix products, arithmetic and copies ran while one was open for 8% of the time, Pallas kernels for 43%

profile of v4, /device:TPU:0, one launch (start us, length us, event | category | flops | bytes accessed | tf_op | source)
XLA Modules:
  0.0 113.0 jit_solution(4830824413060140455)
XLA Ops:
  0.6 1.8 %slice_bitcast_fusion.3 = f32[200,512]{1,0:T(8,128)} fusion(f32[3,800,512]{2,1,0:T(8,128)} %own_ref.3), kind=kLoop, calls=%fused_computation.12 | loop fusion | bytes 819200 | tf_op jit(solution)/shard_map/squeeze | solution.py:414
  2.4 3.0 %collective-permute-start.2 = (f32[200,512]{1,0:T(8,128)}, f32[200,512]{1,0:T(8,128)S(1)}, u32[]{:S(2)}, u32[]{:S(2)}) collective-permute-start(f32[200,512]{1,0:T(8,128)} %slice_bitcast_fusion.3), channel_id=1, source_target_pairs={{0,1},{1,0},{2,3},{3,2},{4,5},{5,4},{6,7},{7,6},{8,9},{9,8},{10,11... | collective-permute-start | bytes 1228808 | tf_op jit(solution)/shard_map/ppermute | solution.py:389
  5.4 2.4 %copy-done = f32[3,800,512]{2,1,0:T(8,128)S(1)} copy-done((f32[3,800,512]{2,1,0:T(8,128)S(1)}, f32[3,800,512]{2,1,0:T(8,128)}, u32[]{:S(2)}) %copy-start) | copy-done | bytes 4915224
  7.8 2.7 %first_pass.1 = (f32[2,8,128]{2,1,0:T(8,128)S(1)}, f32[800,512]{1,0:T(8,128)}) custom-call(s32[1]{0:T(128)} %bitcast.at_ref, f32[3,800,512]{2,1,0:T(8,128)S(1)} %copy-done, f32[1,512]{1,0:T(1,128)S(1)} %compare_select_fusion.weight_ref), custom_call_target="tpu_custom_call" | custom-call | tf_op jit(solution)/shard_map/first_pass/pallas_call | solution.py:142
  10.5 0.0 collective-permute-start.1
  10.5 2.0 %collective-permute-start = (f32[800,512]{1,0:T(8,128)}, f32[800,512]{1,0:T(8,128)}, u32[]{:S(2)}, u32[]{:S(2)}) collective-permute-start(f32[800,512]{1,0:T(8,128)} %get-tuple-element.18), channel_id=1, source_target_pairs={{0,1},{1,0},{2,3},{3,2},{4,5},{5,4},{6,7},{7,6},{8,9},{9,8},{10,11... | collective-permute-start | bytes 4915208 | tf_op jit(solution)/shard_map/ppermute | solution.py:389
  12.5 0.0 copy-done.1
  12.5 1.3 %slice_bitcast_fusion = f32[800,512]{1,0:T(8,128)} fusion(f32[3,800,512]{2,1,0:T(8,128)S(1)} %copy-done.1), kind=kLoop, calls=%fused_computation.1 | loop fusion | bytes 3276800 | tf_op jit(solution)/shard_map/squeeze | solution.py:428
  13.8 0.1 collective-permute-start.13
  13.9 1.0 slice_bitcast_fusion.1
  14.8 2.0 %collective-permute-start.12 = (f32[200,512]{1,0:T(8,128)}, f32[200,512]{1,0:T(8,128)S(1)}, u32[]{:S(2)}, u32[]{:S(2)}) collective-permute-start(f32[200,512]{1,0:T(8,128)} %get-tuple-element.28), channel_id=1, source_target_pairs={{0,1},{1,0},{2,3},{3,2},{4,5},{5,4},{6,7},{7,6},{8,9},{9,8},{10,11... | collective-permute-start | bytes 1228808 | tf_op jit(solution)/shard_map/ppermute | solution.py:389
  16.8 0.6 fusion.8
  21.2 0.0 copy-done.9
  21.2 0.1 add_select_fusion
  21.3 0.0 copy-done.8
  21.3 0.2 dynamic-slice_bitcast_fusion.5
  21.5 0.2 maximum_bitcast_fusion
  21.6 1.5 %pad_maximum_fusion.refs_3_.synth_ref.refs_4_ = bf16[2,2,512,512]{3,2,1,0:T(8,128)(2,1)} fusion(bf16[1,2,512,512]{3,2,1,0:T(8,128)(2,1)S(1)} %get-tuple-element.41, bf16[1,2,512,512]{3,2,1,0:T(8,128)(2,1)S(1)} %get-tuple-element.40), kind=kLoop, calls=%fused_computation | loop fusion | flops 1048576 | bytes 4194304 | tf_op jit(solution)/shard_map/stack | solution.py:470
  23.2 2.7 %dynamic-slice_bitcast_fusion = (bf16[2,2,512,256]{3,2,1,0:T(8,128)(2,1)}, bf16[2,2,512,256]{3,2,1,0:T(8,128)(2,1)S(1)}) fusion(bf16[2,2,2,512,256]{4,3,2,1,0:T(8,128)(2,1)} %constant.80.clone, s32[]{:T(128)S(6)} %select_n.47, s32[]{:T(128)S(6)} %select_n.46), kind=kLoop, calls=%fused_computation.4 | loop fusion | bytes 4194312 | tf_op jit(solution)/shard_map/jit(dynamic_index_in_dim)/squeeze | solution.py:467
  26.0 3.5 %expand.1.refs_5_.inv_ref.refs_6_ = f32[4,25,25,128]{3,2,1,0:T(8,128)S(1)} custom-call(f32[25,25,256]{2,1,0:T(8,128)S(1)} %bitcast.31, bf16[256,512]{1,0:T(8,128)(2,1)S(1)} %copy-done.7), custom_call_target="tpu_custom_call" | custom-call | tf_op jit(solution)/shard_map/expand/pallas_call | solution.py:177
  29.4 0.0 collective-permute-done.1
  29.4 0.0 collective-permute-done.2.refs_1_
  29.5 0.6 slice_reduce_fusion
  30.1 0.0 collective-permute-start.3
  30.1 0.1 copy.21
  30.2 0.1 reshape.101
  30.2 2.4 %collective-permute-start.7 = (f32[32]{0:T(128)S(1)}, f32[32]{0:T(128)S(1)}, u32[]{:S(2)}, u32[]{:S(2)}) collective-permute-start(f32[32]{0:T(128)S(1)} %multiply_multiply_fusion), channel_id=1, source_target_pairs={{0,2},{2,4},{4,6},{6,8},{8,10},{10,12},{12,14},{14,16},{16,18},{18... | collective-permute-start | bytes 392 | tf_op jit(solution)/shard_map/ppermute | solution.py:449
  32.7 0.0 collective-permute-done.3
  33.9 2.9 %collective-permute-start.4 = (f32[]{:T(128)}, f32[]{:T(128)}, u32[]{:S(2)}, u32[]{:S(2)}) collective-permute-start(f32[]{:T(128)} %add.91), channel_id=1, source_target_pairs={{0,4},{2,6},{4,0},{6,2},{8,12},{10,14},{12,8},{14,10},{16,20},{18,... | collective-permute-start | bytes 20 | tf_op jit(solution)/shard_map/ppermute | solution.py:400
  36.8 0.7 collective-permute-done.4
  38.1 2.9 %collective-permute-start.5 = (f32[]{:T(128)}, f32[]{:T(128)}, u32[]{:S(2)}, u32[]{:S(2)}) collective-permute-start(f32[]{:T(128)} %add.92), channel_id=1, source_target_pairs={{0,8},{2,10},{4,12},{6,14},{8,0},{10,2},{12,4},{14,6},{16,24},{18,... | collective-permute-start | bytes 20 | tf_op jit(solution)/shard_map/ppermute | solution.py:400
  41.0 0.6 collective-permute-done.5
  42.3 4.0 %collective-permute-start.6 = (f32[]{:T(128)}, f32[]{:T(128)}, u32[]{:S(2)}, u32[]{:S(2)}) collective-permute-start(f32[]{:T(128)} %add.93), channel_id=1, source_target_pairs={{0,16},{2,18},{4,20},{6,22},{8,24},{10,26},{12,28},{14,30},{16,0},... | collective-permute-start | bytes 20 | tf_op jit(solution)/shard_map/ppermute | solution.py:400
  46.2 0.5 collective-permute-done.6
  46.7 1.5 %collective-permute-start.8 = (f32[32]{0:T(128)S(1)}, f32[32]{0:T(128)S(1)}, u32[]{:S(2)}, u32[]{:S(2)}) collective-permute-start(f32[32]{0:T(128)S(1)} %multiply_multiply_fusion), channel_id=1, source_target_pairs={{2,0},{4,2},{6,4},{8,6},{10,8},{12,10},{14,12},{16,14},{18,16},{20... | collective-permute-start | bytes 392 | tf_op jit(solution)/shard_map/ppermute | solution.py:450
  48.8 0.0 collective-permute-done.7
  48.9 0.3 collective-permute-start.11
  49.1 0.6 collective-permute-done.8
  49.7 0.1 maximum_multiply_fusion
  49.8 0.2 select_reduce_fusion
  50.0 0.0 copy-start.10
  50.0 0.1 broadcast_multiply_fusion
  50.1 0.1 mul.94
  50.2 0.2 broadcast_in_dim.45.refs_2_.damp_ref.refs_3_
  50.4 0.0 copy-start.2
  50.4 2.4 %copy-done.2 = f32[3,800,512]{2,1,0:T(8,128)S(1)} copy-done((f32[3,800,512]{2,1,0:T(8,128)S(1)}, f32[3,800,512]{2,1,0:T(8,128)}, u32[]{:S(2)}) %copy-start.2) | copy-done | bytes 4915224
  52.8 1.6 %copy-done.3 = bf16[2,2,512,512]{3,2,1,0:T(8,128)(2,1)S(1)} copy-done((bf16[2,2,512,512]{3,2,1,0:T(8,128)(2,1)S(1)}, bf16[2,2,512,512]{3,2,1,0:T(8,128)(2,1)}, u32[]{:S(2)}) %copy-start.3) | copy-done | bytes 2097176
  54.4 3.6 %advance_2_0.1 = (f32[3,800,512]{2,1,0:T(8,128)}, f32[800,1024]{1,0:T(8,128)S(1)}) custom-call(f32[3,800,512]{2,1,0:T(8,128)S(1)} %copy-done.2, f32[200,512]{1,0:T(8,128)S(1)} %collective-permute-done.2.refs_1_, f32[800,128]{1,0:T(8,128)S(1)} %broadcast_in_dim.45.refs_2_.damp_ref.refs_3_, bf16[2,2,512,512]{3,2,1,0:T(8,128)(2,1)S(1)} %copy-done.3, ...), custom_call_target="tpu_custom_call" | custom-call | flops 943718400 | bytes 819200 | tf_op jit(solution)/shard_map/advance_2_0/pallas_call | solution.py:293
  57.9 0.0 collective-permute-done.refs_1_.far_ref
  58.0 10.3 %advance_2_200.1 = (f32[3,800,512]{2,1,0:T(8,128)}, f32[800,1024]{1,0:T(8,128)S(1)}) custom-call(f32[3,800,512]{2,1,0:T(8,128)S(1)} %copy-done.2, f32[800,512]{1,0:T(8,128)} %collective-permute-done.refs_1_.far_ref, f32[800,128]{1,0:T(8,128)S(1)} %broadcast_in_dim.45.refs_2_.damp_ref.refs_3_, ...), custom_call_target="tpu_custom_call", output_to_operand_aliasing={{0}: (6, {}), {1}: (7, {})} | custom-call | flops 2831155200 | bytes 2457600 | tf_op jit(solution)/shard_map/advance_2_200/pallas_call | solution.py:293
  68.3 3.3 %both_groups.1 = (f32[200,512]{1,0:T(8,128)S(1)}, f32[200,384]{1,0:T(8,128)S(1)}, f32[200,128]{1,0:T(8,128)S(1)}) custom-call(s32[1]{0:T(128)} %bitcast.2.at_ref, f32[3,800,512]{2,1,0:T(8,128)S(1)} %copy-done.2, f32[800,512]{1,0:T(8,128)} %collective-permute-done.refs_1_.far_ref, f32[800,1024]{1,0:T(8,128)S(1)} %get-tuple-element.23.wphys_ref.refs_2_, ...), custom_call_target="tpu_custom_call" | custom-call | tf_op jit(solution)/shard_map/both_groups/pallas_call | solution.py:328
  71.6 1.3 %collective-permute-start.10 = (f32[200,384]{1,0:T(8,128)S(1)}, f32[200,384]{1,0:T(8,128)S(1)}, u32[]{:S(2)}, u32[]{:S(2)}) collective-permute-start(f32[200,384]{1,0:T(8,128)S(1)} %get-tuple-element.25), channel_id=1, source_target_pairs={{0,1},{1,0},{2,3},{3,2},{4,5},{5,4},{6,7},{7,6},{8,9},{9,8},{10,11... | collective-permute-start | bytes 921608 | tf_op jit(solution)/shard_map/ppermute | solution.py:389
  72.8 0.8 collective-permute-start.9
  73.6 2.0 %finish_here.1.refs_7_ = f32[3,800,512]{2,1,0:T(8,128)} custom-call(s32[1]{0:T(128)} %bitcast.2.at_ref, f32[3,800,512]{2,1,0:T(8,128)S(1)} %copy-done.2, f32[200,512]{1,0:T(8,128)S(1)} %get-tuple-element.26.span_ref, f32[800,128]{1,0:T(8,128)S(1)} %broadcast_in_dim.45.refs_2_.damp_ref.refs_3_, ...), custom_call_target="tpu_custom_call", output_to_operand_aliasing={{}: (5, {})} | custom-call | tf_op jit(solution)/shard_map/finish_here/pallas_call | solution.py:365
  75.7 10.7 %collective-permute-done.13.refs_1_ = f32[800,512]{1,0:T(8,128)} collective-permute-done((f32[800,512]{1,0:T(8,128)}, f32[800,512]{1,0:T(8,128)}, u32[]{:S(2)}, u32[]{:S(2)}) %collective-permute-start.13) | collective-permute-done | bytes 1638432 | tf_op jit(solution)/shard_map/ppermute | solution.py:389
  86.4 13.0 %advance_0_0.1.refs_7_ = f32[3,800,512]{2,1,0:T(8,128)} custom-call(f32[3,800,512]{2,1,0:T(8,128)S(1)} %copy-done.2, f32[800,512]{1,0:T(8,128)} %collective-permute-done.13.refs_1_, f32[800,1024]{1,0:T(8,128)S(1)} %get-tuple-element.23.wphys_ref.refs_2_, f32[800,128]{1,0:T(8,128)S(1)} %broadcast_in_dim.45.refs_2_.damp_ref.refs_3_, ...), custom_call_target="tpu_custom_call", output_to_operand_aliasing={{}: (7, {})} | custom-call | flops 3774873600 | bytes 3276800 | tf_op jit(solution)/shard_map/advance_0_0/pallas_call | solution.py:293
  99.4 0.0 collective-permute-done.12.refs_1_
  99.4 3.5 %advance_1_0.1.refs_7_ = f32[3,800,512]{2,1,0:T(8,128)} custom-call(f32[3,800,512]{2,1,0:T(8,128)S(1)} %copy-done.2, f32[200,512]{1,0:T(8,128)S(1)} %collective-permute-done.12.refs_1_, f32[800,1024]{1,0:T(8,128)S(1)} %get-tuple-element.23.wphys_ref.refs_2_, ...), custom_call_target="tpu_custom_call", output_to_operand_aliasing={{}: (7, {})} | custom-call | flops 943718400 | bytes 819200 | tf_op jit(solution)/shard_map/advance_1_0/pallas_call | solution.py:293
  102.9 1.0 collective-permute-done.11.refs_1_
  103.9 4.5 %advance_1_200.1.held_ref = f32[3,800,512]{2,1,0:T(8,128)} custom-call(f32[3,800,512]{2,1,0:T(8,128)S(1)} %copy-done.2, f32[200,512]{1,0:T(8,128)} %collective-permute-done.11.refs_1_, f32[800,1024]{1,0:T(8,128)S(1)} %get-tuple-element.23.wphys_ref.refs_2_, f32[800,128]{1,0:T(8,128)S(1)} %broadcast_in_dim.45.refs_2_.damp_ref.refs_3_, ...), custom_call_target="tpu_custom_call", output_to_operand_aliasing={{}: (7, {})} | custom-call | flops 943718400 | bytes 819200 | tf_op jit(solution)/shard_map/advance_1_200/pallas_call | solution.py:293
  108.5 1.9 %collective-permute-done.10.span_ref = f32[200,384]{1,0:T(8,128)S(1)} collective-permute-done((f32[200,384]{1,0:T(8,128)S(1)}, f32[200,384]{1,0:T(8,128)S(1)}, u32[]{:S(2)}, u32[]{:S(2)}) %collective-permute-start.10) | collective-permute-done | bytes 307232 | tf_op jit(solution)/shard_map/ppermute | solution.py:389
  110.4 1.8 %finish_there.1.held_ref = f32[3,800,512]{2,1,0:T(8,128)} custom-call(s32[1]{0:T(128)} %bitcast.at_ref, f32[3,800,512]{2,1,0:T(8,128)S(1)} %copy-done.2, f32[200,384]{1,0:T(8,128)S(1)} %collective-permute-done.10.span_ref, f32[800,128]{1,0:T(8,128)S(1)} %broadcast_in_dim.45.refs_2_.damp_ref.refs_3_, ...), custom_call_target="tpu_custom_call", output_to_operand_aliasing={{}: (5, {})} | custom-call | tf_op jit(solution)/shard_map/finish_there/pallas_call | solution.py:365
  112.2 0.0 collective-permute-done.9.span_ref
  112.2 0.9 finish_last.1
  (26 shorter events, 0.1 us)
Async XLA Ops:
  2.4 27.0 %collective-permute-start.2 = (f32[200,512]{1,0:T(8,128)}, f32[200,512]{1,0:T(8,128)S(1)}, u32[]{:S(2)}, u32[]{:S(2)}) collective-permute-start(f32[200,512]{1,0:T(8,128)} %slice_bitcast_fusion.3), channel_id=1, source_target_pairs={{0,1},{1,0},{2,3},{3,2},{4,5},{5,4},{6,7},{7,6},{8,9},{9,8},{10,11... | collective-permute-start | bytes 1228808 | tf_op jit(solution)/shard_map/ppermute | solution.py:389
  5.4 2.4 %copy-start = (f32[3,800,512]{2,1,0:T(8,128)S(1)}, f32[3,800,512]{2,1,0:T(8,128)}, u32[]{:S(2)}) copy-start(f32[3,800,512]{2,1,0:T(8,128)} %own_ref.3) | copy-start | bytes 14745604
  7.8 4.7 %copy-start.1 = (f32[3,800,512]{2,1,0:T(8,128)S(1)}, f32[3,800,512]{2,1,0:T(8,128)}, u32[]{:S(2)}) copy-start(f32[3,800,512]{2,1,0:T(8,128)} %own_ref.3) | copy-start | bytes 14745604
  10.5 19.0 %collective-permute-start.1 = (f32[2,8,128]{2,1,0:T(8,128)S(1)}, f32[2,8,128]{2,1,0:T(8,128)S(1)}, u32[]{:S(2)}, u32[]{:S(2)}) collective-permute-start(f32[2,8,128]{2,1,0:T(8,128)S(1)} %get-tuple-element.16), channel_id=1, source_target_pairs={{0,1},{1,0},{2,3},{3,2},{4,5},{5,4},{6,7},{7,6},{8,9},{9,8},{10,11... | collective-permute-start | bytes 24584 | tf_op jit(solution)/shard_map/ppermute | solution.py:389
  10.5 10.7 %copy-start.9 = (s32[32,4]{0,1:T(4,128)S(1)}, s32[32,4]{0,1:T(4,128)}, u32[]{:S(2)}) copy-start(s32[32,4]{0,1:T(4,128)} %param.11) | copy-start | bytes 1540
  10.5 10.7 %copy-start.12 = (s32[4]{0:T(128)S(1)}, s32[4]{0:T(128)}, u32[]{:S(2)}) copy-start(s32[4]{0:T(128)} %constant.77.clone) | copy-start | bytes 52
  10.5 10.8 %copy-start.8 = (bf16[2,2,2,256,512]{4,3,2,1,0:T(8,128)(2,1)S(1)}, bf16[2,2,2,256,512]{4,3,2,1,0:T(8,128)(2,1)}, u32[]{:S(2)}) copy-start(bf16[2,2,2,256,512]{4,3,2,1,0:T(8,128)(2,1)} %constant.79.clone) | copy-start | bytes 6291460
  10.5 47.4 %collective-permute-start = (f32[800,512]{1,0:T(8,128)}, f32[800,512]{1,0:T(8,128)}, u32[]{:S(2)}, u32[]{:S(2)}) collective-permute-start(f32[800,512]{1,0:T(8,128)} %get-tuple-element.18), channel_id=1, source_target_pairs={{0,1},{1,0},{2,3},{3,2},{4,5},{5,4},{6,7},{7,6},{8,9},{9,8},{10,11... | collective-permute-start | bytes 4915208 | tf_op jit(solution)/shard_map/ppermute | solution.py:389
  13.8 72.6 %collective-permute-start.13 = (f32[800,512]{1,0:T(8,128)}, f32[800,512]{1,0:T(8,128)}, u32[]{:S(2)}, u32[]{:S(2)}) collective-permute-start(f32[800,512]{1,0:T(8,128)} %slice_bitcast_fusion), channel_id=1, source_target_pairs={{0,1},{1,0},{2,3},{3,2},{4,5},{5,4},{6,7},{7,6},{8,9},{9,8},{10,11... | collective-permute-start | bytes 4915208 | tf_op jit(solution)/shard_map/ppermute | solution.py:389
  14.8 84.5 %collective-permute-start.12 = (f32[200,512]{1,0:T(8,128)}, f32[200,512]{1,0:T(8,128)S(1)}, u32[]{:S(2)}, u32[]{:S(2)}) collective-permute-start(f32[200,512]{1,0:T(8,128)} %get-tuple-element.28), channel_id=1, source_target_pairs={{0,1},{1,0},{2,3},{3,2},{4,5},{5,4},{6,7},{7,6},{8,9},{9,8},{10,11... | collective-permute-start | bytes 1228808 | tf_op jit(solution)/shard_map/ppermute | solution.py:389
  23.2 2.8 %copy-start.6 = (f32[256,25,25]{0,2,1:T(8,128)S(1)}, f32[256,25,25]{0,2,1:T(8,128)}, u32[]{:S(2)}) copy-start(f32[256,25,25]{0,2,1:T(8,128)} %param.10) | copy-start | bytes 1920004
  23.2 2.8 %copy-start.7 = (bf16[256,512]{1,0:T(8,128)(2,1)S(1)}, bf16[256,512]{1,0:T(8,128)(2,1)}, u32[]{:S(2)}) copy-start(bf16[256,512]{1,0:T(8,128)(2,1)} %constant.81.clone.spread_ref) | copy-start | bytes 786436
  25.9 4.3 %copy-start.13 = (s32[32]{0:T(128)S(1)}, s32[32]{0:T(128)}, u32[]{:S(2)}) copy-start(s32[32]{0:T(128)} %param.12) | copy-start | bytes 388
  25.9 24.1 %copy-start.11 = (f32[25]{0:T(128)S(1)}, f32[25]{0:T(128)}, u32[]{:S(2)}) copy-start(f32[25]{0:T(128)} %constant.82) | copy-start | bytes 304
  30.1 2.6 %collective-permute-start.3 = (f32[]{:T(128)}, f32[]{:T(128)}, u32[]{:S(2)}, u32[]{:S(2)}) collective-permute-start(f32[]{:T(128)} %get-tuple-element.36), channel_id=1, source_target_pairs={{0,2},{2,0},{4,6},{6,4},{8,10},{10,8},{12,14},{14,12},{16,18},{18,... | collective-permute-start | bytes 20 | tf_op jit(solution)/shard_map/ppermute | solution.py:400
  30.2 18.6 %collective-permute-start.7 = (f32[32]{0:T(128)S(1)}, f32[32]{0:T(128)S(1)}, u32[]{:S(2)}, u32[]{:S(2)}) collective-permute-start(f32[32]{0:T(128)S(1)} %multiply_multiply_fusion), channel_id=1, source_target_pairs={{0,2},{2,4},{4,6},{6,8},{8,10},{10,12},{12,14},{14,16},{16,18},{18... | collective-permute-start | bytes 392 | tf_op jit(solution)/shard_map/ppermute | solution.py:449
  33.9 3.6 %collective-permute-start.4 = (f32[]{:T(128)}, f32[]{:T(128)}, u32[]{:S(2)}, u32[]{:S(2)}) collective-permute-start(f32[]{:T(128)} %add.91), channel_id=1, source_target_pairs={{0,4},{2,6},{4,0},{6,2},{8,12},{10,14},{12,8},{14,10},{16,20},{18,... | collective-permute-start | bytes 20 | tf_op jit(solution)/shard_map/ppermute | solution.py:400
  38.1 3.6 %collective-permute-start.5 = (f32[]{:T(128)}, f32[]{:T(128)}, u32[]{:S(2)}, u32[]{:S(2)}) collective-permute-start(f32[]{:T(128)} %add.92), channel_id=1, source_target_pairs={{0,8},{2,10},{4,12},{6,14},{8,0},{10,2},{12,4},{14,6},{16,24},{18,... | collective-permute-start | bytes 20 | tf_op jit(solution)/shard_map/ppermute | solution.py:400
  42.3 4.5 %collective-permute-start.6 = (f32[]{:T(128)}, f32[]{:T(128)}, u32[]{:S(2)}, u32[]{:S(2)}) collective-permute-start(f32[]{:T(128)} %add.93), channel_id=1, source_target_pairs={{0,16},{2,18},{4,20},{6,22},{8,24},{10,26},{12,28},{14,30},{16,0},... | collective-permute-start | bytes 20 | tf_op jit(solution)/shard_map/ppermute | solution.py:400
  46.7 3.0 %collective-permute-start.8 = (f32[32]{0:T(128)S(1)}, f32[32]{0:T(128)S(1)}, u32[]{:S(2)}, u32[]{:S(2)}) collective-permute-start(f32[32]{0:T(128)S(1)} %multiply_multiply_fusion), channel_id=1, source_target_pairs={{2,0},{4,2},{6,4},{8,6},{10,8},{12,10},{14,12},{16,14},{18,16},{20... | collective-permute-start | bytes 392 | tf_op jit(solution)/shard_map/ppermute | solution.py:450
  48.9 55.1 %collective-permute-start.11 = (f32[200,512]{1,0:T(8,128)}, f32[200,512]{1,0:T(8,128)}, u32[]{:S(2)}, u32[]{:S(2)}) collective-permute-start(f32[200,512]{1,0:T(8,128)} %get-tuple-element.29), channel_id=1, source_target_pairs={{0,1},{1,0},{2,3},{3,2},{4,5},{5,4},{6,7},{7,6},{8,9},{9,8},{10,11... | collective-permute-start | bytes 1228808 | tf_op jit(solution)/shard_map/ppermute | solution.py:389
  50.0 7.9 %copy-start.10 = (f32[32]{0:T(128)}, f32[32]{0:T(128)S(1)}, u32[]{:S(2)}) copy-start(f32[32]{0:T(128)S(1)} %add_multiply_fusion.1) | copy-start | bytes 388
  50.4 2.4 %copy-start.2 = (f32[3,800,512]{2,1,0:T(8,128)S(1)}, f32[3,800,512]{2,1,0:T(8,128)}, u32[]{:S(2)}) copy-start(f32[3,800,512]{2,1,0:T(8,128)} %own_ref.3) | copy-start | bytes 14745604
  52.8 1.6 %copy-start.3 = (bf16[2,2,512,512]{3,2,1,0:T(8,128)(2,1)S(1)}, bf16[2,2,512,512]{3,2,1,0:T(8,128)(2,1)}, u32[]{:S(2)}) copy-start(bf16[2,2,512,512]{3,2,1,0:T(8,128)(2,1)} %pad_maximum_fusion.refs_3_.synth_ref.refs_4_) | copy-start | bytes 6291460
  54.4 3.6 %copy-start.4 = (bf16[2,2,512,512]{3,2,1,0:T(8,128)(2,1)S(1)}, bf16[2,2,512,512]{3,2,1,0:T(8,128)(2,1)}, u32[]{:S(2)}) copy-start(bf16[2,2,512,512]{3,2,1,0:T(8,128)(2,1)} %pad_maximum_fusion.refs_3_.synth_ref.refs_4_) | copy-start | bytes 6291460
  58.0 10.3 %copy-start.5 = (bf16[2,2,512,256]{3,2,1,0:T(8,128)(2,1)S(1)}, bf16[2,2,512,256]{3,2,1,0:T(8,128)(2,1)}, u32[]{:S(2)}) copy-start(bf16[2,2,512,256]{3,2,1,0:T(8,128)(2,1)} %get-tuple-element.30.other_ref) | copy-start | bytes 3145732
  71.6 38.9 %collective-permute-start.10 = (f32[200,384]{1,0:T(8,128)S(1)}, f32[200,384]{1,0:T(8,128)S(1)}, u32[]{:S(2)}, u32[]{:S(2)}) collective-permute-start(f32[200,384]{1,0:T(8,128)S(1)} %get-tuple-element.25), channel_id=1, source_target_pairs={{0,1},{1,0},{2,3},{3,2},{4,5},{5,4},{6,7},{7,6},{8,9},{9,8},{10,11... | collective-permute-start | bytes 921608 | tf_op jit(solution)/shard_map/ppermute | solution.py:389
  72.8 39.3 %collective-permute-start.9 = (f32[200,128]{1,0:T(8,128)S(1)}, f32[200,128]{1,0:T(8,128)S(1)}, u32[]{:S(2)}, u32[]{:S(2)}) collective-permute-start(f32[200,128]{1,0:T(8,128)S(1)} %get-tuple-element.24), channel_id=1, source_target_pairs={{0,1},{1,0},{2,3},{3,2},{4,5},{5,4},{6,7},{7,6},{8,9},{9,8},{10,11... | collective-permute-start | bytes 307208 | tf_op jit(solution)/shard_map/ppermute | solution.py:389

commit v5 on v4

--- a/solution.py
+++ b/solution.py
@@ -15,6 +15,7 @@
 LANES = 128
 SUB = 8
 TILE = SUB * NODES
+HEAD = 80
 
 f32 = jnp.float32
 bf16 = jnp.bfloat16
@@ -411,9 +412,12 @@
     elements = neighbours.shape[0]
     w = comps - 1
 
-    first = velocity[w, :TILE]
-    far = {(w, 0, TILE): exchange(first)}
-    held, velocity = lax.optimization_barrier((first, velocity))
+    pieces = []
+    for begin, end in ((0, HEAD), (HEAD, TILE)):
+        first = velocity[w, begin:end]
+        pieces.append(exchange(first))
+        held, velocity = lax.optimization_barrier((first, velocity))
+    far = {(w, 0, TILE): [jnp.concatenate(x) for x in zip(*pieces)]}
     index = mine * width + lax.iota(jnp.int32, width)
     weight = jnp.where(index < 2, 1.0, 2.0).astype(f32)[None, :]
     blocks = points // TILE
@@ -476,14 +480,16 @@
         if shared and back is None and comp != w:
             lent = far[w, TILE, points - TILE][0]
             other = group(derive_all, 1 - mine)
-            parts = [width // LANES - 1, 1]
+            parts = [width // LANES - 2, 1, 1] if width > 2 * LANES else [1, 1]
             span, *back = both_groups(velocity, w - 1, here, lent, wphys, synth, derive, other, parts)
             back = [exchange(x)[0] for x in back]
             out = finish(velocity, w - 1, here, 0, span, damp, inv, out, "finish_here")
         out, wphys = advance(velocity, blocks, comp, begin, count, wphys, damp, synth, derive, inv, out)
     if shared:
-        out = finish(velocity, w - 1, there, 0, back[0], damp, inv, out, "finish_there")
-        out = finish(velocity, w - 1, there, parts[0], back[1], damp, inv, out, "finish_last")
+        lane = 0
+        for term, count in zip(back, parts):
+            out = finish(velocity, w - 1, there, lane, term, damp, inv, out, f"finish_there_{lane}")
+            lane += count
     return (out, viscosity)
 
 

time: 114 us -> 112 us (0.982)
  waiting for transfers between devices: 16.1 us -> 7.17 us
  starting transfers between devices: 23 us -> 26.5 us
  local copies, waits for them, and re-layouts: 14.4 us -> 17.3 us
    ppermute x8 -> x10, waiting for transfers between devices: 13.7 us -> 6.09 us  [exchange(): lax.ppermute(block, 'mode', [(i, (i + s) % count) for i in range(count)])]
    ppermute x8 -> x10, starting transfers between devices: 9.37 us -> 11.6 us  [exchange(): lax.ppermute(block, 'mode', [(i, (i + s) % count) for i in range(count)])]
    squeeze x1, local copies, waits for them, and re-layouts: 1.29 us -> 2.88 us  [on_device(): far[comp, 0, points] = exchange(velocity[comp])]
    ppermute x4, starting transfers between devices: 9.75 us -> 11.1 us  [sum_over_plane(): lax.ppermute(value, 'plane', [(i, i ^ step) for i in range(count)])]
    squeeze x1, local copies, waits for them, and re-layouts: 0.97 us -> 2.15 us  [on_device(): far[w - 1, begin, TILE] = exchange(velocity[w - 1, begin:begin + TILE])]
    pallas_call x3 -> x4, Pallas kernels: 4.63 us -> 4.87 us  [finish(): pl.pallas_call(finish_kernel, grid_spec=pltpu.PrefetchScalarGridSpec(num_...]
    unnamed x28 -> x24, local copies, waits for them, and re-layouts: 6.42 us -> 6.41 us
  transfers between devices with their start and end apart: 14 -> 16, of which waited for: 7 -> 6; matrix products, arithmetic and copies ran while one was open for 8% -> 12% of each run, Pallas kernels for 43% -> 43%
where the time goes in v5:
time: 112 us
  Pallas kernels  49.2 us (44%)
  starting transfers between devices  26.5 us (24%)
  local copies, waits for them, and re-layouts  17.3 us (15%)
  between operations  7.95 us (7%)
  waiting for transfers between devices  7.17 us (6%)
  other arithmetic  3.78 us (3%)
    pallas_call x5, Pallas kernels, advance(): pl.pallas_call(lambda *refs: chunk_kernel(len(far), is_w, len(aliases), *...  35 us
    ppermute x10, starting transfers between devices, exchange(): lax.ppermute(block, 'mode', [(i, (i + s) % count) for i in range(count)])  11.6 us
    ppermute x4, starting transfers between devices, sum_over_plane(): lax.ppermute(value, 'plane', [(i, i ^ step) for i in range(count)])  11.1 us
    unnamed x24, local copies, waits for them, and re-layouts  6.41 us
    ppermute x10, waiting for transfers between devices, exchange(): lax.ppermute(block, 'mode', [(i, (i + s) % count) for i in range(count)])  6.09 us
    pallas_call x4, Pallas kernels, finish(): pl.pallas_call(finish_kernel, grid_spec=pltpu.PrefetchScalarGridSpec(num_...  4.87 us
    pallas_call x1, Pallas kernels, expand(): pl.pallas_call(expand_kernel, out_shape=jax.ShapeDtypeStruct((width // LA...  3.48 us
    pallas_call x1, Pallas kernels, both_groups(): pl.pallas_call(both_kernel, grid_spec=pltpu.PrefetchScalarGridSpec(num_sc...  3.28 us
  transfers between devices with their start and end apart: 16, of which 6 were waited for; matrix products, arithmetic and copies ran while one was open for 12% of the time, Pallas kernels for 43%

profile of v5, /device:TPU:0, one launch (start us, length us, event | category | flops | bytes accessed | tf_op | source)
XLA Modules:
  0.0 111.9 jit_solution(15567408796157763759)
XLA Ops:
  0.6 0.9 slice_bitcast_fusion.4
  1.6 3.0 %collective-permute-start.2 = (f32[80,512]{1,0:T(8,128)S(1)}, f32[80,512]{1,0:T(8,128)}, u32[]{:S(2)}, u32[]{:S(2)}) collective-permute-start(f32[80,512]{1,0:T(8,128)S(1)} %slice_bitcast_fusion.4), channel_id=1, source_target_pairs={{0,1},{1,0},{2,3},{3,2},{4,5},{5,4},{6,7},{7,6},{8,9},{9,8},{10,11... | collective-permute-start | bytes 491528 | tf_op jit(solution)/shard_map/ppermute | solution.py:390
  4.6 1.0 slice_bitcast_fusion.3
  5.6 0.1 collective-permute-start.3
  5.7 0.0 copy-start
  5.7 2.4 %copy-done = f32[3,800,512]{2,1,0:T(8,128)S(1)} copy-done((f32[3,800,512]{2,1,0:T(8,128)S(1)}, f32[3,800,512]{2,1,0:T(8,128)}, u32[]{:S(2)}) %copy-start) | copy-done | bytes 4915224
  8.1 2.6 %first_pass.1 = (f32[2,8,128]{2,1,0:T(8,128)S(1)}, f32[800,512]{1,0:T(8,128)}) custom-call(s32[1]{0:T(128)} %bitcast.at_ref, f32[3,800,512]{2,1,0:T(8,128)S(1)} %copy-done, f32[1,512]{1,0:T(1,128)S(1)} %compare_select_fusion.weight_ref), custom_call_target="tpu_custom_call" | custom-call | tf_op jit(solution)/shard_map/first_pass/pallas_call | solution.py:143
  10.7 2.0 %collective-permute-start.1 = (f32[2,8,128]{2,1,0:T(8,128)S(1)}, f32[2,8,128]{2,1,0:T(8,128)S(1)}, u32[]{:S(2)}, u32[]{:S(2)}) collective-permute-start(f32[2,8,128]{2,1,0:T(8,128)S(1)} %get-tuple-element.19), channel_id=1, source_target_pairs={{0,1},{1,0},{2,3},{3,2},{4,5},{5,4},{6,7},{7,6},{8,9},{9,8},{10,11... | collective-permute-start | bytes 24584 | tf_op jit(solution)/shard_map/ppermute | solution.py:390
  12.7 0.1 collective-permute-start
  12.8 2.9 %slice_bitcast_fusion = f32[800,512]{1,0:T(8,128)} fusion(f32[3,800,512]{2,1,0:T(8,128)} %own_ref.4), kind=kLoop, calls=%fused_computation.1 | loop fusion | bytes 3276800 | tf_op jit(solution)/shard_map/squeeze | solution.py:432
  15.7 1.8 %collective-permute-start.15 = (f32[800,512]{1,0:T(8,128)}, f32[800,512]{1,0:T(8,128)}, u32[]{:S(2)}, u32[]{:S(2)}) collective-permute-start(f32[800,512]{1,0:T(8,128)} %slice_bitcast_fusion), channel_id=1, source_target_pairs={{0,1},{1,0},{2,3},{3,2},{4,5},{5,4},{6,7},{7,6},{8,9},{9,8},{10,11... | collective-permute-start | bytes 4915208 | tf_op jit(solution)/shard_map/ppermute | solution.py:390
  17.5 0.6 fusion.8
  20.7 2.1 %slice_bitcast_fusion.1 = (f32[200,512]{1,0:T(8,128)}, f32[200,512]{1,0:T(8,128)}) fusion(f32[3,800,512]{2,1,0:T(8,128)} %own_ref.4), kind=kLoop, calls=%fused_computation.11 | loop fusion | bytes 1638400 | tf_op jit(solution)/shard_map/squeeze | solution.py:435
  24.1 0.1 add_select_fusion
  24.2 0.2 dynamic-slice_bitcast_fusion.5
  24.4 0.2 maximum_bitcast_fusion
  24.6 1.5 %pad_maximum_fusion.refs_3_.synth_ref.refs_4_ = bf16[2,2,512,512]{3,2,1,0:T(8,128)(2,1)} fusion(bf16[1,2,512,512]{3,2,1,0:T(8,128)(2,1)S(1)} %get-tuple-element.45, bf16[1,2,512,512]{3,2,1,0:T(8,128)(2,1)S(1)} %get-tuple-element.44), kind=kLoop, calls=%fused_computation | loop fusion | flops 1048576 | bytes 4194304 | tf_op jit(solution)/shard_map/stack | solution.py:474
  26.1 2.7 %dynamic-slice_bitcast_fusion = (bf16[2,2,512,256]{3,2,1,0:T(8,128)(2,1)}, bf16[2,2,512,256]{3,2,1,0:T(8,128)(2,1)S(1)}) fusion(bf16[2,2,2,512,256]{4,3,2,1,0:T(8,128)(2,1)} %constant.80.clone, s32[]{:T(128)S(6)} %select_n.47, s32[]{:T(128)S(6)} %select_n.46), kind=kLoop, calls=%fused_computation.4 | loop fusion | bytes 4194312 | tf_op jit(solution)/shard_map/jit(dynamic_index_in_dim)/squeeze | solution.py:471
  28.8 3.5 %expand.1.refs_5_.inv_ref.refs_6_ = f32[4,25,25,128]{3,2,1,0:T(8,128)S(1)} custom-call(f32[25,25,256]{2,1,0:T(8,128)S(1)} %bitcast.33, bf16[256,512]{1,0:T(8,128)(2,1)S(1)} %copy-done.5), custom_call_target="tpu_custom_call" | custom-call | tf_op jit(solution)/shard_map/expand/pallas_call | solution.py:178
  32.3 0.2 collective-permute-start.14
  32.6 1.1 pad_maximum_fusion.1.refs_1_
  33.7 0.6 slice_reduce_fusion
  34.3 0.0 collective-permute-start.4
  34.3 0.1 copy.22
  34.3 0.1 reshape.101
  34.4 2.4 %collective-permute-start.8 = (f32[32]{0:T(128)S(1)}, f32[32]{0:T(128)S(1)}, u32[]{:S(2)}, u32[]{:S(2)}) collective-permute-start(f32[32]{0:T(128)S(1)} %multiply_multiply_fusion), channel_id=1, source_target_pairs={{0,2},{2,4},{4,6},{6,8},{8,10},{10,12},{12,14},{14,16},{16,18},{18... | collective-permute-start | bytes 392 | tf_op jit(solution)/shard_map/ppermute | solution.py:453
  36.9 0.0 collective-permute-done.4
  38.1 3.3 %collective-permute-start.5 = (f32[]{:T(128)}, f32[]{:T(128)}, u32[]{:S(2)}, u32[]{:S(2)}) collective-permute-start(f32[]{:T(128)} %add.91), channel_id=1, source_target_pairs={{0,4},{2,6},{4,0},{6,2},{8,12},{10,14},{12,8},{14,10},{16,20},{18,... | collective-permute-start | bytes 20 | tf_op jit(solution)/shard_map/ppermute | solution.py:401
  41.4 0.4 collective-permute-done.5
  42.5 3.4 %collective-permute-start.6 = (f32[]{:T(128)}, f32[]{:T(128)}, u32[]{:S(2)}, u32[]{:S(2)}) collective-permute-start(f32[]{:T(128)} %add.92), channel_id=1, source_target_pairs={{0,8},{2,10},{4,12},{6,14},{8,0},{10,2},{12,4},{14,6},{16,24},{18,... | collective-permute-start | bytes 20 | tf_op jit(solution)/shard_map/ppermute | solution.py:401
  45.9 0.3 collective-permute-done.6
  46.8 4.4 %collective-permute-start.7 = (f32[]{:T(128)}, f32[]{:T(128)}, u32[]{:S(2)}, u32[]{:S(2)}) collective-permute-start(f32[]{:T(128)} %add.93), channel_id=1, source_target_pairs={{0,16},{2,18},{4,20},{6,22},{8,24},{10,26},{12,28},{14,30},{16,0},... | collective-permute-start | bytes 20 | tf_op jit(solution)/shard_map/ppermute | solution.py:401
  51.2 0.3 collective-permute-done.7
  51.6 1.5 %collective-permute-start.9 = (f32[32]{0:T(128)S(1)}, f32[32]{0:T(128)S(1)}, u32[]{:S(2)}, u32[]{:S(2)}) collective-permute-start(f32[32]{0:T(128)S(1)} %multiply_multiply_fusion), channel_id=1, source_target_pairs={{2,0},{4,2},{6,4},{8,6},{10,8},{12,10},{14,12},{16,14},{18,16},{20... | collective-permute-start | bytes 392 | tf_op jit(solution)/shard_map/ppermute | solution.py:454
  53.7 0.0 collective-permute-done.8
  53.7 1.8 %collective-permute-start.13 = (f32[200,512]{1,0:T(8,128)}, f32[200,512]{1,0:T(8,128)}, u32[]{:S(2)}, u32[]{:S(2)}) collective-permute-start(f32[200,512]{1,0:T(8,128)} %get-tuple-element.33), channel_id=1, source_target_pairs={{0,1},{1,0},{2,3},{3,2},{4,5},{5,4},{6,7},{7,6},{8,9},{9,8},{10,11... | collective-permute-start | bytes 1228808 | tf_op jit(solution)/shard_map/ppermute | solution.py:390
  55.5 0.0 collective-permute-done.9
  55.5 0.1 maximum_multiply_fusion
  55.6 0.2 select_reduce_fusion
  55.8 0.0 copy-start.8
  55.8 0.1 broadcast_multiply_fusion
  55.9 0.1 mul.94
  56.0 0.2 broadcast_in_dim.45.refs_2_.damp_ref.refs_3_
  56.1 0.0 copy-start.1
  56.1 2.4 %copy-done.1 = f32[3,800,512]{2,1,0:T(8,128)S(1)} copy-done((f32[3,800,512]{2,1,0:T(8,128)S(1)}, f32[3,800,512]{2,1,0:T(8,128)}, u32[]{:S(2)}) %copy-start.1) | copy-done | bytes 4915224
  58.5 1.6 %copy-done.2 = bf16[2,2,512,512]{3,2,1,0:T(8,128)(2,1)S(1)} copy-done((bf16[2,2,512,512]{3,2,1,0:T(8,128)(2,1)S(1)}, bf16[2,2,512,512]{3,2,1,0:T(8,128)(2,1)}, u32[]{:S(2)}) %copy-start.2) | copy-done | bytes 2097176
  60.1 3.6 %advance_2_0.1 = (f32[3,800,512]{2,1,0:T(8,128)}, f32[800,1024]{1,0:T(8,128)S(1)}) custom-call(f32[3,800,512]{2,1,0:T(8,128)S(1)} %copy-done.1, f32[200,512]{1,0:T(8,128)S(1)} %pad_maximum_fusion.1.refs_1_, f32[800,128]{1,0:T(8,128)S(1)} %broadcast_in_dim.45.refs_2_.damp_ref.refs_3_, bf16[2,2,512,512]{3,2,1,0:T(8,128)(2,1)S(1)} %copy-done.2, ...), custom_call_target="tpu_custom_call" | custom-call | flops 943718400 | bytes 819200 | tf_op jit(solution)/shard_map/advance_2_0/pallas_call | solution.py:294
  63.7 0.0 collective-permute-done.refs_1_.far_ref
  63.7 10.3 %advance_2_200.1 = (f32[3,800,512]{2,1,0:T(8,128)}, f32[800,1024]{1,0:T(8,128)S(1)}) custom-call(f32[3,800,512]{2,1,0:T(8,128)S(1)} %copy-done.1, f32[800,512]{1,0:T(8,128)} %collective-permute-done.refs_1_.far_ref, f32[800,128]{1,0:T(8,128)S(1)} %broadcast_in_dim.45.refs_2_.damp_ref.refs_3_, ...), custom_call_target="tpu_custom_call", output_to_operand_aliasing={{0}: (6, {}), {1}: (7, {})} | custom-call | flops 2831155200 | bytes 2457600 | tf_op jit(solution)/shard_map/advance_2_200/pallas_call | solution.py:294
  74.0 3.3 %both_groups.1 = (f32[200,512]{1,0:T(8,128)S(1)}, f32[200,256]{1,0:T(8,128)S(1)}, f32[200,128]{1,0:T(8,128)S(1)}, f32[200,128]{1,0:T(8,128)S(1)}) custom-call(s32[1]{0:T(128)} %bitcast.3.at_ref, f32[3,800,512]{2,1,0:T(8,128)S(1)} %copy-done.1, f32[800,512]{1,0:T(8,128)} %collective-permute-done.refs_1_.far_ref, ...), custom_call_target="tpu_custom_call" | custom-call | tf_op jit(solution)/shard_map/both_groups/pallas_call | solution.py:329
  77.3 0.8 collective-permute-start.12
  78.2 1.2 %collective-permute-start.11 = (f32[200,128]{1,0:T(8,128)S(1)}, f32[200,128]{1,0:T(8,128)S(1)}, u32[]{:S(2)}, u32[]{:S(2)}) collective-permute-start(f32[200,128]{1,0:T(8,128)S(1)} %get-tuple-element.28), channel_id=1, source_target_pairs={{0,1},{1,0},{2,3},{3,2},{4,5},{5,4},{6,7},{7,6},{8,9},{9,8},{10,11... | collective-permute-start | bytes 307208 | tf_op jit(solution)/shard_map/ppermute | solution.py:390
  79.4 2.0 %finish_here.1.refs_7_ = f32[3,800,512]{2,1,0:T(8,128)} custom-call(s32[1]{0:T(128)} %bitcast.3.at_ref, f32[3,800,512]{2,1,0:T(8,128)S(1)} %copy-done.1, f32[200,512]{1,0:T(8,128)S(1)} %get-tuple-element.30.span_ref, f32[800,128]{1,0:T(8,128)S(1)} %broadcast_in_dim.45.refs_2_.damp_ref.refs_3_, ...), custom_call_target="tpu_custom_call", output_to_operand_aliasing={{}: (5, {})} | custom-call | tf_op jit(solution)/shard_map/finish_here/pallas_call | solution.py:366
  81.4 5.4 %collective-permute-done.15.refs_1_ = f32[800,512]{1,0:T(8,128)} collective-permute-done((f32[800,512]{1,0:T(8,128)}, f32[800,512]{1,0:T(8,128)}, u32[]{:S(2)}, u32[]{:S(2)}) %collective-permute-start.15) | collective-permute-done | bytes 1638432 | tf_op jit(solution)/shard_map/ppermute | solution.py:390
  86.9 0.5 collective-permute-start.10
  87.4 13.0 %advance_0_0.1.refs_7_ = f32[3,800,512]{2,1,0:T(8,128)} custom-call(f32[3,800,512]{2,1,0:T(8,128)S(1)} %copy-done.1, f32[800,512]{1,0:T(8,128)} %collective-permute-done.15.refs_1_, f32[800,1024]{1,0:T(8,128)S(1)} %get-tuple-element.26.wphys_ref.refs_2_, f32[800,128]{1,0:T(8,128)S(1)} %broadcast_in_dim.45.refs_2_.damp_ref.refs_3_, ...), custom_call_target="tpu_custom_call", output_to_operand_aliasing={{}: (7, {})} | custom-call | flops 3774873600 | bytes 3276800 | tf_op jit(solution)/shard_map/advance_0_0/pallas_call | solution.py:294
  100.3 0.0 collective-permute-done.14.refs_1_
  100.3 3.5 %advance_1_0.1.refs_7_ = f32[3,800,512]{2,1,0:T(8,128)} custom-call(f32[3,800,512]{2,1,0:T(8,128)S(1)} %copy-done.1, f32[200,512]{1,0:T(8,128)S(1)} %collective-permute-done.14.refs_1_, f32[800,1024]{1,0:T(8,128)S(1)} %get-tuple-element.26.wphys_ref.refs_2_, ...), custom_call_target="tpu_custom_call", output_to_operand_aliasing={{}: (7, {})} | custom-call | flops 943718400 | bytes 819200 | tf_op jit(solution)/shard_map/advance_1_0/pallas_call | solution.py:294
  103.9 0.5 collective-permute-done.13.refs_1_
  104.4 4.5 %advance_1_200.1.held_ref = f32[3,800,512]{2,1,0:T(8,128)} custom-call(f32[3,800,512]{2,1,0:T(8,128)S(1)} %copy-done.1, f32[200,512]{1,0:T(8,128)} %collective-permute-done.13.refs_1_, f32[800,1024]{1,0:T(8,128)S(1)} %get-tuple-element.26.wphys_ref.refs_2_, f32[800,128]{1,0:T(8,128)S(1)} %broadcast_in_dim.45.refs_2_.damp_ref.refs_3_, ...), custom_call_target="tpu_custom_call", output_to_operand_aliasing={{}: (7, {})} | custom-call | flops 943718400 | bytes 819200 | tf_op jit(solution)/shard_map/advance_1_200/pallas_call | solution.py:294
  109.0 1.1 %finish_there_0.1.held_ref = f32[3,800,512]{2,1,0:T(8,128)} custom-call(s32[1]{0:T(128)} %bitcast.at_ref, f32[3,800,512]{2,1,0:T(8,128)S(1)} %copy-done.1, f32[200,256]{1,0:T(8,128)S(1)} %collective-permute-done.12.span_ref, f32[800,128]{1,0:T(8,128)S(1)} %broadcast_in_dim.45.refs_2_.damp_ref.refs_3_, ...), custom_call_target="tpu_custom_call", output_to_operand_aliasing={{}: (5, {})} | custom-call | tf_op jit(solution)/shard_map/finish_there_0/pallas_call | solution.py:366
  110.1 0.9 finish_there_2.1.held_ref
  111.0 0.1 collective-permute-done.10.span_ref
  111.1 0.9 finish_there_3.1
  (29 shorter events, 0.1 us)
Async XLA Ops:
  1.6 30.8 %collective-permute-start.2 = (f32[80,512]{1,0:T(8,128)S(1)}, f32[80,512]{1,0:T(8,128)}, u32[]{:S(2)}, u32[]{:S(2)}) collective-permute-start(f32[80,512]{1,0:T(8,128)S(1)} %slice_bitcast_fusion.4), channel_id=1, source_target_pairs={{0,1},{1,0},{2,3},{3,2},{4,5},{5,4},{6,7},{7,6},{8,9},{9,8},{10,11... | collective-permute-start | bytes 491528 | tf_op jit(solution)/shard_map/ppermute | solution.py:390
  5.6 27.0 %collective-permute-start.3 = (f32[120,512]{1,0:T(8,128)S(1)}, f32[120,512]{1,0:T(8,128)}, u32[]{:S(2)}, u32[]{:S(2)}) collective-permute-start(f32[120,512]{1,0:T(8,128)S(1)} %slice_bitcast_fusion.3), channel_id=1, source_target_pairs={{0,1},{1,0},{2,3},{3,2},{4,5},{5,4},{6,7},{7,6},{8,9},{9,8},{10,11... | collective-permute-start | bytes 737288 | tf_op jit(solution)/shard_map/ppermute | solution.py:390
  5.7 2.4 %copy-start = (f32[3,800,512]{2,1,0:T(8,128)S(1)}, f32[3,800,512]{2,1,0:T(8,128)}, u32[]{:S(2)}) copy-start(f32[3,800,512]{2,1,0:T(8,128)} %own_ref.4) | copy-start | bytes 14745604
  10.7 22.9 %collective-permute-start.1 = (f32[2,8,128]{2,1,0:T(8,128)S(1)}, f32[2,8,128]{2,1,0:T(8,128)S(1)}, u32[]{:S(2)}, u32[]{:S(2)}) collective-permute-start(f32[2,8,128]{2,1,0:T(8,128)S(1)} %get-tuple-element.19), channel_id=1, source_target_pairs={{0,1},{1,0},{2,3},{3,2},{4,5},{5,4},{6,7},{7,6},{8,9},{9,8},{10,11... | collective-permute-start | bytes 24584 | tf_op jit(solution)/shard_map/ppermute | solution.py:390
  12.7 11.4 %copy-start.7 = (s32[32,4]{0,1:T(4,128)S(1)}, s32[32,4]{0,1:T(4,128)}, u32[]{:S(2)}) copy-start(s32[32,4]{0,1:T(4,128)} %param.11) | copy-start | bytes 1540
  12.7 11.4 %copy-start.10 = (s32[4]{0:T(128)S(1)}, s32[4]{0:T(128)}, u32[]{:S(2)}) copy-start(s32[4]{0:T(128)} %constant.77.clone) | copy-start | bytes 52
  12.7 11.5 %copy-start.6 = (bf16[2,2,2,256,512]{4,3,2,1,0:T(8,128)(2,1)S(1)}, bf16[2,2,2,256,512]{4,3,2,1,0:T(8,128)(2,1)}, u32[]{:S(2)}) copy-start(bf16[2,2,2,256,512]{4,3,2,1,0:T(8,128)(2,1)} %constant.79.clone) | copy-start | bytes 6291460
  12.7 51.0 %collective-permute-start = (f32[800,512]{1,0:T(8,128)}, f32[800,512]{1,0:T(8,128)}, u32[]{:S(2)}, u32[]{:S(2)}) collective-permute-start(f32[800,512]{1,0:T(8,128)} %get-tuple-element.21), channel_id=1, source_target_pairs={{0,1},{1,0},{2,3},{3,2},{4,5},{5,4},{6,7},{7,6},{8,9},{9,8},{10,11... | collective-permute-start | bytes 4915208 | tf_op jit(solution)/shard_map/ppermute | solution.py:390
  15.7 71.2 %collective-permute-start.15 = (f32[800,512]{1,0:T(8,128)}, f32[800,512]{1,0:T(8,128)}, u32[]{:S(2)}, u32[]{:S(2)}) collective-permute-start(f32[800,512]{1,0:T(8,128)} %slice_bitcast_fusion), channel_id=1, source_target_pairs={{0,1},{1,0},{2,3},{3,2},{4,5},{5,4},{6,7},{7,6},{8,9},{9,8},{10,11... | collective-permute-start | bytes 4915208 | tf_op jit(solution)/shard_map/ppermute | solution.py:390
  26.1 2.8 %copy-start.4 = (f32[256,25,25]{0,2,1:T(8,128)S(1)}, f32[256,25,25]{0,2,1:T(8,128)}, u32[]{:S(2)}) copy-start(f32[256,25,25]{0,2,1:T(8,128)} %param.10) | copy-start | bytes 1920004
  26.1 2.8 %copy-start.5 = (bf16[256,512]{1,0:T(8,128)(2,1)S(1)}, bf16[256,512]{1,0:T(8,128)(2,1)}, u32[]{:S(2)}) copy-start(bf16[256,512]{1,0:T(8,128)(2,1)} %constant.81.clone.spread_ref) | copy-start | bytes 786436
  28.8 5.6 %copy-start.11 = (s32[32]{0:T(128)S(1)}, s32[32]{0:T(128)}, u32[]{:S(2)}) copy-start(s32[32]{0:T(128)} %param.12) | copy-start | bytes 388
  28.8 26.9 %copy-start.9 = (f32[25]{0:T(128)S(1)}, f32[25]{0:T(128)}, u32[]{:S(2)}) copy-start(f32[25]{0:T(128)} %constant.82) | copy-start | bytes 304
  32.3 68.0 %collective-permute-start.14 = (f32[200,512]{1,0:T(8,128)}, f32[200,512]{1,0:T(8,128)S(1)}, u32[]{:S(2)}, u32[]{:S(2)}) collective-permute-start(f32[200,512]{1,0:T(8,128)} %get-tuple-element.32), channel_id=1, source_target_pairs={{0,1},{1,0},{2,3},{3,2},{4,5},{5,4},{6,7},{7,6},{8,9},{9,8},{10,11... | collective-permute-start | bytes 1228808 | tf_op jit(solution)/shard_map/ppermute | solution.py:390
  34.3 2.6 %collective-permute-start.4 = (f32[]{:T(128)}, f32[]{:T(128)}, u32[]{:S(2)}, u32[]{:S(2)}) collective-permute-start(f32[]{:T(128)} %get-tuple-element.40), channel_id=1, source_target_pairs={{0,2},{2,0},{4,6},{6,4},{8,10},{10,8},{12,14},{14,12},{16,18},{18,... | collective-permute-start | bytes 20 | tf_op jit(solution)/shard_map/ppermute | solution.py:401
  34.4 19.3 %collective-permute-start.8 = (f32[32]{0:T(128)S(1)}, f32[32]{0:T(128)S(1)}, u32[]{:S(2)}, u32[]{:S(2)}) collective-permute-start(f32[32]{0:T(128)S(1)} %multiply_multiply_fusion), channel_id=1, source_target_pairs={{0,2},{2,4},{4,6},{6,8},{8,10},{10,12},{12,14},{14,16},{16,18},{18... | collective-permute-start | bytes 392 | tf_op jit(solution)/shard_map/ppermute | solution.py:453
  38.1 3.7 %collective-permute-start.5 = (f32[]{:T(128)}, f32[]{:T(128)}, u32[]{:S(2)}, u32[]{:S(2)}) collective-permute-start(f32[]{:T(128)} %add.91), channel_id=1, source_target_pairs={{0,4},{2,6},{4,0},{6,2},{8,12},{10,14},{12,8},{14,10},{16,20},{18,... | collective-permute-start | bytes 20 | tf_op jit(solution)/shard_map/ppermute | solution.py:401
  42.5 3.7 %collective-permute-start.6 = (f32[]{:T(128)}, f32[]{:T(128)}, u32[]{:S(2)}, u32[]{:S(2)}) collective-permute-start(f32[]{:T(128)} %add.92), channel_id=1, source_target_pairs={{0,8},{2,10},{4,12},{6,14},{8,0},{10,2},{12,4},{14,6},{16,24},{18,... | collective-permute-start | bytes 20 | tf_op jit(solution)/shard_map/ppermute | solution.py:401
  46.8 4.7 %collective-permute-start.7 = (f32[]{:T(128)}, f32[]{:T(128)}, u32[]{:S(2)}, u32[]{:S(2)}) collective-permute-start(f32[]{:T(128)} %add.93), channel_id=1, source_target_pairs={{0,16},{2,18},{4,20},{6,22},{8,24},{10,26},{12,28},{14,30},{16,0},... | collective-permute-start | bytes 20 | tf_op jit(solution)/shard_map/ppermute | solution.py:401
  51.6 3.9 %collective-permute-start.9 = (f32[32]{0:T(128)S(1)}, f32[32]{0:T(128)S(1)}, u32[]{:S(2)}, u32[]{:S(2)}) collective-permute-start(f32[32]{0:T(128)S(1)} %multiply_multiply_fusion), channel_id=1, source_target_pairs={{2,0},{4,2},{6,4},{8,6},{10,8},{12,10},{14,12},{16,14},{18,16},{20... | collective-permute-start | bytes 392 | tf_op jit(solution)/shard_map/ppermute | solution.py:454
  53.7 50.7 %collective-permute-start.13 = (f32[200,512]{1,0:T(8,128)}, f32[200,512]{1,0:T(8,128)}, u32[]{:S(2)}, u32[]{:S(2)}) collective-permute-start(f32[200,512]{1,0:T(8,128)} %get-tuple-element.33), channel_id=1, source_target_pairs={{0,1},{1,0},{2,3},{3,2},{4,5},{5,4},{6,7},{7,6},{8,9},{9,8},{10,11... | collective-permute-start | bytes 1228808 | tf_op jit(solution)/shard_map/ppermute | solution.py:390
  55.8 7.9 %copy-start.8 = (f32[32]{0:T(128)}, f32[32]{0:T(128)S(1)}, u32[]{:S(2)}) copy-start(f32[32]{0:T(128)S(1)} %add_multiply_fusion.1) | copy-start | bytes 388
  56.1 2.4 %copy-start.1 = (f32[3,800,512]{2,1,0:T(8,128)S(1)}, f32[3,800,512]{2,1,0:T(8,128)}, u32[]{:S(2)}) copy-start(f32[3,800,512]{2,1,0:T(8,128)} %own_ref.4) | copy-start | bytes 14745604
  58.5 1.6 %copy-start.2 = (bf16[2,2,512,512]{3,2,1,0:T(8,128)(2,1)S(1)}, bf16[2,2,512,512]{3,2,1,0:T(8,128)(2,1)}, u32[]{:S(2)}) copy-start(bf16[2,2,512,512]{3,2,1,0:T(8,128)(2,1)} %pad_maximum_fusion.refs_3_.synth_ref.refs_4_) | copy-start | bytes 6291460
  63.7 10.3 %copy-start.3 = (bf16[2,2,512,256]{3,2,1,0:T(8,128)(2,1)S(1)}, bf16[2,2,512,256]{3,2,1,0:T(8,128)(2,1)}, u32[]{:S(2)}) copy-start(bf16[2,2,512,256]{3,2,1,0:T(8,128)(2,1)} %get-tuple-element.34.other_ref) | copy-start | bytes 3145732
  77.3 31.7 %collective-permute-start.12 = (f32[200,256]{1,0:T(8,128)S(1)}, f32[200,256]{1,0:T(8,128)S(1)}, u32[]{:S(2)}, u32[]{:S(2)}) collective-permute-start(f32[200,256]{1,0:T(8,128)S(1)} %get-tuple-element.29), channel_id=1, source_target_pairs={{0,1},{1,0},{2,3},{3,2},{4,5},{5,4},{6,7},{7,6},{8,9},{9,8},{10,11... | collective-permute-start | bytes 614408 | tf_op jit(solution)/shard_map/ppermute | solution.py:390
  78.2 31.9 %collective-permute-start.11 = (f32[200,128]{1,0:T(8,128)S(1)}, f32[200,128]{1,0:T(8,128)S(1)}, u32[]{:S(2)}, u32[]{:S(2)}) collective-permute-start(f32[200,128]{1,0:T(8,128)S(1)} %get-tuple-element.28), channel_id=1, source_target_pairs={{0,1},{1,0},{2,3},{3,2},{4,5},{5,4},{6,7},{7,6},{8,9},{9,8},{10,11... | collective-permute-start | bytes 307208 | tf_op jit(solution)/shard_map/ppermute | solution.py:390
  86.9 24.2 %collective-permute-start.10 = (f32[200,128]{1,0:T(8,128)S(1)}, f32[200,128]{1,0:T(8,128)S(1)}, u32[]{:S(2)}, u32[]{:S(2)}) collective-permute-start(f32[200,128]{1,0:T(8,128)S(1)} %get-tuple-element.27), channel_id=1, source_target_pairs={{0,1},{1,0},{2,3},{3,2},{4,5},{5,4},{6,7},{7,6},{8,9},{9,8},{10,11... | collective-permute-start | bytes 307208 | tf_op jit(solution)/shard_map/ppermute | solution.py:390

commit v6 on v5

--- a/solution.py
+++ b/solution.py
@@ -429,7 +429,8 @@
     far[w, TILE, points - TILE] = exchange(rest)
     tail, velocity = lax.optimization_barrier((packed, velocity))
     for comp in range(w - 1):
-        far[comp, 0, points] = exchange(velocity[comp])
+        for begin, end in ((0, points - TILE), (points - TILE, points)):
+            far[comp, begin, end - begin] = exchange(velocity[comp, begin:end])
     stop = points - 2 * TILE if shared else points
     for begin in range(0, stop, TILE):
         far[w - 1, begin, TILE] = exchange(velocity[w - 1, begin : begin + TILE])

time: 112 us -> 113 us (level)
  waiting for transfers between devices: 7.17 us -> 3.56 us
  Pallas kernels: 49.2 us -> 51.1 us
  starting transfers between devices: 26.5 us -> 28 us
    ppermute x10 -> x11, waiting for transfers between devices: 6.09 us -> 2.95 us  [exchange(): lax.ppermute(block, 'mode', [(i, (i + s) % count) for i in range(count)])]
    pallas_call x5 -> x6, Pallas kernels: 35 us -> 36.9 us  [advance(): pl.pallas_call(lambda *refs: chunk_kernel(len(far), is_w, len(aliases), *...]
    ppermute x10 -> x11, starting transfers between devices: 11.6 us -> 13.2 us  [exchange(): lax.ppermute(block, 'mode', [(i, (i + s) % count) for i in range(count)])]
    squeeze x2, local copies, waits for them, and re-layouts: 5.03 us -> 3.45 us  [on_device(): far[comp, begin, end - begin] = exchange(velocity[comp, begin:end])]
    squeeze x1, local copies, waits for them, and re-layouts: 0.18 us -> 1.69 us  [on_device(): x[p]]
    unnamed x24 -> x22, local copies, waits for them, and re-layouts: 6.41 us -> 6.4 us
  transfers between devices with their start and end apart: 16 -> 17, of which waited for: 6 -> 5; matrix products, arithmetic and copies ran while one was open for 12% -> 12% of each run, Pallas kernels for 43% -> 45%
where the time goes in v6:
time: 113 us; the launch traced here: 112 us
  Pallas kernels  51.1 us (45%)
  starting transfers between devices  28 us (25%)
  local copies, waits for them, and re-layouts  17.2 us (15%)
  between operations  8.13 us (7%)
  other arithmetic  3.83 us (3%)
  waiting for transfers between devices  3.56 us (3%)
    pallas_call x6, Pallas kernels, advance(): pl.pallas_call(lambda *refs: chunk_kernel(len(far), is_w, len(aliases), *...  36.9 us
    ppermute x11, starting transfers between devices, exchange(): lax.ppermute(block, 'mode', [(i, (i + s) % count) for i in range(count)])  13.2 us
    ppermute x4, starting transfers between devices, sum_over_plane(): lax.ppermute(value, 'plane', [(i, i ^ step) for i in range(count)])  11.1 us
    unnamed x22, local copies, waits for them, and re-layouts  6.4 us
    pallas_call x4, Pallas kernels, finish(): pl.pallas_call(finish_kernel, grid_spec=pltpu.PrefetchScalarGridSpec(num_...  4.87 us
    pallas_call x1, Pallas kernels, expand(): pl.pallas_call(expand_kernel, out_shape=jax.ShapeDtypeStruct((width // LA...  3.48 us
    squeeze x2, local copies, waits for them, and re-layouts, on_device(): far[comp, begin, end - begin] = exchange(velocity[comp, begin:end])  3.45 us
    pallas_call x1, Pallas kernels, both_groups(): pl.pallas_call(both_kernel, grid_spec=pltpu.PrefetchScalarGridSpec(num_sc...  3.29 us
  transfers between devices with their start and end apart: 17, of which 5 were waited for; matrix products, arithmetic and copies ran while one was open for 12% of the time, Pallas kernels for 45%

profile of v6, /device:TPU:0, one launch (start us, length us, event | category | flops | bytes accessed | tf_op | source)
XLA Modules:
  0.0 111.9 jit_solution(10232020207861487080)
XLA Ops:
  0.6 0.9 slice_bitcast_fusion.5
  1.6 3.0 %collective-permute-start.2 = (f32[80,512]{1,0:T(8,128)S(1)}, f32[80,512]{1,0:T(8,128)}, u32[]{:S(2)}, u32[]{:S(2)}) collective-permute-start(f32[80,512]{1,0:T(8,128)S(1)} %slice_bitcast_fusion.5), channel_id=1, source_target_pairs={{0,1},{1,0},{2,3},{3,2},{4,5},{5,4},{6,7},{7,6},{8,9},{9,8},{10,11... | collective-permute-start | bytes 491528 | tf_op jit(solution)/shard_map/ppermute | solution.py:390
  4.6 1.0 slice_bitcast_fusion.4
  5.6 0.1 collective-permute-start.3
  5.7 0.0 copy-start
  5.7 2.4 %copy-done = f32[3,800,512]{2,1,0:T(8,128)S(1)} copy-done((f32[3,800,512]{2,1,0:T(8,128)S(1)}, f32[3,800,512]{2,1,0:T(8,128)}, u32[]{:S(2)}) %copy-start) | copy-done | bytes 4915224
  8.1 2.6 %first_pass.1 = (f32[2,8,128]{2,1,0:T(8,128)S(1)}, f32[800,512]{1,0:T(8,128)}) custom-call(s32[1]{0:T(128)} %bitcast.at_ref, f32[3,800,512]{2,1,0:T(8,128)S(1)} %copy-done, f32[1,512]{1,0:T(1,128)S(1)} %compare_select_fusion.weight_ref), custom_call_target="tpu_custom_call" | custom-call | tf_op jit(solution)/shard_map/first_pass/pallas_call | solution.py:143
  10.7 2.0 %collective-permute-start.1 = (f32[2,8,128]{2,1,0:T(8,128)S(1)}, f32[2,8,128]{2,1,0:T(8,128)S(1)}, u32[]{:S(2)}, u32[]{:S(2)}) collective-permute-start(f32[2,8,128]{2,1,0:T(8,128)S(1)} %get-tuple-element.19), channel_id=1, source_target_pairs={{0,1},{1,0},{2,3},{3,2},{4,5},{5,4},{6,7},{7,6},{8,9},{9,8},{10,11... | collective-permute-start | bytes 24584 | tf_op jit(solution)/shard_map/ppermute | solution.py:390
  12.7 0.0 collective-permute-start
  12.7 1.1 %slice_bitcast_fusion = f32[600,512]{1,0:T(8,128)} fusion(f32[3,800,512]{2,1,0:T(8,128)S(1)} %copy-done), kind=kLoop, calls=%fused_computation.1 | loop fusion | bytes 2457600 | tf_op jit(solution)/shard_map/squeeze | solution.py:433
  13.8 2.0 %collective-permute-start.16 = (f32[600,512]{1,0:T(8,128)}, f32[600,512]{1,0:T(8,128)}, u32[]{:S(2)}, u32[]{:S(2)}) collective-permute-start(f32[600,512]{1,0:T(8,128)} %slice_bitcast_fusion), channel_id=1, source_target_pairs={{0,1},{1,0},{2,3},{3,2},{4,5},{5,4},{6,7},{7,6},{8,9},{9,8},{10,11... | collective-permute-start | bytes 3686408 | tf_op jit(solution)/shard_map/ppermute | solution.py:390
  15.8 0.6 fusion.8
  19.0 2.3 %slice_bitcast_fusion.1 = (f32[200,512]{1,0:T(8,128)}, f32[200,512]{1,0:T(8,128)}, f32[200,512]{1,0:T(8,128)}) fusion(f32[3,800,512]{2,1,0:T(8,128)} %own_ref.4), kind=kLoop, calls=%fused_computation.11 | loop fusion | bytes 2457600 | tf_op jit(solution)/shard_map/squeeze | solution.py:433
  22.7 0.1 add_select_fusion
  22.7 1.7 %dynamic-slice_bitcast_fusion.5 = (bf16[2,256,512]{2,1,0:T(8,128)(2,1)S(1)}, bf16[2,256,512]{2,1,0:T(8,128)(2,1)S(1)}, bf16[2,256,512]{2,1,0:T(8,128)(2,1)S(1)}, bf16[2,256,512]{2,1,0:T(8,128)(2,1)S(1)}) fusion(bf16[2,2,2,256,512]{4,3,2,1,0:T(8,128)(2,1)} %constant.79.clone, s32[]{:T(128)S(6)} %select_n.44, s32[]{:T(128)S(6)} %select_n.45, s32[]{:T(128)S(6)} %add.110), kind=kLoop, calls=%fused_computation.9 | loop fusion | bytes 4194316 | tf_op jit(solution)/shard_map/squeeze | solution.py:475
  24.4 0.2 maximum_bitcast_fusion
  24.6 1.5 %pad_maximum_fusion.refs_3_.synth_ref.refs_4_ = bf16[2,2,512,512]{3,2,1,0:T(8,128)(2,1)} fusion(bf16[1,2,512,512]{3,2,1,0:T(8,128)(2,1)S(1)} %get-tuple-element.46, bf16[1,2,512,512]{3,2,1,0:T(8,128)(2,1)S(1)} %get-tuple-element.45), kind=kLoop, calls=%fused_computation | loop fusion | flops 1048576 | bytes 4194304 | tf_op jit(solution)/shard_map/stack | solution.py:475
  26.2 2.8 %dynamic-slice_bitcast_fusion = (bf16[2,2,512,256]{3,2,1,0:T(8,128)(2,1)}, bf16[2,2,512,256]{3,2,1,0:T(8,128)(2,1)S(1)}) fusion(bf16[2,2,2,512,256]{4,3,2,1,0:T(8,128)(2,1)} %constant.80.clone, s32[]{:T(128)S(6)} %select_n.47, s32[]{:T(128)S(6)} %select_n.46), kind=kLoop, calls=%fused_computation.4 | loop fusion | bytes 4194312 | tf_op jit(solution)/shard_map/jit(dynamic_index_in_dim)/squeeze | solution.py:472
  28.9 3.5 %expand.1.refs_5_.inv_ref.refs_6_ = f32[4,25,25,128]{3,2,1,0:T(8,128)S(1)} custom-call(f32[25,25,256]{2,1,0:T(8,128)S(1)} %bitcast.35, bf16[256,512]{1,0:T(8,128)(2,1)S(1)} %copy-done.5), custom_call_target="tpu_custom_call" | custom-call | tf_op jit(solution)/shard_map/expand/pallas_call | solution.py:178
  32.4 0.1 collective-permute-start.15
  32.5 0.0 collective-permute-done.3
  32.5 1.1 pad_maximum_fusion.1.refs_1_
  33.5 0.0 collective-permute-done.1
  33.6 0.6 slice_reduce_fusion
  34.2 0.0 collective-permute-start.4
  34.2 0.1 copy.23
  34.2 0.1 reshape.101
  34.3 2.4 %collective-permute-start.8 = (f32[32]{0:T(128)S(1)}, f32[32]{0:T(128)S(1)}, u32[]{:S(2)}, u32[]{:S(2)}) collective-permute-start(f32[32]{0:T(128)S(1)} %multiply_multiply_fusion), channel_id=1, source_target_pairs={{0,2},{2,4},{4,6},{6,8},{8,10},{10,12},{12,14},{14,16},{16,18},{18... | collective-permute-start | bytes 392 | tf_op jit(solution)/shard_map/ppermute | solution.py:454
  36.8 0.0 collective-permute-done.4
  38.1 3.3 %collective-permute-start.5 = (f32[]{:T(128)}, f32[]{:T(128)}, u32[]{:S(2)}, u32[]{:S(2)}) collective-permute-start(f32[]{:T(128)} %add.91), channel_id=1, source_target_pairs={{0,4},{2,6},{4,0},{6,2},{8,12},{10,14},{12,8},{14,10},{16,20},{18,... | collective-permute-start | bytes 20 | tf_op jit(solution)/shard_map/ppermute | solution.py:401
  41.4 0.2 collective-permute-done.5
  42.3 3.4 %collective-permute-start.6 = (f32[]{:T(128)}, f32[]{:T(128)}, u32[]{:S(2)}, u32[]{:S(2)}) collective-permute-start(f32[]{:T(128)} %add.92), channel_id=1, source_target_pairs={{0,8},{2,10},{4,12},{6,14},{8,0},{10,2},{12,4},{14,6},{16,24},{18,... | collective-permute-start | bytes 20 | tf_op jit(solution)/shard_map/ppermute | solution.py:401
  45.7 0.2 collective-permute-done.6
  46.6 4.4 %collective-permute-start.7 = (f32[]{:T(128)}, f32[]{:T(128)}, u32[]{:S(2)}, u32[]{:S(2)}) collective-permute-start(f32[]{:T(128)} %add.93), channel_id=1, source_target_pairs={{0,16},{2,18},{4,20},{6,22},{8,24},{10,26},{12,28},{14,30},{16,0},... | collective-permute-start | bytes 20 | tf_op jit(solution)/shard_map/ppermute | solution.py:401
  51.0 0.2 collective-permute-done.7
  51.2 1.3 %collective-permute-start.9 = (f32[32]{0:T(128)S(1)}, f32[32]{0:T(128)S(1)}, u32[]{:S(2)}, u32[]{:S(2)}) collective-permute-start(f32[32]{0:T(128)S(1)} %multiply_multiply_fusion), channel_id=1, source_target_pairs={{2,0},{4,2},{6,4},{8,6},{10,8},{12,10},{14,12},{16,14},{18,16},{20... | collective-permute-start | bytes 392 | tf_op jit(solution)/shard_map/ppermute | solution.py:455
  53.2 0.0 collective-permute-done.8
  53.2 1.9 %collective-permute-start.14 = (f32[200,512]{1,0:T(8,128)}, f32[200,512]{1,0:T(8,128)}, u32[]{:S(2)}, u32[]{:S(2)}) collective-permute-start(f32[200,512]{1,0:T(8,128)} %get-tuple-element.33), channel_id=1, source_target_pairs={{0,1},{1,0},{2,3},{3,2},{4,5},{5,4},{6,7},{7,6},{8,9},{9,8},{10,11... | collective-permute-start | bytes 1228808 | tf_op jit(solution)/shard_map/ppermute | solution.py:390
  55.1 0.9 collective-permute-start.13
  56.0 0.1 maximum_multiply_fusion
  56.1 0.2 select_reduce_fusion
  56.3 0.0 copy-start.7
  56.3 0.1 broadcast_multiply_fusion
  56.4 0.1 mul.94
  56.5 0.2 broadcast_in_dim.45.refs_2_.damp_ref.refs_3_
  56.7 0.0 copy-start.1
  56.7 2.4 %copy-done.1 = f32[3,800,512]{2,1,0:T(8,128)S(1)} copy-done((f32[3,800,512]{2,1,0:T(8,128)S(1)}, f32[3,800,512]{2,1,0:T(8,128)}, u32[]{:S(2)}) %copy-start.1) | copy-done | bytes 4915224
  59.1 1.6 %copy-done.2 = bf16[2,2,512,512]{3,2,1,0:T(8,128)(2,1)S(1)} copy-done((bf16[2,2,512,512]{3,2,1,0:T(8,128)(2,1)S(1)}, bf16[2,2,512,512]{3,2,1,0:T(8,128)(2,1)}, u32[]{:S(2)}) %copy-start.2) | copy-done | bytes 2097176
  60.7 3.7 %advance_2_0.1 = (f32[3,800,512]{2,1,0:T(8,128)}, f32[800,1024]{1,0:T(8,128)S(1)}) custom-call(f32[3,800,512]{2,1,0:T(8,128)S(1)} %copy-done.1, f32[200,512]{1,0:T(8,128)S(1)} %pad_maximum_fusion.1.refs_1_, f32[800,128]{1,0:T(8,128)S(1)} %broadcast_in_dim.45.refs_2_.damp_ref.refs_3_, bf16[2,2,512,512]{3,2,1,0:T(8,128)(2,1)S(1)} %copy-done.2, ...), custom_call_target="tpu_custom_call" | custom-call | flops 943718400 | bytes 819200 | tf_op jit(solution)/shard_map/advance_2_0/pallas_call | solution.py:294
  64.4 10.3 %advance_2_200.1 = (f32[3,800,512]{2,1,0:T(8,128)}, f32[800,1024]{1,0:T(8,128)S(1)}) custom-call(f32[3,800,512]{2,1,0:T(8,128)S(1)} %copy-done.1, f32[800,512]{1,0:T(8,128)} %collective-permute-done.refs_1_.far_ref, f32[800,128]{1,0:T(8,128)S(1)} %broadcast_in_dim.45.refs_2_.damp_ref.refs_3_, ...), custom_call_target="tpu_custom_call", output_to_operand_aliasing={{0}: (6, {}), {1}: (7, {})} | custom-call | flops 2831155200 | bytes 2457600 | tf_op jit(solution)/shard_map/advance_2_200/pallas_call | solution.py:294
  74.8 3.3 %both_groups.1 = (f32[200,512]{1,0:T(8,128)S(1)}, f32[200,256]{1,0:T(8,128)S(1)}, f32[200,128]{1,0:T(8,128)S(1)}, f32[200,128]{1,0:T(8,128)S(1)}) custom-call(s32[1]{0:T(128)} %bitcast.3.at_ref, f32[3,800,512]{2,1,0:T(8,128)S(1)} %copy-done.1, f32[800,512]{1,0:T(8,128)} %collective-permute-done.refs_1_.far_ref, ...), custom_call_target="tpu_custom_call" | custom-call | tf_op jit(solution)/shard_map/both_groups/pallas_call | solution.py:329
  78.0 1.2 %collective-permute-start.12 = (f32[200,256]{1,0:T(8,128)S(1)}, f32[200,256]{1,0:T(8,128)S(1)}, u32[]{:S(2)}, u32[]{:S(2)}) collective-permute-start(f32[200,256]{1,0:T(8,128)S(1)} %get-tuple-element.29), channel_id=1, source_target_pairs={{0,1},{1,0},{2,3},{3,2},{4,5},{5,4},{6,7},{7,6},{8,9},{9,8},{10,11... | collective-permute-start | bytes 614408 | tf_op jit(solution)/shard_map/ppermute | solution.py:390
  79.2 2.0 %finish_here.1.refs_7_ = f32[3,800,512]{2,1,0:T(8,128)} custom-call(s32[1]{0:T(128)} %bitcast.3.at_ref, f32[3,800,512]{2,1,0:T(8,128)S(1)} %copy-done.1, f32[200,512]{1,0:T(8,128)S(1)} %get-tuple-element.30.span_ref, f32[800,128]{1,0:T(8,128)S(1)} %broadcast_in_dim.45.refs_2_.damp_ref.refs_3_, ...), custom_call_target="tpu_custom_call", output_to_operand_aliasing={{}: (5, {})} | custom-call | tf_op jit(solution)/shard_map/finish_here/pallas_call | solution.py:366
  81.2 0.9 collective-permute-start.11
  82.2 10.2 %advance_0_0.1.refs_7_ = f32[3,800,512]{2,1,0:T(8,128)} custom-call(f32[3,800,512]{2,1,0:T(8,128)S(1)} %copy-done.1, f32[600,512]{1,0:T(8,128)} %collective-permute-done.16.refs_1_, f32[800,1024]{1,0:T(8,128)S(1)} %get-tuple-element.26.wphys_ref.refs_2_, f32[800,128]{1,0:T(8,128)S(1)} %broadcast_in_dim.45.refs_2_.damp_ref.refs_3_, ...), custom_call_target="tpu_custom_call", output_to_operand_aliasing={{}: (7, {})} | custom-call | flops 2831155200 | bytes 2457600 | tf_op jit(solution)/shard_map/advance_0_0/pallas_call | solution.py:294
  92.3 1.1 collective-permute-start.10
  93.4 3.5 %advance_0_600.1.refs_7_ = f32[3,800,512]{2,1,0:T(8,128)} custom-call(f32[3,800,512]{2,1,0:T(8,128)S(1)} %copy-done.1, f32[200,512]{1,0:T(8,128)S(1)} %collective-permute-done.15.refs_1_, f32[800,1024]{1,0:T(8,128)S(1)} %get-tuple-element.26.wphys_ref.refs_2_, ...), custom_call_target="tpu_custom_call", output_to_operand_aliasing={{}: (7, {})} | custom-call | flops 943718400 | bytes 819200 | tf_op jit(solution)/shard_map/advance_0_600/pallas_call | solution.py:294
  97.0 4.5 %advance_1_0.1.refs_7_ = f32[3,800,512]{2,1,0:T(8,128)} custom-call(f32[3,800,512]{2,1,0:T(8,128)S(1)} %copy-done.1, f32[200,512]{1,0:T(8,128)} %collective-permute-done.14.refs_1_, f32[800,1024]{1,0:T(8,128)S(1)} %get-tuple-element.26.wphys_ref.refs_2_, f32[800,128]{1,0:T(8,128)S(1)} %broadcast_in_dim.45.refs_2_.damp_ref.refs_3_, ...), custom_call_target="tpu_custom_call", output_to_operand_aliasing={{}: (7, {})} | custom-call | flops 943718400 | bytes 819200 | tf_op jit(solution)/shard_map/advance_1_0/pallas_call | solution.py:294
  101.5 2.8 %collective-permute-done.13.refs_1_ = f32[200,512]{1,0:T(8,128)} collective-permute-done((f32[200,512]{1,0:T(8,128)}, f32[200,512]{1,0:T(8,128)}, u32[]{:S(2)}, u32[]{:S(2)}) %collective-permute-start.13) | collective-permute-done | bytes 409632 | tf_op jit(solution)/shard_map/ppermute | solution.py:390
  104.4 4.5 %advance_1_200.1.held_ref = f32[3,800,512]{2,1,0:T(8,128)} custom-call(f32[3,800,512]{2,1,0:T(8,128)S(1)} %copy-done.1, f32[200,512]{1,0:T(8,128)} %collective-permute-done.13.refs_1_, f32[800,1024]{1,0:T(8,128)S(1)} %get-tuple-element.26.wphys_ref.refs_2_, f32[800,128]{1,0:T(8,128)S(1)} %broadcast_in_dim.45.refs_2_.damp_ref.refs_3_, ...), custom_call_target="tpu_custom_call", output_to_operand_aliasing={{}: (7, {})} | custom-call | flops 943718400 | bytes 819200 | tf_op jit(solution)/shard_map/advance_1_200/pallas_call | solution.py:294
  108.9 1.1 %finish_there_0.1.held_ref = f32[3,800,512]{2,1,0:T(8,128)} custom-call(s32[1]{0:T(128)} %bitcast.at_ref, f32[3,800,512]{2,1,0:T(8,128)S(1)} %copy-done.1, f32[200,256]{1,0:T(8,128)S(1)} %collective-permute-done.12.span_ref, f32[800,128]{1,0:T(8,128)S(1)} %broadcast_in_dim.45.refs_2_.damp_ref.refs_3_, ...), custom_call_target="tpu_custom_call", output_to_operand_aliasing={{}: (5, {})} | custom-call | tf_op jit(solution)/shard_map/finish_there_0/pallas_call | solution.py:366
  110.1 0.9 finish_there_2.1.held_ref
  110.9 0.1 collective-permute-done.10.span_ref
  111.0 0.9 finish_there_3.1
  (30 shorter events, 0.1 us)
Async XLA Ops:
  1.6 30.8 %collective-permute-start.2 = (f32[80,512]{1,0:T(8,128)S(1)}, f32[80,512]{1,0:T(8,128)}, u32[]{:S(2)}, u32[]{:S(2)}) collective-permute-start(f32[80,512]{1,0:T(8,128)S(1)} %slice_bitcast_fusion.5), channel_id=1, source_target_pairs={{0,1},{1,0},{2,3},{3,2},{4,5},{5,4},{6,7},{7,6},{8,9},{9,8},{10,11... | collective-permute-start | bytes 491528 | tf_op jit(solution)/shard_map/ppermute | solution.py:390
  5.6 26.9 %collective-permute-start.3 = (f32[120,512]{1,0:T(8,128)S(1)}, f32[120,512]{1,0:T(8,128)}, u32[]{:S(2)}, u32[]{:S(2)}) collective-permute-start(f32[120,512]{1,0:T(8,128)S(1)} %slice_bitcast_fusion.4), channel_id=1, source_target_pairs={{0,1},{1,0},{2,3},{3,2},{4,5},{5,4},{6,7},{7,6},{8,9},{9,8},{10,11... | collective-permute-start | bytes 737288 | tf_op jit(solution)/shard_map/ppermute | solution.py:390
  5.7 2.4 %copy-start = (f32[3,800,512]{2,1,0:T(8,128)S(1)}, f32[3,800,512]{2,1,0:T(8,128)}, u32[]{:S(2)}) copy-start(f32[3,800,512]{2,1,0:T(8,128)} %own_ref.4) | copy-start | bytes 14745604
  10.7 22.9 %collective-permute-start.1 = (f32[2,8,128]{2,1,0:T(8,128)S(1)}, f32[2,8,128]{2,1,0:T(8,128)S(1)}, u32[]{:S(2)}, u32[]{:S(2)}) collective-permute-start(f32[2,8,128]{2,1,0:T(8,128)S(1)} %get-tuple-element.19), channel_id=1, source_target_pairs={{0,1},{1,0},{2,3},{3,2},{4,5},{5,4},{6,7},{7,6},{8,9},{9,8},{10,11... | collective-permute-start | bytes 24584 | tf_op jit(solution)/shard_map/ppermute | solution.py:390
  12.7 10.0 %copy-start.6 = (s32[32,4]{0,1:T(4,128)S(1)}, s32[32,4]{0,1:T(4,128)}, u32[]{:S(2)}) copy-start(s32[32,4]{0,1:T(4,128)} %param.11) | copy-start | bytes 1540
  12.7 10.0 %copy-start.9 = (s32[4]{0:T(128)S(1)}, s32[4]{0:T(128)}, u32[]{:S(2)}) copy-start(s32[4]{0:T(128)} %constant.77.clone) | copy-start | bytes 52
  12.7 51.8 %collective-permute-start = (f32[800,512]{1,0:T(8,128)}, f32[800,512]{1,0:T(8,128)}, u32[]{:S(2)}, u32[]{:S(2)}) collective-permute-start(f32[800,512]{1,0:T(8,128)} %get-tuple-element.21), channel_id=1, source_target_pairs={{0,1},{1,0},{2,3},{3,2},{4,5},{5,4},{6,7},{7,6},{8,9},{9,8},{10,11... | collective-permute-start | bytes 4915208 | tf_op jit(solution)/shard_map/ppermute | solution.py:390
  13.8 67.4 %collective-permute-start.16 = (f32[600,512]{1,0:T(8,128)}, f32[600,512]{1,0:T(8,128)}, u32[]{:S(2)}, u32[]{:S(2)}) collective-permute-start(f32[600,512]{1,0:T(8,128)} %slice_bitcast_fusion), channel_id=1, source_target_pairs={{0,1},{1,0},{2,3},{3,2},{4,5},{5,4},{6,7},{7,6},{8,9},{9,8},{10,11... | collective-permute-start | bytes 3686408 | tf_op jit(solution)/shard_map/ppermute | solution.py:390
  26.1 2.8 %copy-start.4 = (f32[256,25,25]{0,2,1:T(8,128)S(1)}, f32[256,25,25]{0,2,1:T(8,128)}, u32[]{:S(2)}) copy-start(f32[256,25,25]{0,2,1:T(8,128)} %param.10) | copy-start | bytes 1920004
  26.1 2.8 %copy-start.5 = (bf16[256,512]{1,0:T(8,128)(2,1)S(1)}, bf16[256,512]{1,0:T(8,128)(2,1)}, u32[]{:S(2)}) copy-start(bf16[256,512]{1,0:T(8,128)(2,1)} %constant.81.clone.spread_ref) | copy-start | bytes 786436
  28.9 5.4 %copy-start.10 = (s32[32]{0:T(128)S(1)}, s32[32]{0:T(128)}, u32[]{:S(2)}) copy-start(s32[32]{0:T(128)} %param.12) | copy-start | bytes 388
  28.9 27.4 %copy-start.8 = (f32[25]{0:T(128)S(1)}, f32[25]{0:T(128)}, u32[]{:S(2)}) copy-start(f32[25]{0:T(128)} %constant.82) | copy-start | bytes 304
  32.4 59.9 %collective-permute-start.15 = (f32[200,512]{1,0:T(8,128)}, f32[200,512]{1,0:T(8,128)S(1)}, u32[]{:S(2)}, u32[]{:S(2)}) collective-permute-start(f32[200,512]{1,0:T(8,128)} %get-tuple-element.32), channel_id=1, source_target_pairs={{0,1},{1,0},{2,3},{3,2},{4,5},{5,4},{6,7},{7,6},{8,9},{9,8},{10,11... | collective-permute-start | bytes 1228808 | tf_op jit(solution)/shard_map/ppermute | solution.py:390
  34.2 2.6 %collective-permute-start.4 = (f32[]{:T(128)}, f32[]{:T(128)}, u32[]{:S(2)}, u32[]{:S(2)}) collective-permute-start(f32[]{:T(128)} %get-tuple-element.41), channel_id=1, source_target_pairs={{0,2},{2,0},{4,6},{6,4},{8,10},{10,8},{12,14},{14,12},{16,18},{18,... | collective-permute-start | bytes 20 | tf_op jit(solution)/shard_map/ppermute | solution.py:401
  34.3 18.8 %collective-permute-start.8 = (f32[32]{0:T(128)S(1)}, f32[32]{0:T(128)S(1)}, u32[]{:S(2)}, u32[]{:S(2)}) collective-permute-start(f32[32]{0:T(128)S(1)} %multiply_multiply_fusion), channel_id=1, source_target_pairs={{0,2},{2,4},{4,6},{6,8},{8,10},{10,12},{12,14},{14,16},{16,18},{18... | collective-permute-start | bytes 392 | tf_op jit(solution)/shard_map/ppermute | solution.py:454
  38.1 3.6 %collective-permute-start.5 = (f32[]{:T(128)}, f32[]{:T(128)}, u32[]{:S(2)}, u32[]{:S(2)}) collective-permute-start(f32[]{:T(128)} %add.91), channel_id=1, source_target_pairs={{0,4},{2,6},{4,0},{6,2},{8,12},{10,14},{12,8},{14,10},{16,20},{18,... | collective-permute-start | bytes 20 | tf_op jit(solution)/shard_map/ppermute | solution.py:401
  42.3 3.6 %collective-permute-start.6 = (f32[]{:T(128)}, f32[]{:T(128)}, u32[]{:S(2)}, u32[]{:S(2)}) collective-permute-start(f32[]{:T(128)} %add.92), channel_id=1, source_target_pairs={{0,8},{2,10},{4,12},{6,14},{8,0},{10,2},{12,4},{14,6},{16,24},{18,... | collective-permute-start | bytes 20 | tf_op jit(solution)/shard_map/ppermute | solution.py:401
  46.6 4.6 %collective-permute-start.7 = (f32[]{:T(128)}, f32[]{:T(128)}, u32[]{:S(2)}, u32[]{:S(2)}) collective-permute-start(f32[]{:T(128)} %add.93), channel_id=1, source_target_pairs={{0,16},{2,18},{4,20},{6,22},{8,24},{10,26},{12,28},{14,30},{16,0},... | collective-permute-start | bytes 20 | tf_op jit(solution)/shard_map/ppermute | solution.py:401
  51.2 3.9 %collective-permute-start.9 = (f32[32]{0:T(128)S(1)}, f32[32]{0:T(128)S(1)}, u32[]{:S(2)}, u32[]{:S(2)}) collective-permute-start(f32[32]{0:T(128)S(1)} %multiply_multiply_fusion), channel_id=1, source_target_pairs={{2,0},{4,2},{6,4},{8,6},{10,8},{12,10},{14,12},{16,14},{18,16},{20... | collective-permute-start | bytes 392 | tf_op jit(solution)/shard_map/ppermute | solution.py:455
  53.2 43.8 %collective-permute-start.14 = (f32[200,512]{1,0:T(8,128)}, f32[200,512]{1,0:T(8,128)}, u32[]{:S(2)}, u32[]{:S(2)}) collective-permute-start(f32[200,512]{1,0:T(8,128)} %get-tuple-element.33), channel_id=1, source_target_pairs={{0,1},{1,0},{2,3},{3,2},{4,5},{5,4},{6,7},{7,6},{8,9},{9,8},{10,11... | collective-permute-start | bytes 1228808 | tf_op jit(solution)/shard_map/ppermute | solution.py:390
  55.1 49.3 %collective-permute-start.13 = (f32[200,512]{1,0:T(8,128)}, f32[200,512]{1,0:T(8,128)}, u32[]{:S(2)}, u32[]{:S(2)}) collective-permute-start(f32[200,512]{1,0:T(8,128)} %get-tuple-element.34), channel_id=1, source_target_pairs={{0,1},{1,0},{2,3},{3,2},{4,5},{5,4},{6,7},{7,6},{8,9},{9,8},{10,11... | collective-permute-start | bytes 1228808 | tf_op jit(solution)/shard_map/ppermute | solution.py:390
  56.3 8.1 %copy-start.7 = (f32[32]{0:T(128)}, f32[32]{0:T(128)S(1)}, u32[]{:S(2)}) copy-start(f32[32]{0:T(128)S(1)} %add_multiply_fusion.1) | copy-start | bytes 388
  56.7 2.4 %copy-start.1 = (f32[3,800,512]{2,1,0:T(8,128)S(1)}, f32[3,800,512]{2,1,0:T(8,128)}, u32[]{:S(2)}) copy-start(f32[3,800,512]{2,1,0:T(8,128)} %own_ref.4) | copy-start | bytes 14745604
  59.1 1.6 %copy-start.2 = (bf16[2,2,512,512]{3,2,1,0:T(8,128)(2,1)S(1)}, bf16[2,2,512,512]{3,2,1,0:T(8,128)(2,1)}, u32[]{:S(2)}) copy-start(bf16[2,2,512,512]{3,2,1,0:T(8,128)(2,1)} %pad_maximum_fusion.refs_3_.synth_ref.refs_4_) | copy-start | bytes 6291460
  64.4 10.3 %copy-start.3 = (bf16[2,2,512,256]{3,2,1,0:T(8,128)(2,1)S(1)}, bf16[2,2,512,256]{3,2,1,0:T(8,128)(2,1)}, u32[]{:S(2)}) copy-start(bf16[2,2,512,256]{3,2,1,0:T(8,128)(2,1)} %get-tuple-element.35.other_ref) | copy-start | bytes 3145732
  78.0 30.9 %collective-permute-start.12 = (f32[200,256]{1,0:T(8,128)S(1)}, f32[200,256]{1,0:T(8,128)S(1)}, u32[]{:S(2)}, u32[]{:S(2)}) collective-permute-start(f32[200,256]{1,0:T(8,128)S(1)} %get-tuple-element.29), channel_id=1, source_target_pairs={{0,1},{1,0},{2,3},{3,2},{4,5},{5,4},{6,7},{7,6},{8,9},{9,8},{10,11... | collective-permute-start | bytes 614408 | tf_op jit(solution)/shard_map/ppermute | solution.py:390
  81.2 28.8 %collective-permute-start.11 = (f32[200,128]{1,0:T(8,128)S(1)}, f32[200,128]{1,0:T(8,128)S(1)}, u32[]{:S(2)}, u32[]{:S(2)}) collective-permute-start(f32[200,128]{1,0:T(8,128)S(1)} %get-tuple-element.28), channel_id=1, source_target_pairs={{0,1},{1,0},{2,3},{3,2},{4,5},{5,4},{6,7},{7,6},{8,9},{9,8},{10,11... | collective-permute-start | bytes 307208 | tf_op jit(solution)/shard_map/ppermute | solution.py:390
  92.3 18.7 %collective-permute-start.10 = (f32[200,128]{1,0:T(8,128)S(1)}, f32[200,128]{1,0:T(8,128)S(1)}, u32[]{:S(2)}, u32[]{:S(2)}) collective-permute-start(f32[200,128]{1,0:T(8,128)S(1)} %get-tuple-element.27), channel_id=1, source_target_pairs={{0,1},{1,0},{2,3},{3,2},{4,5},{5,4},{6,7},{7,6},{8,9},{9,8},{10,11... | collective-permute-start | bytes 307208 | tf_op jit(solution)/shard_map/ppermute | solution.py:390

commit v7 on v5

--- a/solution.py
+++ b/solution.py
@@ -100,14 +100,15 @@
     return jnp.dot(a, b, preferred_element_type=f32)
 
 
-def first_kernel(at_ref, vel_ref, weight_ref, energy_ref, rest_ref, point_ref):
+def first_kernel(at_ref, *refs):
+    *vel_refs, weight_ref, energy_ref, rest_ref, point_ref = refs
     step = pl.program_id(0)
-    comps, _, width = vel_ref.shape
+    width = weight_ref.shape[1]
     weight = weight_ref[...]
     acc = None
     for lane in range(0, width, LANES):
-        for comp in range(comps):
-            x = vel_ref[comp, :, lane : lane + LANES]
+        for vel_ref in vel_refs:
+            x = vel_ref[0, :, lane : lane + LANES]
             term = x * x * weight[:, lane : lane + LANES]
             acc = term if acc is None else acc + term
     point_ref[...] = acc
@@ -129,11 +130,11 @@
 
     @pl.when(step > 0)
     def _():
-        rest_ref[pl.ds(pl.multiple_of((step - 1) * TILE, SUB), TILE), :] = vel_ref[comps - 1]
+        rest_ref[pl.ds(pl.multiple_of((step - 1) * TILE, SUB), TILE), :] = vel_refs[-1][0]
 
     @pl.when(step == at_ref[0])
     def _():
-        rest_ref[rest_ref.shape[0] - TILE :, :] = vel_ref[comps - 2]
+        rest_ref[rest_ref.shape[0] - TILE :, :] = vel_refs[-2][0]
 
 
 def first_pass(velocity, weight, there, lend):
@@ -146,7 +147,7 @@
             num_scalar_prefetch=1,
             grid=(points // TILE,),
             in_specs=[
-                pl.BlockSpec((comps, TILE, width), lambda t, at: (0, t, 0)),
+                *[pl.BlockSpec((1, TILE, width), lambda t, at, c=c: (c, t, 0)) for c in range(comps)],
                 pl.BlockSpec((1, width), lambda t, at: (0, 0)),
             ],
             out_specs=[
@@ -158,7 +159,7 @@
         out_shape=[jax.ShapeDtypeStruct(shape, f32), jax.ShapeDtypeStruct((rest, width), f32)],
         compiler_params=pltpu.CompilerParams(vmem_limit_bytes=16 << 20),
         name="first_pass",
-    )(there, velocity, weight)
+    )(there, *[velocity] * comps, weight)
 
 
 def expand_kernel(inv_ref, spread_ref, out_ref):
@@ -299,7 +300,7 @@
         out_shape=out_shape,
         scratch_shapes=[pltpu.VMEM((tiles, TILE, LANES), f32)] * 2,
         input_output_aliases=aliases,
-        compiler_params=pltpu.CompilerParams(vmem_limit_bytes=20 << 20),
+        compiler_params=pltpu.CompilerParams(vmem_limit_bytes=14 << 20),
         cost_estimate=pl.CostEstimate(
             flops=3 * rows * coefs * (coefs + width), bytes_accessed=8 * rows * width, transcendentals=0
         ),
@@ -342,7 +343,7 @@
             out_specs=[pl.BlockSpec(shape, lambda t, at: (0, 0)) for shape in shapes],
         ),
         out_shape=[jax.ShapeDtypeStruct(shape, f32) for shape in shapes],
-        compiler_params=pltpu.CompilerParams(vmem_limit_bytes=20 << 20),
+        compiler_params=pltpu.CompilerParams(vmem_limit_bytes=14 << 20),
         name="both_groups",
     )(at, velocity, far, wphys, synth, derive, other)
 

time: 112 us -> 112 us (level)
    unnamed x24 -> x28, local copies, waits for them, and re-layouts: 6.41 us -> 6.41 us
where the time goes in v7:
time: 112 us
  Pallas kernels  49 us (44%)
  starting transfers between devices  27 us (24%)
  local copies, waits for them, and re-layouts  17.3 us (15%)
  between operations  7.95 us (7%)
  waiting for transfers between devices  6.64 us (6%)
  other arithmetic  3.78 us (3%)
    pallas_call x5, Pallas kernels, advance(): pl.pallas_call(lambda *refs: chunk_kernel(len(far), is_w, len(aliases), *...  35 us
    ppermute x10, starting transfers between devices, exchange(): lax.ppermute(block, 'mode', [(i, (i + s) % count) for i in range(count)])  12 us
    ppermute x4, starting transfers between devices, sum_over_plane(): lax.ppermute(value, 'plane', [(i, i ^ step) for i in range(count)])  11.1 us
    unnamed x28, local copies, waits for them, and re-layouts  6.41 us
    ppermute x10, waiting for transfers between devices, exchange(): lax.ppermute(block, 'mode', [(i, (i + s) % count) for i in range(count)])  5.57 us
    pallas_call x4, Pallas kernels, finish(): pl.pallas_call(finish_kernel, grid_spec=pltpu.PrefetchScalarGridSpec(num_...  4.87 us
    pallas_call x1, Pallas kernels, expand(): pl.pallas_call(expand_kernel, out_shape=jax.ShapeDtypeStruct((width // LA...  3.48 us
    pallas_call x1, Pallas kernels, both_groups(): pl.pallas_call(both_kernel, grid_spec=pltpu.PrefetchScalarGridSpec(num_sc...  3.42 us
  transfers between devices with their start and end apart: 16, of which 6 were waited for; matrix products, arithmetic and copies ran while one was open for 12% of the time, Pallas kernels for 43%

profile of v7, /device:TPU:0, one launch (start us, length us, event | category | flops | bytes accessed | tf_op | source)
XLA Modules:
  0.0 111.6 jit_solution(4950455279312974461)
XLA Ops:
  0.6 0.9 slice_bitcast_fusion.4
  1.6 3.0 %collective-permute-start.2 = (f32[80,512]{1,0:T(8,128)S(1)}, f32[80,512]{1,0:T(8,128)}, u32[]{:S(2)}, u32[]{:S(2)}) collective-permute-start(f32[80,512]{1,0:T(8,128)S(1)} %slice_bitcast_fusion.4), channel_id=1, source_target_pairs={{0,1},{1,0},{2,3},{3,2},{4,5},{5,4},{6,7},{7,6},{8,9},{9,8},{10,11... | collective-permute-start | bytes 491528 | tf_op jit(solution)/shard_map/ppermute | solution.py:391
  4.6 1.0 slice_bitcast_fusion.3
  5.6 0.1 collective-permute-start.3
  5.7 0.0 copy-start
  5.7 2.4 %copy-done = f32[3,800,512]{2,1,0:T(8,128)S(1)} copy-done((f32[3,800,512]{2,1,0:T(8,128)S(1)}, f32[3,800,512]{2,1,0:T(8,128)}, u32[]{:S(2)}) %copy-start) | copy-done | bytes 4915224
  8.1 2.3 %first_pass.1 = (f32[2,8,128]{2,1,0:T(8,128)S(1)}, f32[800,512]{1,0:T(8,128)}) custom-call(s32[1]{0:T(128)} %bitcast.at_ref, f32[3,800,512]{2,1,0:T(8,128)S(1)} %copy-done, f32[3,800,512]{2,1,0:T(8,128)S(1)} %copy-done, f32[3,800,512]{2,1,0:T(8,128)S(1)} %copy-done, f32[1,512]{1,0:T(1,128)S(1)} %compare_select_fusion.refs_3_), custom_call_target="tpu_custom_call" | custom-call | tf_op jit(solution)/shard_map/first_pass/pallas_call | solution.py:144
  10.4 2.0 %collective-permute-start.1 = (f32[2,8,128]{2,1,0:T(8,128)S(1)}, f32[2,8,128]{2,1,0:T(8,128)S(1)}, u32[]{:S(2)}, u32[]{:S(2)}) collective-permute-start(f32[2,8,128]{2,1,0:T(8,128)S(1)} %get-tuple-element.19), channel_id=1, source_target_pairs={{0,1},{1,0},{2,3},{3,2},{4,5},{5,4},{6,7},{7,6},{8,9},{9,8},{10,11... | collective-permute-start | bytes 24584 | tf_op jit(solution)/shard_map/ppermute | solution.py:391
  12.4 0.1 collective-permute-start
  12.4 2.9 %slice_bitcast_fusion = f32[800,512]{1,0:T(8,128)} fusion(f32[3,800,512]{2,1,0:T(8,128)} %own_ref.4), kind=kLoop, calls=%fused_computation.1 | loop fusion | bytes 3276800 | tf_op jit(solution)/shard_map/squeeze | solution.py:433
  15.3 1.8 %collective-permute-start.15 = (f32[800,512]{1,0:T(8,128)}, f32[800,512]{1,0:T(8,128)}, u32[]{:S(2)}, u32[]{:S(2)}) collective-permute-start(f32[800,512]{1,0:T(8,128)} %slice_bitcast_fusion), channel_id=1, source_target_pairs={{0,1},{1,0},{2,3},{3,2},{4,5},{5,4},{6,7},{7,6},{8,9},{9,8},{10,11... | collective-permute-start | bytes 4915208 | tf_op jit(solution)/shard_map/ppermute | solution.py:391
  17.2 0.6 fusion.8
  20.4 2.1 %slice_bitcast_fusion.1 = (f32[200,512]{1,0:T(8,128)}, f32[200,512]{1,0:T(8,128)}) fusion(f32[3,800,512]{2,1,0:T(8,128)} %own_ref.4), kind=kLoop, calls=%fused_computation.11 | loop fusion | bytes 1638400 | tf_op jit(solution)/shard_map/squeeze | solution.py:436
  23.8 0.1 add_select_fusion
  23.9 0.2 dynamic-slice_bitcast_fusion.5
  24.1 0.2 maximum_bitcast_fusion
  24.2 1.5 %pad_maximum_fusion.refs_3_.synth_ref.refs_4_ = bf16[2,2,512,512]{3,2,1,0:T(8,128)(2,1)} fusion(bf16[1,2,512,512]{3,2,1,0:T(8,128)(2,1)S(1)} %get-tuple-element.45, bf16[1,2,512,512]{3,2,1,0:T(8,128)(2,1)S(1)} %get-tuple-element.44), kind=kLoop, calls=%fused_computation | loop fusion | flops 1048576 | bytes 4194304 | tf_op jit(solution)/shard_map/stack | solution.py:475
  25.8 2.7 %dynamic-slice_bitcast_fusion = (bf16[2,2,512,256]{3,2,1,0:T(8,128)(2,1)}, bf16[2,2,512,256]{3,2,1,0:T(8,128)(2,1)S(1)}) fusion(bf16[2,2,2,512,256]{4,3,2,1,0:T(8,128)(2,1)} %constant.80.clone, s32[]{:T(128)S(6)} %select_n.47, s32[]{:T(128)S(6)} %select_n.46), kind=kLoop, calls=%fused_computation.4 | loop fusion | bytes 4194312 | tf_op jit(solution)/shard_map/jit(dynamic_index_in_dim)/squeeze | solution.py:472
  28.5 3.5 %expand.1.refs_5_.inv_ref.refs_6_ = f32[4,25,25,128]{3,2,1,0:T(8,128)S(1)} custom-call(f32[25,25,256]{2,1,0:T(8,128)S(1)} %bitcast.35, bf16[256,512]{1,0:T(8,128)(2,1)S(1)} %copy-done.5), custom_call_target="tpu_custom_call" | custom-call | tf_op jit(solution)/shard_map/expand/pallas_call | solution.py:179
  32.0 0.0 collective-permute-done.2
  32.0 0.2 collective-permute-start.14
  32.2 0.0 collective-permute-done.3
  32.2 1.1 pad_maximum_fusion.1.refs_1_
  33.3 0.0 collective-permute-done.1
  33.3 0.6 slice_reduce_fusion
  33.9 0.1 copy.22
  34.0 0.1 reshape.101
  34.1 2.4 %collective-permute-start.8 = (f32[32]{0:T(128)S(1)}, f32[32]{0:T(128)S(1)}, u32[]{:S(2)}, u32[]{:S(2)}) collective-permute-start(f32[32]{0:T(128)S(1)} %multiply_multiply_fusion), channel_id=1, source_target_pairs={{0,2},{2,4},{4,6},{6,8},{8,10},{10,12},{12,14},{14,16},{16,18},{18... | collective-permute-start | bytes 392 | tf_op jit(solution)/shard_map/ppermute | solution.py:454
  37.8 3.3 %collective-permute-start.5 = (f32[]{:T(128)}, f32[]{:T(128)}, u32[]{:S(2)}, u32[]{:S(2)}) collective-permute-start(f32[]{:T(128)} %add.91), channel_id=1, source_target_pairs={{0,4},{2,6},{4,0},{6,2},{8,12},{10,14},{12,8},{14,10},{16,20},{18,... | collective-permute-start | bytes 20 | tf_op jit(solution)/shard_map/ppermute | solution.py:402
  41.1 0.4 collective-permute-done.5
  42.2 3.4 %collective-permute-start.6 = (f32[]{:T(128)}, f32[]{:T(128)}, u32[]{:S(2)}, u32[]{:S(2)}) collective-permute-start(f32[]{:T(128)} %add.92), channel_id=1, source_target_pairs={{0,8},{2,10},{4,12},{6,14},{8,0},{10,2},{12,4},{14,6},{16,24},{18,... | collective-permute-start | bytes 20 | tf_op jit(solution)/shard_map/ppermute | solution.py:402
  45.5 0.3 collective-permute-done.6
  46.5 4.4 %collective-permute-start.7 = (f32[]{:T(128)}, f32[]{:T(128)}, u32[]{:S(2)}, u32[]{:S(2)}) collective-permute-start(f32[]{:T(128)} %add.93), channel_id=1, source_target_pairs={{0,16},{2,18},{4,20},{6,22},{8,24},{10,26},{12,28},{14,30},{16,0},... | collective-permute-start | bytes 20 | tf_op jit(solution)/shard_map/ppermute | solution.py:402
  50.9 0.3 collective-permute-done.7
  51.2 1.5 %collective-permute-start.9 = (f32[32]{0:T(128)S(1)}, f32[32]{0:T(128)S(1)}, u32[]{:S(2)}, u32[]{:S(2)}) collective-permute-start(f32[32]{0:T(128)S(1)} %multiply_multiply_fusion), channel_id=1, source_target_pairs={{2,0},{4,2},{6,4},{8,6},{10,8},{12,10},{14,12},{16,14},{18,16},{20... | collective-permute-start | bytes 392 | tf_op jit(solution)/shard_map/ppermute | solution.py:455
  53.4 1.8 %collective-permute-start.13 = (f32[200,512]{1,0:T(8,128)}, f32[200,512]{1,0:T(8,128)}, u32[]{:S(2)}, u32[]{:S(2)}) collective-permute-start(f32[200,512]{1,0:T(8,128)} %get-tuple-element.33), channel_id=1, source_target_pairs={{0,1},{1,0},{2,3},{3,2},{4,5},{5,4},{6,7},{7,6},{8,9},{9,8},{10,11... | collective-permute-start | bytes 1228808 | tf_op jit(solution)/shard_map/ppermute | solution.py:391
  55.1 0.0 collective-permute-done.9
  55.2 0.1 maximum_multiply_fusion
  55.2 0.2 select_reduce_fusion
  55.4 0.0 copy-start.8
  55.5 0.1 broadcast_multiply_fusion
  55.5 0.1 mul.94
  55.6 0.2 broadcast_in_dim.45.refs_2_.damp_ref.refs_3_
  55.8 0.0 copy-start.1
  55.8 2.4 %copy-done.1 = f32[3,800,512]{2,1,0:T(8,128)S(1)} copy-done((f32[3,800,512]{2,1,0:T(8,128)S(1)}, f32[3,800,512]{2,1,0:T(8,128)}, u32[]{:S(2)}) %copy-start.1) | copy-done | bytes 4915224
  58.2 1.6 %copy-done.2 = bf16[2,2,512,512]{3,2,1,0:T(8,128)(2,1)S(1)} copy-done((bf16[2,2,512,512]{3,2,1,0:T(8,128)(2,1)S(1)}, bf16[2,2,512,512]{3,2,1,0:T(8,128)(2,1)}, u32[]{:S(2)}) %copy-start.2) | copy-done | bytes 2097176
  59.8 3.6 %advance_2_0.1 = (f32[3,800,512]{2,1,0:T(8,128)}, f32[800,1024]{1,0:T(8,128)S(1)}) custom-call(f32[3,800,512]{2,1,0:T(8,128)S(1)} %copy-done.1, f32[200,512]{1,0:T(8,128)S(1)} %pad_maximum_fusion.1.refs_1_, f32[800,128]{1,0:T(8,128)S(1)} %broadcast_in_dim.45.refs_2_.damp_ref.refs_3_, bf16[2,2,512,512]{3,2,1,0:T(8,128)(2,1)S(1)} %copy-done.2, ...), custom_call_target="tpu_custom_call" | custom-call | flops 943718400 | bytes 819200 | tf_op jit(solution)/shard_map/advance_2_0/pallas_call | solution.py:295
  63.4 0.0 collective-permute-done.refs_1_.far_ref
  63.4 10.3 %advance_2_200.1 = (f32[3,800,512]{2,1,0:T(8,128)}, f32[800,1024]{1,0:T(8,128)S(1)}) custom-call(f32[3,800,512]{2,1,0:T(8,128)S(1)} %copy-done.1, f32[800,512]{1,0:T(8,128)} %collective-permute-done.refs_1_.far_ref, f32[800,128]{1,0:T(8,128)S(1)} %broadcast_in_dim.45.refs_2_.damp_ref.refs_3_, ...), custom_call_target="tpu_custom_call", output_to_operand_aliasing={{0}: (6, {}), {1}: (7, {})} | custom-call | flops 2831155200 | bytes 2457600 | tf_op jit(solution)/shard_map/advance_2_200/pallas_call | solution.py:295
  73.7 3.4 %both_groups.1 = (f32[200,512]{1,0:T(8,128)S(1)}, f32[200,256]{1,0:T(8,128)S(1)}, f32[200,128]{1,0:T(8,128)S(1)}, f32[200,128]{1,0:T(8,128)S(1)}) custom-call(s32[1]{0:T(128)} %bitcast.3.at_ref, f32[3,800,512]{2,1,0:T(8,128)S(1)} %copy-done.1, f32[800,512]{1,0:T(8,128)} %collective-permute-done.refs_1_.far_ref, ...), custom_call_target="tpu_custom_call" | custom-call | tf_op jit(solution)/shard_map/both_groups/pallas_call | solution.py:330
  77.1 0.8 collective-permute-start.12
  78.0 1.2 %collective-permute-start.11 = (f32[200,128]{1,0:T(8,128)S(1)}, f32[200,128]{1,0:T(8,128)S(1)}, u32[]{:S(2)}, u32[]{:S(2)}) collective-permute-start(f32[200,128]{1,0:T(8,128)S(1)} %get-tuple-element.28), channel_id=1, source_target_pairs={{0,1},{1,0},{2,3},{3,2},{4,5},{5,4},{6,7},{7,6},{8,9},{9,8},{10,11... | collective-permute-start | bytes 307208 | tf_op jit(solution)/shard_map/ppermute | solution.py:391
  79.2 2.0 %finish_here.1.refs_7_ = f32[3,800,512]{2,1,0:T(8,128)} custom-call(s32[1]{0:T(128)} %bitcast.3.at_ref, f32[3,800,512]{2,1,0:T(8,128)S(1)} %bitcast.34, f32[200,512]{1,0:T(8,128)S(1)} %get-tuple-element.30.span_ref, f32[800,128]{1,0:T(8,128)S(1)} %broadcast_in_dim.45.refs_2_.damp_ref.refs_3_, ...), custom_call_target="tpu_custom_call", output_to_operand_aliasing={{}: (5, {})} | custom-call | tf_op jit(solution)/shard_map/finish_here/pallas_call | solution.py:367
  81.2 5.3 %collective-permute-done.15.refs_1_ = f32[800,512]{1,0:T(8,128)} collective-permute-done((f32[800,512]{1,0:T(8,128)}, f32[800,512]{1,0:T(8,128)}, u32[]{:S(2)}, u32[]{:S(2)}) %collective-permute-start.15) | collective-permute-done | bytes 1638432 | tf_op jit(solution)/shard_map/ppermute | solution.py:391
  86.5 0.9 collective-permute-start.10
  87.5 13.0 %advance_0_0.1.refs_7_ = f32[3,800,512]{2,1,0:T(8,128)} custom-call(f32[3,800,512]{2,1,0:T(8,128)S(1)} %bitcast.34, f32[800,512]{1,0:T(8,128)} %collective-permute-done.15.refs_1_, f32[800,1024]{1,0:T(8,128)S(1)} %get-tuple-element.26.wphys_ref.refs_2_, f32[800,128]{1,0:T(8,128)S(1)} %broadcast_in_dim.45.refs_2_.damp_ref.refs_3_, ...), custom_call_target="tpu_custom_call", output_to_operand_aliasing={{}: (7, {})} | custom-call | flops 3774873600 | bytes 3276800 | tf_op jit(solution)/shard_map/advance_0_0/pallas_call | solution.py:295
  100.4 0.0 collective-permute-done.14.refs_1_
  100.4 3.5 %advance_1_0.1.refs_7_ = f32[3,800,512]{2,1,0:T(8,128)} custom-call(f32[3,800,512]{2,1,0:T(8,128)S(1)} %bitcast.34, f32[200,512]{1,0:T(8,128)S(1)} %collective-permute-done.14.refs_1_, f32[800,1024]{1,0:T(8,128)S(1)} %get-tuple-element.26.wphys_ref.refs_2_, f32[800,128]{1,0:T(8,128)S(1)} %broadcast_in_dim.45.refs_2_.damp_ref.refs_3_, ...), custom_call_target="tpu_custom_call", output_to_operand_aliasing={{}: (7, {})} | custom-call | flops 943718400 | bytes 819200 | tf_op jit(solution)/shard_map/advance_1_0/pallas_call | solution.py:295
  104.0 0.1 collective-permute-done.13.refs_1_
  104.1 4.5 %advance_1_200.1.held_ref = f32[3,800,512]{2,1,0:T(8,128)} custom-call(f32[3,800,512]{2,1,0:T(8,128)S(1)} %bitcast.34, f32[200,512]{1,0:T(8,128)} %collective-permute-done.13.refs_1_, f32[800,1024]{1,0:T(8,128)S(1)} %get-tuple-element.26.wphys_ref.refs_2_, f32[800,128]{1,0:T(8,128)S(1)} %broadcast_in_dim.45.refs_2_.damp_ref.refs_3_, ...), custom_call_target="tpu_custom_call", output_to_operand_aliasing={{}: (7, {})} | custom-call | flops 943718400 | bytes 819200 | tf_op jit(solution)/shard_map/advance_1_200/pallas_call | solution.py:295
  108.6 1.1 %finish_there_0.1.held_ref = f32[3,800,512]{2,1,0:T(8,128)} custom-call(s32[1]{0:T(128)} %bitcast.at_ref, f32[3,800,512]{2,1,0:T(8,128)S(1)} %bitcast.34, f32[200,256]{1,0:T(8,128)S(1)} %collective-permute-done.12.span_ref, f32[800,128]{1,0:T(8,128)S(1)} %broadcast_in_dim.45.refs_2_.damp_ref.refs_3_, ...), custom_call_target="tpu_custom_call", output_to_operand_aliasing={{}: (5, {})} | custom-call | tf_op jit(solution)/shard_map/finish_there_0/pallas_call | solution.py:367
  109.8 0.9 finish_there_2.1.held_ref
  110.6 0.2 collective-permute-done.10.span_ref
  110.8 0.9 finish_there_3.1
  (34 shorter events, 0.1 us)
Async XLA Ops:
  1.6 30.4 %collective-permute-start.2 = (f32[80,512]{1,0:T(8,128)S(1)}, f32[80,512]{1,0:T(8,128)}, u32[]{:S(2)}, u32[]{:S(2)}) collective-permute-start(f32[80,512]{1,0:T(8,128)S(1)} %slice_bitcast_fusion.4), channel_id=1, source_target_pairs={{0,1},{1,0},{2,3},{3,2},{4,5},{5,4},{6,7},{7,6},{8,9},{9,8},{10,11... | collective-permute-start | bytes 491528 | tf_op jit(solution)/shard_map/ppermute | solution.py:391
  5.6 26.7 %collective-permute-start.3 = (f32[120,512]{1,0:T(8,128)S(1)}, f32[120,512]{1,0:T(8,128)}, u32[]{:S(2)}, u32[]{:S(2)}) collective-permute-start(f32[120,512]{1,0:T(8,128)S(1)} %slice_bitcast_fusion.3), channel_id=1, source_target_pairs={{0,1},{1,0},{2,3},{3,2},{4,5},{5,4},{6,7},{7,6},{8,9},{9,8},{10,11... | collective-permute-start | bytes 737288 | tf_op jit(solution)/shard_map/ppermute | solution.py:391
  5.7 2.4 %copy-start = (f32[3,800,512]{2,1,0:T(8,128)S(1)}, f32[3,800,512]{2,1,0:T(8,128)}, u32[]{:S(2)}) copy-start(f32[3,800,512]{2,1,0:T(8,128)} %own_ref.4) | copy-start | bytes 14745604
  10.4 22.9 %collective-permute-start.1 = (f32[2,8,128]{2,1,0:T(8,128)S(1)}, f32[2,8,128]{2,1,0:T(8,128)S(1)}, u32[]{:S(2)}, u32[]{:S(2)}) collective-permute-start(f32[2,8,128]{2,1,0:T(8,128)S(1)} %get-tuple-element.19), channel_id=1, source_target_pairs={{0,1},{1,0},{2,3},{3,2},{4,5},{5,4},{6,7},{7,6},{8,9},{9,8},{10,11... | collective-permute-start | bytes 24584 | tf_op jit(solution)/shard_map/ppermute | solution.py:391
  12.4 11.4 %copy-start.7 = (s32[32,4]{0,1:T(4,128)S(1)}, s32[32,4]{0,1:T(4,128)}, u32[]{:S(2)}) copy-start(s32[32,4]{0,1:T(4,128)} %param.11) | copy-start | bytes 1540
  12.4 11.4 %copy-start.10 = (s32[4]{0:T(128)S(1)}, s32[4]{0:T(128)}, u32[]{:S(2)}) copy-start(s32[4]{0:T(128)} %constant.77.clone) | copy-start | bytes 52
  12.4 11.5 %copy-start.6 = (bf16[2,2,2,256,512]{4,3,2,1,0:T(8,128)(2,1)S(1)}, bf16[2,2,2,256,512]{4,3,2,1,0:T(8,128)(2,1)}, u32[]{:S(2)}) copy-start(bf16[2,2,2,256,512]{4,3,2,1,0:T(8,128)(2,1)} %constant.79.clone) | copy-start | bytes 6291460
  12.4 51.0 %collective-permute-start = (f32[800,512]{1,0:T(8,128)}, f32[800,512]{1,0:T(8,128)}, u32[]{:S(2)}, u32[]{:S(2)}) collective-permute-start(f32[800,512]{1,0:T(8,128)} %get-tuple-element.21), channel_id=1, source_target_pairs={{0,1},{1,0},{2,3},{3,2},{4,5},{5,4},{6,7},{7,6},{8,9},{9,8},{10,11... | collective-permute-start | bytes 4915208 | tf_op jit(solution)/shard_map/ppermute | solution.py:391
  15.3 71.2 %collective-permute-start.15 = (f32[800,512]{1,0:T(8,128)}, f32[800,512]{1,0:T(8,128)}, u32[]{:S(2)}, u32[]{:S(2)}) collective-permute-start(f32[800,512]{1,0:T(8,128)} %slice_bitcast_fusion), channel_id=1, source_target_pairs={{0,1},{1,0},{2,3},{3,2},{4,5},{5,4},{6,7},{7,6},{8,9},{9,8},{10,11... | collective-permute-start | bytes 4915208 | tf_op jit(solution)/shard_map/ppermute | solution.py:391
  25.7 2.8 %copy-start.4 = (f32[256,25,25]{0,2,1:T(8,128)S(1)}, f32[256,25,25]{0,2,1:T(8,128)}, u32[]{:S(2)}) copy-start(f32[256,25,25]{0,2,1:T(8,128)} %param.10) | copy-start | bytes 1920004
  25.7 2.8 %copy-start.5 = (bf16[256,512]{1,0:T(8,128)(2,1)S(1)}, bf16[256,512]{1,0:T(8,128)(2,1)}, u32[]{:S(2)}) copy-start(bf16[256,512]{1,0:T(8,128)(2,1)} %constant.81.clone.spread_ref) | copy-start | bytes 786436
  28.5 5.6 %copy-start.11 = (s32[32]{0:T(128)S(1)}, s32[32]{0:T(128)}, u32[]{:S(2)}) copy-start(s32[32]{0:T(128)} %param.12) | copy-start | bytes 388
  28.5 26.9 %copy-start.9 = (f32[25]{0:T(128)S(1)}, f32[25]{0:T(128)}, u32[]{:S(2)}) copy-start(f32[25]{0:T(128)} %constant.82) | copy-start | bytes 304
  32.0 68.4 %collective-permute-start.14 = (f32[200,512]{1,0:T(8,128)}, f32[200,512]{1,0:T(8,128)S(1)}, u32[]{:S(2)}, u32[]{:S(2)}) collective-permute-start(f32[200,512]{1,0:T(8,128)} %get-tuple-element.32), channel_id=1, source_target_pairs={{0,1},{1,0},{2,3},{3,2},{4,5},{5,4},{6,7},{7,6},{8,9},{9,8},{10,11... | collective-permute-start | bytes 1228808 | tf_op jit(solution)/shard_map/ppermute | solution.py:391
  33.9 2.6 %collective-permute-start.4 = (f32[]{:T(128)}, f32[]{:T(128)}, u32[]{:S(2)}, u32[]{:S(2)}) collective-permute-start(f32[]{:T(128)} %get-tuple-element.40), channel_id=1, source_target_pairs={{0,2},{2,0},{4,6},{6,4},{8,10},{10,8},{12,14},{14,12},{16,18},{18,... | collective-permute-start | bytes 20 | tf_op jit(solution)/shard_map/ppermute | solution.py:402
  34.1 19.3 %collective-permute-start.8 = (f32[32]{0:T(128)S(1)}, f32[32]{0:T(128)S(1)}, u32[]{:S(2)}, u32[]{:S(2)}) collective-permute-start(f32[32]{0:T(128)S(1)} %multiply_multiply_fusion), channel_id=1, source_target_pairs={{0,2},{2,4},{4,6},{6,8},{8,10},{10,12},{12,14},{14,16},{16,18},{18... | collective-permute-start | bytes 392 | tf_op jit(solution)/shard_map/ppermute | solution.py:454
  37.8 3.7 %collective-permute-start.5 = (f32[]{:T(128)}, f32[]{:T(128)}, u32[]{:S(2)}, u32[]{:S(2)}) collective-permute-start(f32[]{:T(128)} %add.91), channel_id=1, source_target_pairs={{0,4},{2,6},{4,0},{6,2},{8,12},{10,14},{12,8},{14,10},{16,20},{18,... | collective-permute-start | bytes 20 | tf_op jit(solution)/shard_map/ppermute | solution.py:402
  42.2 3.7 %collective-permute-start.6 = (f32[]{:T(128)}, f32[]{:T(128)}, u32[]{:S(2)}, u32[]{:S(2)}) collective-permute-start(f32[]{:T(128)} %add.92), channel_id=1, source_target_pairs={{0,8},{2,10},{4,12},{6,14},{8,0},{10,2},{12,4},{14,6},{16,24},{18,... | collective-permute-start | bytes 20 | tf_op jit(solution)/shard_map/ppermute | solution.py:402
  46.5 4.7 %collective-permute-start.7 = (f32[]{:T(128)}, f32[]{:T(128)}, u32[]{:S(2)}, u32[]{:S(2)}) collective-permute-start(f32[]{:T(128)} %add.93), channel_id=1, source_target_pairs={{0,16},{2,18},{4,20},{6,22},{8,24},{10,26},{12,28},{14,30},{16,0},... | collective-permute-start | bytes 20 | tf_op jit(solution)/shard_map/ppermute | solution.py:402
  51.2 3.9 %collective-permute-start.9 = (f32[32]{0:T(128)S(1)}, f32[32]{0:T(128)S(1)}, u32[]{:S(2)}, u32[]{:S(2)}) collective-permute-start(f32[32]{0:T(128)S(1)} %multiply_multiply_fusion), channel_id=1, source_target_pairs={{2,0},{4,2},{6,4},{8,6},{10,8},{12,10},{14,12},{16,14},{18,16},{20... | collective-permute-start | bytes 392 | tf_op jit(solution)/shard_map/ppermute | solution.py:455
  53.4 50.7 %collective-permute-start.13 = (f32[200,512]{1,0:T(8,128)}, f32[200,512]{1,0:T(8,128)}, u32[]{:S(2)}, u32[]{:S(2)}) collective-permute-start(f32[200,512]{1,0:T(8,128)} %get-tuple-element.33), channel_id=1, source_target_pairs={{0,1},{1,0},{2,3},{3,2},{4,5},{5,4},{6,7},{7,6},{8,9},{9,8},{10,11... | collective-permute-start | bytes 1228808 | tf_op jit(solution)/shard_map/ppermute | solution.py:391
  55.4 7.9 %copy-start.8 = (f32[32]{0:T(128)}, f32[32]{0:T(128)S(1)}, u32[]{:S(2)}) copy-start(f32[32]{0:T(128)S(1)} %add_multiply_fusion.1) | copy-start | bytes 388
  55.8 2.4 %copy-start.1 = (f32[3,800,512]{2,1,0:T(8,128)S(1)}, f32[3,800,512]{2,1,0:T(8,128)}, u32[]{:S(2)}) copy-start(f32[3,800,512]{2,1,0:T(8,128)} %own_ref.4) | copy-start | bytes 14745604
  58.2 1.6 %copy-start.2 = (bf16[2,2,512,512]{3,2,1,0:T(8,128)(2,1)S(1)}, bf16[2,2,512,512]{3,2,1,0:T(8,128)(2,1)}, u32[]{:S(2)}) copy-start(bf16[2,2,512,512]{3,2,1,0:T(8,128)(2,1)} %pad_maximum_fusion.refs_3_.synth_ref.refs_4_) | copy-start | bytes 6291460
  63.4 10.3 %copy-start.3 = (bf16[2,2,512,256]{3,2,1,0:T(8,128)(2,1)S(1)}, bf16[2,2,512,256]{3,2,1,0:T(8,128)(2,1)}, u32[]{:S(2)}) copy-start(bf16[2,2,512,256]{3,2,1,0:T(8,128)(2,1)} %get-tuple-element.34.other_ref) | copy-start | bytes 3145732
  73.7 5.5 %slice-start = ((s8[4915200]{0:T(1024)(128)(4,1)}), s8[4194304]{0:T(1024)(128)(4,1)S(1)}, s32[]{:S(2)}) async-start(s8[4915200]{0:T(1024)(128)(4,1)} %bitcast.33), calls=%async_computation | async-start | bytes 8388608
  73.7 5.5 %slice-start.1 = ((s8[4915200]{0:T(1024)(128)(4,1)}), s8[720896]{0:T(1024)(128)(4,1)S(1)}, s32[]{:S(2)}) async-start(s8[4915200]{0:T(1024)(128)(4,1)} %bitcast.33), calls=%async_computation.1 | async-start | bytes 1441792
  77.1 31.5 %collective-permute-start.12 = (f32[200,256]{1,0:T(8,128)S(1)}, f32[200,256]{1,0:T(8,128)S(1)}, u32[]{:S(2)}, u32[]{:S(2)}) collective-permute-start(f32[200,256]{1,0:T(8,128)S(1)} %get-tuple-element.29), channel_id=1, source_target_pairs={{0,1},{1,0},{2,3},{3,2},{4,5},{5,4},{6,7},{7,6},{8,9},{9,8},{10,11... | collective-permute-start | bytes 614408 | tf_op jit(solution)/shard_map/ppermute | solution.py:391
  78.0 31.8 %collective-permute-start.11 = (f32[200,128]{1,0:T(8,128)S(1)}, f32[200,128]{1,0:T(8,128)S(1)}, u32[]{:S(2)}, u32[]{:S(2)}) collective-permute-start(f32[200,128]{1,0:T(8,128)S(1)} %get-tuple-element.28), channel_id=1, source_target_pairs={{0,1},{1,0},{2,3},{3,2},{4,5},{5,4},{6,7},{7,6},{8,9},{9,8},{10,11... | collective-permute-start | bytes 307208 | tf_op jit(solution)/shard_map/ppermute | solution.py:391
  86.5 24.3 %collective-permute-start.10 = (f32[200,128]{1,0:T(8,128)S(1)}, f32[200,128]{1,0:T(8,128)S(1)}, u32[]{:S(2)}, u32[]{:S(2)}) collective-permute-start(f32[200,128]{1,0:T(8,128)S(1)} %get-tuple-element.27), channel_id=1, source_target_pairs={{0,1},{1,0},{2,3},{3,2},{4,5},{5,4},{6,7},{7,6},{8,9},{9,8},{10,11... | collective-permute-start | bytes 307208 | tf_op jit(solution)/shard_map/ppermute | solution.py:391

commit v8 on v5

--- a/solution.py
+++ b/solution.py
@@ -15,7 +15,7 @@
 LANES = 128
 SUB = 8
 TILE = SUB * NODES
-HEAD = 80
+HEAD = 64
 
 f32 = jnp.float32
 bf16 = jnp.bfloat16

time: 112 us -> 113 us (level)
    squeeze x1, local copies, waits for them, and re-layouts: 2.74 us -> 1.11 us  [on_device(): lax.dynamic_index_in_dim(table, at, 0, keepdims=False)]
    unnamed x24 -> x26, local copies, waits for them, and re-layouts: 6.41 us -> 7.7 us
  transfers between devices with their start and end apart: 16 -> 16, of which waited for: 6 -> 6; matrix products, arithmetic and copies ran while one was open for 12% -> 11% of each run, Pallas kernels for 43% -> 43%
where the time goes in v8:
time: 113 us; the launch traced here: 112 us
  Pallas kernels  49.2 us (44%)
  starting transfers between devices  26.5 us (23%)
  local copies, waits for them, and re-layouts  16.9 us (15%)
  between operations  7.94 us (7%)
  waiting for transfers between devices  7.57 us (7%)
  other arithmetic  3.73 us (3%)
    pallas_call x5, Pallas kernels, advance(): pl.pallas_call(lambda *refs: chunk_kernel(len(far), is_w, len(aliases), *...  35 us
    ppermute x10, starting transfers between devices, exchange(): lax.ppermute(block, 'mode', [(i, (i + s) % count) for i in range(count)])  11.6 us
    ppermute x4, starting transfers between devices, sum_over_plane(): lax.ppermute(value, 'plane', [(i, i ^ step) for i in range(count)])  11.1 us
    unnamed x26, local copies, waits for them, and re-layouts  7.7 us
    ppermute x10, waiting for transfers between devices, exchange(): lax.ppermute(block, 'mode', [(i, (i + s) % count) for i in range(count)])  6.49 us
    pallas_call x4, Pallas kernels, finish(): pl.pallas_call(finish_kernel, grid_spec=pltpu.PrefetchScalarGridSpec(num_...  4.87 us
    pallas_call x1, Pallas kernels, expand(): pl.pallas_call(expand_kernel, out_shape=jax.ShapeDtypeStruct((width // LA...  3.48 us
    pallas_call x1, Pallas kernels, both_groups(): pl.pallas_call(both_kernel, grid_spec=pltpu.PrefetchScalarGridSpec(num_sc...  3.27 us
  transfers between devices with their start and end apart: 16, of which 6 were waited for; matrix products, arithmetic and copies ran while one was open for 11% of the time, Pallas kernels for 43%

profile of v8, /device:TPU:0, one launch (start us, length us, event | category | flops | bytes accessed | tf_op | source)
XLA Modules:
  0.0 111.9 jit_solution(9455090306797716575)
XLA Ops:
  0.6 0.9 slice_bitcast_fusion.4
  1.5 3.0 %collective-permute-start.2 = (f32[64,512]{1,0:T(8,128)S(1)}, f32[64,512]{1,0:T(8,128)}, u32[]{:S(2)}, u32[]{:S(2)}) collective-permute-start(f32[64,512]{1,0:T(8,128)S(1)} %slice_bitcast_fusion.4), channel_id=1, source_target_pairs={{0,1},{1,0},{2,3},{3,2},{4,5},{5,4},{6,7},{7,6},{8,9},{9,8},{10,11... | collective-permute-start | bytes 393224 | tf_op jit(solution)/shard_map/ppermute | solution.py:390
  4.6 1.0 slice_bitcast_fusion.3
  5.6 0.1 collective-permute-start.3
  5.7 0.0 copy-start
  5.7 2.4 %copy-done = f32[3,800,512]{2,1,0:T(8,128)S(1)} copy-done((f32[3,800,512]{2,1,0:T(8,128)S(1)}, f32[3,800,512]{2,1,0:T(8,128)}, u32[]{:S(2)}) %copy-start) | copy-done | bytes 4915224
  8.1 2.6 %first_pass.1 = (f32[2,8,128]{2,1,0:T(8,128)S(1)}, f32[800,512]{1,0:T(8,128)}) custom-call(s32[1]{0:T(128)} %bitcast.at_ref, f32[3,800,512]{2,1,0:T(8,128)S(1)} %copy-done, f32[1,512]{1,0:T(1,128)S(1)} %compare_select_fusion.weight_ref), custom_call_target="tpu_custom_call" | custom-call | tf_op jit(solution)/shard_map/first_pass/pallas_call | solution.py:143
  10.7 2.0 %collective-permute-start.1 = (f32[2,8,128]{2,1,0:T(8,128)S(1)}, f32[2,8,128]{2,1,0:T(8,128)S(1)}, u32[]{:S(2)}, u32[]{:S(2)}) collective-permute-start(f32[2,8,128]{2,1,0:T(8,128)S(1)} %get-tuple-element.19), channel_id=1, source_target_pairs={{0,1},{1,0},{2,3},{3,2},{4,5},{5,4},{6,7},{7,6},{8,9},{9,8},{10,11... | collective-permute-start | bytes 24584 | tf_op jit(solution)/shard_map/ppermute | solution.py:390
  12.7 0.1 collective-permute-start
  12.8 2.9 %slice_bitcast_fusion = f32[800,512]{1,0:T(8,128)} fusion(f32[3,800,512]{2,1,0:T(8,128)} %own_ref.4), kind=kLoop, calls=%fused_computation.1 | loop fusion | bytes 3276800 | tf_op jit(solution)/shard_map/squeeze | solution.py:432
  15.7 1.8 %collective-permute-start.15 = (f32[800,512]{1,0:T(8,128)}, f32[800,512]{1,0:T(8,128)}, u32[]{:S(2)}, u32[]{:S(2)}) collective-permute-start(f32[800,512]{1,0:T(8,128)} %slice_bitcast_fusion), channel_id=1, source_target_pairs={{0,1},{1,0},{2,3},{3,2},{4,5},{5,4},{6,7},{7,6},{8,9},{9,8},{10,11... | collective-permute-start | bytes 4915208 | tf_op jit(solution)/shard_map/ppermute | solution.py:390
  17.5 0.6 fusion.8
  20.7 2.1 %slice_bitcast_fusion.1 = (f32[200,512]{1,0:T(8,128)}, f32[200,512]{1,0:T(8,128)}) fusion(f32[3,800,512]{2,1,0:T(8,128)} %own_ref.4), kind=kLoop, calls=%fused_computation.11 | loop fusion | bytes 1638400 | tf_op jit(solution)/shard_map/squeeze | solution.py:435
  24.1 0.1 add_select_fusion
  24.2 0.2 dynamic-slice_bitcast_fusion.5
  24.4 0.2 maximum_bitcast_fusion
  24.6 0.0 copy-start.6
  24.6 1.5 %pad_maximum_fusion.refs_3_.synth_ref.refs_4_ = bf16[2,2,512,512]{3,2,1,0:T(8,128)(2,1)} fusion(bf16[1,2,512,512]{3,2,1,0:T(8,128)(2,1)S(1)} %get-tuple-element.45, bf16[1,2,512,512]{3,2,1,0:T(8,128)(2,1)S(1)} %get-tuple-element.44), kind=kLoop, calls=%fused_computation | loop fusion | flops 1048576 | bytes 4194304 | tf_op jit(solution)/shard_map/stack | solution.py:474
  26.1 0.8 copy-done.6
  26.9 1.1 dynamic-slice_bitcast_fusion
  28.0 0.2 copy-done.4
  28.3 0.2 copy-done.5
  28.5 3.5 %expand.1.refs_5_.inv_ref.refs_6_ = f32[4,25,25,128]{3,2,1,0:T(8,128)S(1)} custom-call(f32[25,25,256]{2,1,0:T(8,128)S(1)} %bitcast.33, bf16[256,512]{1,0:T(8,128)(2,1)S(1)} %copy-done.5), custom_call_target="tpu_custom_call" | custom-call | tf_op jit(solution)/shard_map/expand/pallas_call | solution.py:178
  32.0 0.0 collective-permute-done.2
  32.0 0.2 collective-permute-start.14
  32.2 0.0 collective-permute-done.3
  32.2 1.0 pad_maximum_fusion.1.refs_1_
  33.3 0.6 slice_reduce_fusion
  33.9 0.1 copy.22
  34.0 0.1 reshape.101
  34.1 2.4 %collective-permute-start.8 = (f32[32]{0:T(128)S(1)}, f32[32]{0:T(128)S(1)}, u32[]{:S(2)}, u32[]{:S(2)}) collective-permute-start(f32[32]{0:T(128)S(1)} %multiply_multiply_fusion), channel_id=1, source_target_pairs={{0,2},{2,4},{4,6},{6,8},{8,10},{10,12},{12,14},{14,16},{16,18},{18... | collective-permute-start | bytes 392 | tf_op jit(solution)/shard_map/ppermute | solution.py:453
  37.8 3.3 %collective-permute-start.5 = (f32[]{:T(128)}, f32[]{:T(128)}, u32[]{:S(2)}, u32[]{:S(2)}) collective-permute-start(f32[]{:T(128)} %add.91), channel_id=1, source_target_pairs={{0,4},{2,6},{4,0},{6,2},{8,12},{10,14},{12,8},{14,10},{16,20},{18,... | collective-permute-start | bytes 20 | tf_op jit(solution)/shard_map/ppermute | solution.py:401
  41.1 0.4 collective-permute-done.5
  42.1 3.4 %collective-permute-start.6 = (f32[]{:T(128)}, f32[]{:T(128)}, u32[]{:S(2)}, u32[]{:S(2)}) collective-permute-start(f32[]{:T(128)} %add.92), channel_id=1, source_target_pairs={{0,8},{2,10},{4,12},{6,14},{8,0},{10,2},{12,4},{14,6},{16,24},{18,... | collective-permute-start | bytes 20 | tf_op jit(solution)/shard_map/ppermute | solution.py:401
  45.5 0.3 collective-permute-done.6
  46.5 4.4 %collective-permute-start.7 = (f32[]{:T(128)}, f32[]{:T(128)}, u32[]{:S(2)}, u32[]{:S(2)}) collective-permute-start(f32[]{:T(128)} %add.93), channel_id=1, source_target_pairs={{0,16},{2,18},{4,20},{6,22},{8,24},{10,26},{12,28},{14,30},{16,0},... | collective-permute-start | bytes 20 | tf_op jit(solution)/shard_map/ppermute | solution.py:401
  50.8 0.3 collective-permute-done.7
  51.2 1.5 %collective-permute-start.9 = (f32[32]{0:T(128)S(1)}, f32[32]{0:T(128)S(1)}, u32[]{:S(2)}, u32[]{:S(2)}) collective-permute-start(f32[32]{0:T(128)S(1)} %multiply_multiply_fusion), channel_id=1, source_target_pairs={{2,0},{4,2},{6,4},{8,6},{10,8},{12,10},{14,12},{16,14},{18,16},{20... | collective-permute-start | bytes 392 | tf_op jit(solution)/shard_map/ppermute | solution.py:454
  53.3 1.8 %collective-permute-start.13 = (f32[200,512]{1,0:T(8,128)}, f32[200,512]{1,0:T(8,128)}, u32[]{:S(2)}, u32[]{:S(2)}) collective-permute-start(f32[200,512]{1,0:T(8,128)} %get-tuple-element.33), channel_id=1, source_target_pairs={{0,1},{1,0},{2,3},{3,2},{4,5},{5,4},{6,7},{7,6},{8,9},{9,8},{10,11... | collective-permute-start | bytes 1228808 | tf_op jit(solution)/shard_map/ppermute | solution.py:390
  55.1 0.1 maximum_multiply_fusion
  55.2 0.2 select_reduce_fusion
  55.4 0.0 copy-start.9
  55.4 0.1 broadcast_multiply_fusion
  55.5 0.1 mul.94
  55.6 0.2 broadcast_in_dim.45.refs_2_.damp_ref.refs_3_
  55.7 0.0 copy-start.1
  55.8 2.4 %copy-done.1 = f32[3,800,512]{2,1,0:T(8,128)S(1)} copy-done((f32[3,800,512]{2,1,0:T(8,128)S(1)}, f32[3,800,512]{2,1,0:T(8,128)}, u32[]{:S(2)}) %copy-start.1) | copy-done | bytes 4915224
  58.1 1.6 %copy-done.2 = bf16[2,2,512,512]{3,2,1,0:T(8,128)(2,1)S(1)} copy-done((bf16[2,2,512,512]{3,2,1,0:T(8,128)(2,1)S(1)}, bf16[2,2,512,512]{3,2,1,0:T(8,128)(2,1)}, u32[]{:S(2)}) %copy-start.2) | copy-done | bytes 2097176
  59.7 3.6 %advance_2_0.1 = (f32[3,800,512]{2,1,0:T(8,128)}, f32[800,1024]{1,0:T(8,128)S(1)}) custom-call(f32[3,800,512]{2,1,0:T(8,128)S(1)} %copy-done.1, f32[200,512]{1,0:T(8,128)S(1)} %pad_maximum_fusion.1.refs_1_, f32[800,128]{1,0:T(8,128)S(1)} %broadcast_in_dim.45.refs_2_.damp_ref.refs_3_, bf16[2,2,512,512]{3,2,1,0:T(8,128)(2,1)S(1)} %copy-done.2, ...), custom_call_target="tpu_custom_call" | custom-call | flops 943718400 | bytes 819200 | tf_op jit(solution)/shard_map/advance_2_0/pallas_call | solution.py:294
  63.3 10.3 %advance_2_200.1 = (f32[3,800,512]{2,1,0:T(8,128)}, f32[800,1024]{1,0:T(8,128)S(1)}) custom-call(f32[3,800,512]{2,1,0:T(8,128)S(1)} %copy-done.1, f32[800,512]{1,0:T(8,128)} %collective-permute-done.refs_1_.far_ref, f32[800,128]{1,0:T(8,128)S(1)} %broadcast_in_dim.45.refs_2_.damp_ref.refs_3_, ...), custom_call_target="tpu_custom_call", output_to_operand_aliasing={{0}: (6, {}), {1}: (7, {})} | custom-call | flops 2831155200 | bytes 2457600 | tf_op jit(solution)/shard_map/advance_2_200/pallas_call | solution.py:294
  73.7 3.3 %both_groups.1 = (f32[200,512]{1,0:T(8,128)S(1)}, f32[200,256]{1,0:T(8,128)S(1)}, f32[200,128]{1,0:T(8,128)S(1)}, f32[200,128]{1,0:T(8,128)S(1)}) custom-call(s32[1]{0:T(128)} %bitcast.3.at_ref, f32[3,800,512]{2,1,0:T(8,128)S(1)} %copy-done.1, f32[800,512]{1,0:T(8,128)} %collective-permute-done.refs_1_.far_ref, ...), custom_call_target="tpu_custom_call" | custom-call | tf_op jit(solution)/shard_map/both_groups/pallas_call | solution.py:329
  76.9 0.8 collective-permute-start.12
  77.8 1.2 %collective-permute-start.11 = (f32[200,128]{1,0:T(8,128)S(1)}, f32[200,128]{1,0:T(8,128)S(1)}, u32[]{:S(2)}, u32[]{:S(2)}) collective-permute-start(f32[200,128]{1,0:T(8,128)S(1)} %get-tuple-element.28), channel_id=1, source_target_pairs={{0,1},{1,0},{2,3},{3,2},{4,5},{5,4},{6,7},{7,6},{8,9},{9,8},{10,11... | collective-permute-start | bytes 307208 | tf_op jit(solution)/shard_map/ppermute | solution.py:390
  79.0 2.0 %finish_here.1.refs_7_ = f32[3,800,512]{2,1,0:T(8,128)} custom-call(s32[1]{0:T(128)} %bitcast.3.at_ref, f32[3,800,512]{2,1,0:T(8,128)S(1)} %copy-done.1, f32[200,512]{1,0:T(8,128)S(1)} %get-tuple-element.30.span_ref, f32[800,128]{1,0:T(8,128)S(1)} %broadcast_in_dim.45.refs_2_.damp_ref.refs_3_, ...), custom_call_target="tpu_custom_call", output_to_operand_aliasing={{}: (5, {})} | custom-call | tf_op jit(solution)/shard_map/finish_here/pallas_call | solution.py:366
  81.0 5.8 %collective-permute-done.15.refs_1_ = f32[800,512]{1,0:T(8,128)} collective-permute-done((f32[800,512]{1,0:T(8,128)}, f32[800,512]{1,0:T(8,128)}, u32[]{:S(2)}, u32[]{:S(2)}) %collective-permute-start.15) | collective-permute-done | bytes 1638432 | tf_op jit(solution)/shard_map/ppermute | solution.py:390
  86.9 0.5 collective-permute-start.10
  87.3 13.0 %advance_0_0.1.refs_7_ = f32[3,800,512]{2,1,0:T(8,128)} custom-call(f32[3,800,512]{2,1,0:T(8,128)S(1)} %copy-done.1, f32[800,512]{1,0:T(8,128)} %collective-permute-done.15.refs_1_, f32[800,1024]{1,0:T(8,128)S(1)} %get-tuple-element.26.wphys_ref.refs_2_, f32[800,128]{1,0:T(8,128)S(1)} %broadcast_in_dim.45.refs_2_.damp_ref.refs_3_, ...), custom_call_target="tpu_custom_call", output_to_operand_aliasing={{}: (7, {})} | custom-call | flops 3774873600 | bytes 3276800 | tf_op jit(solution)/shard_map/advance_0_0/pallas_call | solution.py:294
  100.3 3.5 %advance_1_0.1.refs_7_ = f32[3,800,512]{2,1,0:T(8,128)} custom-call(f32[3,800,512]{2,1,0:T(8,128)S(1)} %copy-done.1, f32[200,512]{1,0:T(8,128)S(1)} %collective-permute-done.14.refs_1_, f32[800,1024]{1,0:T(8,128)S(1)} %get-tuple-element.26.wphys_ref.refs_2_, ...), custom_call_target="tpu_custom_call", output_to_operand_aliasing={{}: (7, {})} | custom-call | flops 943718400 | bytes 819200 | tf_op jit(solution)/shard_map/advance_1_0/pallas_call | solution.py:294
  103.9 0.6 collective-permute-done.13.refs_1_
  104.4 4.5 %advance_1_200.1.held_ref = f32[3,800,512]{2,1,0:T(8,128)} custom-call(f32[3,800,512]{2,1,0:T(8,128)S(1)} %copy-done.1, f32[200,512]{1,0:T(8,128)} %collective-permute-done.13.refs_1_, f32[800,1024]{1,0:T(8,128)S(1)} %get-tuple-element.26.wphys_ref.refs_2_, f32[800,128]{1,0:T(8,128)S(1)} %broadcast_in_dim.45.refs_2_.damp_ref.refs_3_, ...), custom_call_target="tpu_custom_call", output_to_operand_aliasing={{}: (7, {})} | custom-call | flops 943718400 | bytes 819200 | tf_op jit(solution)/shard_map/advance_1_200/pallas_call | solution.py:294
  109.0 1.1 %finish_there_0.1.held_ref = f32[3,800,512]{2,1,0:T(8,128)} custom-call(s32[1]{0:T(128)} %bitcast.at_ref, f32[3,800,512]{2,1,0:T(8,128)S(1)} %copy-done.1, f32[200,256]{1,0:T(8,128)S(1)} %collective-permute-done.12.span_ref, f32[800,128]{1,0:T(8,128)S(1)} %broadcast_in_dim.45.refs_2_.damp_ref.refs_3_, ...), custom_call_target="tpu_custom_call", output_to_operand_aliasing={{}: (5, {})} | custom-call | tf_op jit(solution)/shard_map/finish_there_0/pallas_call | solution.py:366
  110.1 0.9 finish_there_2.1.held_ref
  111.0 0.1 collective-permute-done.10.span_ref
  111.1 0.9 finish_there_3.1
  (31 shorter events, 0.1 us)
Async XLA Ops:
  1.5 30.4 %collective-permute-start.2 = (f32[64,512]{1,0:T(8,128)S(1)}, f32[64,512]{1,0:T(8,128)}, u32[]{:S(2)}, u32[]{:S(2)}) collective-permute-start(f32[64,512]{1,0:T(8,128)S(1)} %slice_bitcast_fusion.4), channel_id=1, source_target_pairs={{0,1},{1,0},{2,3},{3,2},{4,5},{5,4},{6,7},{7,6},{8,9},{9,8},{10,11... | collective-permute-start | bytes 393224 | tf_op jit(solution)/shard_map/ppermute | solution.py:390
  5.6 26.7 %collective-permute-start.3 = (f32[136,512]{1,0:T(8,128)S(1)}, f32[136,512]{1,0:T(8,128)}, u32[]{:S(2)}, u32[]{:S(2)}) collective-permute-start(f32[136,512]{1,0:T(8,128)S(1)} %slice_bitcast_fusion.3), channel_id=1, source_target_pairs={{0,1},{1,0},{2,3},{3,2},{4,5},{5,4},{6,7},{7,6},{8,9},{9,8},{10,11... | collective-permute-start | bytes 835592 | tf_op jit(solution)/shard_map/ppermute | solution.py:390
  5.7 2.4 %copy-start = (f32[3,800,512]{2,1,0:T(8,128)S(1)}, f32[3,800,512]{2,1,0:T(8,128)}, u32[]{:S(2)}) copy-start(f32[3,800,512]{2,1,0:T(8,128)} %own_ref.4) | copy-start | bytes 14745604
  10.7 22.6 %collective-permute-start.1 = (f32[2,8,128]{2,1,0:T(8,128)S(1)}, f32[2,8,128]{2,1,0:T(8,128)S(1)}, u32[]{:S(2)}, u32[]{:S(2)}) collective-permute-start(f32[2,8,128]{2,1,0:T(8,128)S(1)} %get-tuple-element.19), channel_id=1, source_target_pairs={{0,1},{1,0},{2,3},{3,2},{4,5},{5,4},{6,7},{7,6},{8,9},{9,8},{10,11... | collective-permute-start | bytes 24584 | tf_op jit(solution)/shard_map/ppermute | solution.py:390
  12.7 11.4 %copy-start.8 = (s32[32,4]{0,1:T(4,128)S(1)}, s32[32,4]{0,1:T(4,128)}, u32[]{:S(2)}) copy-start(s32[32,4]{0,1:T(4,128)} %param.11) | copy-start | bytes 1540
  12.7 11.4 %copy-start.11 = (s32[4]{0:T(128)S(1)}, s32[4]{0:T(128)}, u32[]{:S(2)}) copy-start(s32[4]{0:T(128)} %constant.77.clone) | copy-start | bytes 52
  12.7 11.5 %copy-start.7 = (bf16[2,2,2,256,512]{4,3,2,1,0:T(8,128)(2,1)S(1)}, bf16[2,2,2,256,512]{4,3,2,1,0:T(8,128)(2,1)}, u32[]{:S(2)}) copy-start(bf16[2,2,2,256,512]{4,3,2,1,0:T(8,128)(2,1)} %constant.79.clone) | copy-start | bytes 6291460
  12.7 50.6 %collective-permute-start = (f32[800,512]{1,0:T(8,128)}, f32[800,512]{1,0:T(8,128)}, u32[]{:S(2)}, u32[]{:S(2)}) collective-permute-start(f32[800,512]{1,0:T(8,128)} %get-tuple-element.21), channel_id=1, source_target_pairs={{0,1},{1,0},{2,3},{3,2},{4,5},{5,4},{6,7},{7,6},{8,9},{9,8},{10,11... | collective-permute-start | bytes 4915208 | tf_op jit(solution)/shard_map/ppermute | solution.py:390
  15.7 71.2 %collective-permute-start.15 = (f32[800,512]{1,0:T(8,128)}, f32[800,512]{1,0:T(8,128)}, u32[]{:S(2)}, u32[]{:S(2)}) collective-permute-start(f32[800,512]{1,0:T(8,128)} %slice_bitcast_fusion), channel_id=1, source_target_pairs={{0,1},{1,0},{2,3},{3,2},{4,5},{5,4},{6,7},{7,6},{8,9},{9,8},{10,11... | collective-permute-start | bytes 4915208 | tf_op jit(solution)/shard_map/ppermute | solution.py:390
  24.6 2.4 %copy-start.6 = (bf16[2,2,2,512,256]{4,3,2,1,0:T(8,128)(2,1)S(1)}, bf16[2,2,2,512,256]{4,3,2,1,0:T(8,128)(2,1)}, u32[]{:S(2)}) copy-start(bf16[2,2,2,512,256]{4,3,2,1,0:T(8,128)(2,1)} %constant.80.clone) | copy-start | bytes 6291460
  26.9 1.4 %copy-start.4 = (f32[256,25,25]{0,2,1:T(8,128)S(1)}, f32[256,25,25]{0,2,1:T(8,128)}, u32[]{:S(2)}) copy-start(f32[256,25,25]{0,2,1:T(8,128)} %param.10) | copy-start | bytes 1920004
  26.9 1.6 %copy-start.5 = (bf16[256,512]{1,0:T(8,128)(2,1)S(1)}, bf16[256,512]{1,0:T(8,128)(2,1)}, u32[]{:S(2)}) copy-start(bf16[256,512]{1,0:T(8,128)(2,1)} %constant.81.clone.spread_ref) | copy-start | bytes 786436
  28.0 6.0 %copy-start.12 = (s32[32]{0:T(128)S(1)}, s32[32]{0:T(128)}, u32[]{:S(2)}) copy-start(s32[32]{0:T(128)} %param.12) | copy-start | bytes 388
  28.0 27.3 %copy-start.10 = (f32[25]{0:T(128)S(1)}, f32[25]{0:T(128)}, u32[]{:S(2)}) copy-start(f32[25]{0:T(128)} %constant.82) | copy-start | bytes 304
  32.0 68.3 %collective-permute-start.14 = (f32[200,512]{1,0:T(8,128)}, f32[200,512]{1,0:T(8,128)S(1)}, u32[]{:S(2)}, u32[]{:S(2)}) collective-permute-start(f32[200,512]{1,0:T(8,128)} %get-tuple-element.32), channel_id=1, source_target_pairs={{0,1},{1,0},{2,3},{3,2},{4,5},{5,4},{6,7},{7,6},{8,9},{9,8},{10,11... | collective-permute-start | bytes 1228808 | tf_op jit(solution)/shard_map/ppermute | solution.py:390
  33.9 2.6 %collective-permute-start.4 = (f32[]{:T(128)}, f32[]{:T(128)}, u32[]{:S(2)}, u32[]{:S(2)}) collective-permute-start(f32[]{:T(128)} %get-tuple-element.40), channel_id=1, source_target_pairs={{0,2},{2,0},{4,6},{6,4},{8,10},{10,8},{12,14},{14,12},{16,18},{18,... | collective-permute-start | bytes 20 | tf_op jit(solution)/shard_map/ppermute | solution.py:401
  34.1 19.3 %collective-permute-start.8 = (f32[32]{0:T(128)S(1)}, f32[32]{0:T(128)S(1)}, u32[]{:S(2)}, u32[]{:S(2)}) collective-permute-start(f32[32]{0:T(128)S(1)} %multiply_multiply_fusion), channel_id=1, source_target_pairs={{0,2},{2,4},{4,6},{6,8},{8,10},{10,12},{12,14},{14,16},{16,18},{18... | collective-permute-start | bytes 392 | tf_op jit(solution)/shard_map/ppermute | solution.py:453
  37.8 3.7 %collective-permute-start.5 = (f32[]{:T(128)}, f32[]{:T(128)}, u32[]{:S(2)}, u32[]{:S(2)}) collective-permute-start(f32[]{:T(128)} %add.91), channel_id=1, source_target_pairs={{0,4},{2,6},{4,0},{6,2},{8,12},{10,14},{12,8},{14,10},{16,20},{18,... | collective-permute-start | bytes 20 | tf_op jit(solution)/shard_map/ppermute | solution.py:401
  42.1 3.7 %collective-permute-start.6 = (f32[]{:T(128)}, f32[]{:T(128)}, u32[]{:S(2)}, u32[]{:S(2)}) collective-permute-start(f32[]{:T(128)} %add.92), channel_id=1, source_target_pairs={{0,8},{2,10},{4,12},{6,14},{8,0},{10,2},{12,4},{14,6},{16,24},{18,... | collective-permute-start | bytes 20 | tf_op jit(solution)/shard_map/ppermute | solution.py:401
  46.5 4.7 %collective-permute-start.7 = (f32[]{:T(128)}, f32[]{:T(128)}, u32[]{:S(2)}, u32[]{:S(2)}) collective-permute-start(f32[]{:T(128)} %add.93), channel_id=1, source_target_pairs={{0,16},{2,18},{4,20},{6,22},{8,24},{10,26},{12,28},{14,30},{16,0},... | collective-permute-start | bytes 20 | tf_op jit(solution)/shard_map/ppermute | solution.py:401
  51.2 3.9 %collective-permute-start.9 = (f32[32]{0:T(128)S(1)}, f32[32]{0:T(128)S(1)}, u32[]{:S(2)}, u32[]{:S(2)}) collective-permute-start(f32[32]{0:T(128)S(1)} %multiply_multiply_fusion), channel_id=1, source_target_pairs={{2,0},{4,2},{6,4},{8,6},{10,8},{12,10},{14,12},{16,14},{18,16},{20... | collective-permute-start | bytes 392 | tf_op jit(solution)/shard_map/ppermute | solution.py:454
  53.3 51.1 %collective-permute-start.13 = (f32[200,512]{1,0:T(8,128)}, f32[200,512]{1,0:T(8,128)}, u32[]{:S(2)}, u32[]{:S(2)}) collective-permute-start(f32[200,512]{1,0:T(8,128)} %get-tuple-element.33), channel_id=1, source_target_pairs={{0,1},{1,0},{2,3},{3,2},{4,5},{5,4},{6,7},{7,6},{8,9},{9,8},{10,11... | collective-permute-start | bytes 1228808 | tf_op jit(solution)/shard_map/ppermute | solution.py:390
  55.4 7.9 %copy-start.9 = (f32[32]{0:T(128)}, f32[32]{0:T(128)S(1)}, u32[]{:S(2)}) copy-start(f32[32]{0:T(128)S(1)} %add_multiply_fusion.1) | copy-start | bytes 388
  55.7 2.4 %copy-start.1 = (f32[3,800,512]{2,1,0:T(8,128)S(1)}, f32[3,800,512]{2,1,0:T(8,128)}, u32[]{:S(2)}) copy-start(f32[3,800,512]{2,1,0:T(8,128)} %own_ref.4) | copy-start | bytes 14745604
  58.1 1.6 %copy-start.2 = (bf16[2,2,512,512]{3,2,1,0:T(8,128)(2,1)S(1)}, bf16[2,2,512,512]{3,2,1,0:T(8,128)(2,1)}, u32[]{:S(2)}) copy-start(bf16[2,2,512,512]{3,2,1,0:T(8,128)(2,1)} %pad_maximum_fusion.refs_3_.synth_ref.refs_4_) | copy-start | bytes 6291460
  63.3 10.3 %copy-start.3 = (bf16[2,2,512,256]{3,2,1,0:T(8,128)(2,1)S(1)}, bf16[2,2,512,256]{3,2,1,0:T(8,128)(2,1)}, u32[]{:S(2)}) copy-start(bf16[2,2,512,256]{3,2,1,0:T(8,128)(2,1)} %get-tuple-element.34.other_ref) | copy-start | bytes 3145732
  76.9 32.0 %collective-permute-start.12 = (f32[200,256]{1,0:T(8,128)S(1)}, f32[200,256]{1,0:T(8,128)S(1)}, u32[]{:S(2)}, u32[]{:S(2)}) collective-permute-start(f32[200,256]{1,0:T(8,128)S(1)} %get-tuple-element.29), channel_id=1, source_target_pairs={{0,1},{1,0},{2,3},{3,2},{4,5},{5,4},{6,7},{7,6},{8,9},{9,8},{10,11... | collective-permute-start | bytes 614408 | tf_op jit(solution)/shard_map/ppermute | solution.py:390
  77.8 32.3 %collective-permute-start.11 = (f32[200,128]{1,0:T(8,128)S(1)}, f32[200,128]{1,0:T(8,128)S(1)}, u32[]{:S(2)}, u32[]{:S(2)}) collective-permute-start(f32[200,128]{1,0:T(8,128)S(1)} %get-tuple-element.28), channel_id=1, source_target_pairs={{0,1},{1,0},{2,3},{3,2},{4,5},{5,4},{6,7},{7,6},{8,9},{9,8},{10,11... | collective-permute-start | bytes 307208 | tf_op jit(solution)/shard_map/ppermute | solution.py:390
  86.9 24.2 %collective-permute-start.10 = (f32[200,128]{1,0:T(8,128)S(1)}, f32[200,128]{1,0:T(8,128)S(1)}, u32[]{:S(2)}, u32[]{:S(2)}) collective-permute-start(f32[200,128]{1,0:T(8,128)S(1)} %get-tuple-element.27), channel_id=1, source_target_pairs={{0,1},{1,0},{2,3},{3,2},{4,5},{5,4},{6,7},{7,6},{8,9},{9,8},{10,11... | collective-permute-start | bytes 307208 | tf_op jit(solution)/shard_map/ppermute | solution.py:390
